TPU v7x, 32 devices: a whole 2x2x4 slice. The times are simulated.
32 devices in a mesh: blk: 8 (over z, core), split: 4 (over y, x).
Axes of the slice: x: 2, y: 2, z: 4, core: 2. Of those that a mesh axis runs over, the one named last changes fastest.
Arguments:
- orbitals: float32 [4096, 512], P('blk'), may hold values from -6 to 6
- kernel: float32 [4096, 4, 1024], P('blk', 'split'), as said below
Outputs:
- exchange_out: float32 [4096, 512], P(('blk', 'split'))
Inputs may be any that keep to these rules, and one draw needn't show every extreme that they name: Z built from kernel as in the first step is a symmetric matrix.
All inputs are finite; a program needn't handle non-finite values.
Results may differ from a plain program's by a relative error of at most 0.00013.
Values sent between devices are 32-bit elements; how exact they have to be, the bound alone decides.
No kernel may reach another device: no remote copies, remote signals or barrier semaphores. Data moves between devices by JAX's collectives and lax.ppermute only.
A program may use at most 64 MiB of HBM per device.

v0:
```python
import jax
import jax.numpy as jnp
from jax import lax
from jax.sharding import PartitionSpec as P


def apply_rows(weights, visitor):
    return jnp.dot(
        weights, visitor, precision=lax.Precision.HIGHEST, preferred_element_type=jnp.float32
    )


def per_device(orbitals, kernel):
    nshares = lax.axis_size("split")
    share_id = lax.axis_index("split")
    home_rows = orbitals.shape[0]
    share_rows = home_rows // nshares
    kernel = kernel[:, 0, :]
    own = lax.dynamic_slice_in_dim(orbitals, share_id * share_rows, share_rows, 0)
    piece = lax.all_gather(own, "blk", axis=0, tiled=True)
    correlation = lax.dot_general(
        orbitals,
        piece,
        (((1,), (1,)), ((), ())),
        precision=lax.Precision.HIGHEST,
        preferred_element_type=jnp.float32,
    )
    home = apply_rows(kernel * correlation, piece)
    folded = lax.psum_scatter(home, "split", scatter_dimension=0, tiled=True)
    return folded


def solution(mesh):
    placed = (P("blk", None), P("blk", "split", None))
    return jax.shard_map(
        per_device, mesh=mesh, in_specs=placed, out_specs=P(("blk", "split"), None), check_vma=False
    )
```

profile of v0, /device:TPU:0, one launch (start us, length us, event | category | flops | bytes accessed | tf_op | source)
XLA Modules:
  0.0 85.0 jit_solution(1565839492176027375)
XLA Ops:
  6.5 0.0 copy-start
  6.5 0.0 all-gather.2.cloned.1.call-start
  6.5 1.2 %copy-done = f32[512,512]{1,0:T(8,128)S(1)} copy-done((f32[512,512]{1,0:T(8,128)S(1)}, f32[512,512]{1,0:T(8,128)}, u32[]{:S(2)}) %copy-start) | copy-done | bytes 1048600
  7.8 0.7 constant_dynamic-slice_fusion
  8.5 0.0 all-gather.2.cloned.1.call-update
  8.5 0.0 copy-start.2
  8.5 0.0 reduce-scatter.2.cloned.1.call-start
  8.6 32.2 %all-gather.2.cloned.1.call-done = f32[1024,512]{1,0:T(8,128)} async-done(((f32[128,512]{1,0:T(8,128)}), f32[1024,512]{1,0:T(8,128)}) %all-gather.2.cloned.1.call-update) | async-done | bytes 2097168 | tf_op jit(solution)/shard_map/all_gather | solution.py:20
  40.8 0.0 copy-start.1
  40.8 5.3 %fusion.3 = f32[1024,512]{0,1:T(8,128)S(1)} fusion(f32[1024,512]{1,0:T(8,128)} %all-gather.2.cloned.1.call-done, f32[512,512]{1,0:T(8,128)S(1)} %copy-done), kind=kOutput, calls=%fused_computation.5 | convolution fusion | flops 3221225472 | bytes 5242880 | tf_op jit(solution)/shard_map/dot_general | solution.py:21
  46.1 0.0 copy-done.2
  46.1 0.0 copy-done.1
  46.1 4.7 %fusion = f32[512,512]{1,0:T(8,128)} fusion(f32[1024,512]{1,0:T(8,128)S(1)} %copy-done.1, f32[512,1,1024]{2,1,0:T(1,128)S(1)} %copy-done.2, f32[1024,512]{0,1:T(8,128)S(1)} %fusion.3), kind=kOutput, calls=%fused_computation.1 | convolution fusion | flops 3221749760 | bytes 7340032 | tf_op jit(solution)/shard_map/dot_general | solution.py:8
  50.8 0.0 reduce-scatter.2.cloned.1.call-update
  50.8 27.3 %reduce-scatter.2.cloned.1.call-done = f32[128,512]{1,0:T(8,128)} async-done(((f32[512,512]{1,0:T(8,128)}), f32[128,512]{1,0:T(8,128)}) %reduce-scatter.2.cloned.1.call-update) | async-done | bytes 262160 | tf_op jit(solution)/shard_map/reduce_scatter | solution.py:29
Async XLA Ops:
  6.5 1.2 %copy-start = (f32[512,512]{1,0:T(8,128)S(1)}, f32[512,512]{1,0:T(8,128)}, u32[]{:S(2)}) copy-start(f32[512,512]{1,0:T(8,128)} %param.2) | copy-start | bytes 3145732
  6.5 34.3 %all-gather.2.cloned.1.call-start = ((), (), s32[]{:S(2)}) async-start(), calls=%async_computation.1 | async-start | bytes 2359296 | tf_op jit(solution)/shard_map/all_gather | solution.py:20
  8.5 37.6 %copy-start.2 = (f32[512,1,1024]{2,1,0:T(1,128)S(1)}, f32[512,1,1024]{2,1,0:T(1,128)}, u32[]{:S(2)}) copy-start(f32[512,1,1024]{2,1,0:T(1,128)} %param.3) | copy-start | bytes 6291460
  8.5 69.6 %reduce-scatter.2.cloned.1.call-start = ((), (), s32[]{:S(2)}) async-start(), calls=%async_computation.2 | async-start | bytes 1310720 | tf_op jit(solution)/shard_map/reduce_scatter | solution.py:29
  40.8 5.3 %copy-start.1 = (f32[1024,512]{1,0:T(8,128)S(1)}, f32[1024,512]{1,0:T(8,128)}, u32[]{:S(2)}) copy-start(f32[1024,512]{1,0:T(8,128)} %all-gather.2.cloned.1.call-done) | copy-start | bytes 6291460
Sparse Core Ops, SparseCore 0:
  9.0 31.7 all-gather.1
  50.9 27.1 reduce-scatter.1
where the time goes:
time: 85.1 us; the launch traced here: 85 us
  waiting for transfers between devices  59.6 us (70%)
  between operations  13.4 us (16%)
  matrix products  9.96 us (12%)
  local copies, waits for them, and re-layouts  1.95 us (2%)
    all_gather x1, waiting for transfers between devices, per_device(): piece = lax.all_gather(own, 'blk', axis=0, tiled=True)  32.2 us
    reduce_scatter x1, waiting for transfers between devices, per_device(): folded = lax.psum_scatter(home, 'split', scatter_dimension=0, tiled=True)  27.3 us
    dot_general x1, matrix products, per_device(): lax.dot_general(orbitals, piece, (((1,), (1,)), ((), ())), precision=lax....  5.25 us
    dot_general x1, matrix products, apply_rows(): jnp.dot(weights, visitor, precision=lax.Precision.HIGHEST, preferred_elem...  4.71 us
  transfers between devices with their start and end apart: 2, of which 2 were waited for; matrix products, arithmetic and copies ran while one was open for 0% of the time, Pallas kernels for 0%

commit v1 on v0

v1 whole, which is shorter than its diff:
```python
import jax
import jax.numpy as jnp
from jax import lax
from jax.sharding import PartitionSpec as P

CORES = 2


def product(a, b, dims):
    return lax.dot_general(
        a, b, (dims, ((), ())), precision=lax.Precision.HIGH, preferred_element_type=jnp.float32
    )


def per_device(orbitals, kernel):
    nchips = lax.axis_size("blk") // CORES
    nshares = lax.axis_size("split")
    q = lax.axis_index("blk")
    share_id = lax.axis_index("split")
    chip, core = q // CORES, q % CORES
    share = orbitals.shape[0] // nshares
    width = CORES * share
    half = nchips // 2
    z_rows = kernel[:, 0, :]

    def is_inner(c):
        return abs(2 * c - nchips + 1) < half

    inner_chips = [c for c in range(nchips) if is_inner(c)]
    outer_chips = [c for c in range(nchips) if not is_inner(c)]
    inner = jnp.abs(2 * chip - nchips + 1) < half

    def along(value, pairs):
        full = [(CORES * a + c, CORES * b + c) for a, b in pairs for c in range(CORES)]
        return lax.ppermute(value, "blk", full)

    def other_core(value):
        return lax.ppermute(value, "blk", [(i, i ^ 1) for i in range(nchips * CORES)])

    def in_order(mine, other):
        first = jnp.where(core == 0, mine, other)
        second = jnp.where(core == 0, other, mine)
        return jnp.concatenate([first, second], axis=0)

    own = lax.dynamic_slice_in_dim(orbitals, share_id * share, share, 0)
    far = along(own, [(c, c ^ half) for c in outer_chips])
    arrived = {}
    for k in range(1, half):
        arrived[k] = along(own, [(c, c ^ k) for c in range(nchips)])
    for k in range(half + 1, nchips):
        arrived[k] = along(own, [(c, c ^ k) for c in inner_chips])

    def weighted(k, points):
        z_part = lax.dynamic_slice_in_dim(z_rows, (chip ^ k) * width, width, 1)
        return z_part * product(orbitals, points, ((1,), (1,)))

    def rows_of(weights, points):
        return product(weights, points, ((1,), (0,)))

    points = in_order(own, other_core(own))
    total = rows_of(weighted(0, points), points)

    points = in_order(far, other_core(far))
    weights = weighted(half, points)
    back = product(weights, orbitals, ((0,), (0,)))
    mine = lax.dynamic_slice_in_dim(back, core * share, share, 0)
    theirs = lax.dynamic_slice_in_dim(back, (1 - core) * share, share, 0)
    returned = along(mine + other_core(theirs), [(c, c ^ half) for c in inner_chips])
    total += rows_of(weights, points)

    for k in range(1, half):
        points = in_order(arrived[k], other_core(arrived[k]))
        total += rows_of(weighted(k, points), points)
    for k in range(half + 1, nchips):
        passed = along(far, [(c, c ^ half ^ k) for c in inner_chips])
        here = jnp.where(inner, arrived[k], passed)
        points = in_order(here, other_core(here))
        total += rows_of(weighted(k, points), points)

    bits = nshares.bit_length() - 1
    ncols = orbitals.shape[1] // bits
    parts = []
    for part in range(bits):
        held = total[:, part * ncols : (part + 1) * ncols].reshape((2,) * bits + (share, ncols))
        for step in range(bits):
            bit = (part + step) % bits
            axis = bits - 1 - bit
            my_bit = (share_id >> bit) & 1
            keep = lax.dynamic_slice_in_dim(held, my_bit, 1, axis)
            send = lax.dynamic_slice_in_dim(held, 1 - my_bit, 1, axis)
            got = lax.ppermute(send, "split", [(i, i ^ (1 << bit)) for i in range(nshares)])
            held = keep + got
        parts.append(held.reshape(share, ncols))
    return jnp.concatenate(parts, axis=1) + returned


def solution(mesh):
    placed = (P("blk", None), P("blk", "split", None))
    return jax.shard_map(
        per_device, mesh=mesh, in_specs=placed, out_specs=P(("blk", "split"), None), check_vma=False
    )
```

time: 85.1 us -> 49.8 us (0.59)
  waiting for transfers between devices: 59.6 us -> 16 us
  starting transfers between devices: 0.04 us -> 17.8 us
  between operations: 13.4 us -> 0.28 us
  local copies, waits for them, and re-layouts: 1.95 us -> 6.93 us
  matrix products: 9.96 us -> 5.52 us
  other arithmetic: 0 us -> 2.99 us
    all_gather x1 -> x0, waiting for transfers between devices: 32.2 us -> none  [per_device(): piece = lax.all_gather(own, 'blk', axis=0, tiled=True)]
    reduce_scatter x1 -> x0, waiting for transfers between devices: 27.3 us -> none  [per_device(): folded = lax.psum_scatter(home, 'split', scatter_dimension=0, tiled=True)]
    ppermute x0 -> x14, starting transfers between devices: none -> 17.8 us  [the longest x5 10.1 us: along(): return lax.ppermute(value, 'blk', full)]
    ppermute x0 -> x14, waiting for transfers between devices: none -> 16 us  [the longest x5 8.7 us: along(): return lax.ppermute(value, 'blk', full)]
    dynamic_slice x1 -> x8, local copies, waits for them, and re-layouts: 0.72 us -> 6.85 us  [the longest x2 5.07 us: weighted(): z_part = lax.dynamic_slice_in_dim(z_rows, (chip ^ k) * width, width, 1)]
    dot_general x2 -> x9, matrix products: 9.96 us -> 5.52 us  [product(): lax.dot_general(a, b, (dims, ((), ())), precision=lax.Precision.HIGH, pre...]
    select_n x0 -> x5, other arithmetic: none -> 2.12 us  [the longest x4 2.08 us: in_order(): first = jnp.where(core == 0, mine, other)]
    unnamed x6 -> x2, local copies, waits for them, and re-layouts: 1.23 us -> 0.01 us
  transfers between devices with their start and end apart: 2 -> 14, of which waited for: 2 -> 5; matrix products, arithmetic and copies ran while one was open for 0% -> 26% of each run, Pallas kernels for 0% -> 0%
where the time goes in v1:
time: 49.8 us; the launch traced here: 49.5 us
  starting transfers between devices  17.8 us (36%)
  waiting for transfers between devices  16 us (32%)
  local copies, waits for them, and re-layouts  6.93 us (14%)
  matrix products  5.52 us (11%)
  other arithmetic  2.99 us (6%)
    ppermute x5, starting transfers between devices, along(): return lax.ppermute(value, 'blk', full)  10.1 us
    ppermute x5, waiting for transfers between devices, along(): return lax.ppermute(value, 'blk', full)  8.7 us
    ppermute x4, waiting for transfers between devices, per_device(): lax.ppermute(send, 'split', [(i, i ^ 1 << bit) for i in range(nshares)])  7.26 us
    ppermute x4, starting transfers between devices, per_device(): lax.ppermute(send, 'split', [(i, i ^ 1 << bit) for i in range(nshares)])  6.27 us
    dot_general x9, matrix products, product(): lax.dot_general(a, b, (dims, ((), ())), precision=lax.Precision.HIGH, pre...  5.52 us
    dynamic_slice x2, local copies, waits for them, and re-layouts, weighted(): z_part = lax.dynamic_slice_in_dim(z_rows, (chip ^ k) * width, width, 1)  5.07 us
    select_n x4, other arithmetic, in_order(): first = jnp.where(core == 0, mine, other)  2.08 us
    dynamic_slice x1, local copies, waits for them, and re-layouts, per_device(): own = lax.dynamic_slice_in_dim(orbitals, share_id * share, share, 0)  1.67 us
  transfers between devices with their start and end apart: 14, of which 5 were waited for; matrix products, arithmetic and copies ran while one was open for 26% of the time, Pallas kernels for 0%

profile of v1, /device:TPU:0, one launch (start us, length us, event | category | flops | bytes accessed | tf_op | source)
XLA Modules:
  0.0 49.5 jit_solution(2413501890290864822)
XLA Ops:
  0.0 1.7 %constant_dynamic-slice_fusion.8 = f32[128,512]{1,0:T(8,128)} fusion(f32[512,512]{1,0:T(8,128)} %param.2, s32[]{:T(128)S(6)} %select_n.94), kind=kLoop, calls=%fused_computation.40 | loop fusion | bytes 524292 | tf_op jit(solution)/shard_map/dynamic_slice | solution.py:45
  2.1 6.2 %collective-permute-start.1 = (f32[128,512]{1,0:T(8,128)}, f32[128,512]{1,0:T(8,128)}, u32[]{:S(2)}, u32[]{:S(2)}) collective-permute-start(f32[128,512]{1,0:T(8,128)} %constant_dynamic-slice_fusion.8), channel_id=1, source_target_pairs={{0,16},{4,20},{24,8},{28,12},{1,17},{5,21},{25,9},{29,13},{2,18},{... | collective-permute-start | bytes 786440 | tf_op jit(solution)/shard_map/ppermute | solution.py:35
  8.3 1.4 %collective-permute-start.5 = (f32[128,512]{1,0:T(8,128)}, f32[128,512]{1,0:T(8,128)}, u32[]{:S(2)}, u32[]{:S(2)}) collective-permute-start(f32[128,512]{1,0:T(8,128)} %constant_dynamic-slice_fusion.8), channel_id=1, source_target_pairs={{8,16},{12,20},{16,8},{20,12},{9,17},{13,21},{17,9},{21,13},{10,18... | collective-permute-start | bytes 786440 | tf_op jit(solution)/shard_map/ppermute | solution.py:35
  9.7 3.8 %constant_dynamic-slice_fusion.6 = (f32[512,1,256]{2,1,0:T(1,128)S(1)}, f32[512,1,256]{2,1,0:T(1,128)}, f32[512,1,256]{2,1,0:T(1,128)S(1)}, f32[512,1,256]{2,1,0:T(1,128)S(1)}) fusion(f32[512,1,1024]{2,1,0:T(1,128)} %param.3, s32[]{:T(128)S(6)} %select_n.100, s32[]{:T(128)S(6)} %select_n.97, s32[]{:T(128)S(6)} %select_n.91, s32[]{:T(128)S(6)} %select_n.103), kind=kLoop, calls=%fused_computation.38 | loop fusion | bytes 4194320 | tf_op jit(solution)/shard_map/dynamic_slice | solution.py:54
  13.5 1.2 %copy.3 = f32[512,1,256]{0,2,1:T(8,128)S(1)} copy(f32[512,1,256]{2,1,0:T(1,128)} %get-tuple-element.6) | data formatting | bytes 1048576 | tf_op jit(solution)/shard_map/dynamic_slice | solution.py:54
  14.9 0.6 %fusion.4 = f32[512,256]{1,0:T(8,128)S(1)} fusion(f32[512,512]{1,0:T(8,128)S(1)} %copy-done, f32[512,1,256]{2,1,0:T(1,128)S(1)} %get-tuple-element.7, f32[128,512]{1,0:T(8,128)S(1)} %get-tuple-element.14, f32[128,512]{1,0:T(8,128)S(1)} %get-tuple-element.13), kind=kOutput, calls=%fused_computation.10 | convolution fusion | flops 402915328 | bytes 2621440 | tf_op jit(solution)/shard_map/dot_general | solution.py:10
  15.8 1.3 %collective-permute-start.6 = (f32[128,512]{1,0:T(8,128)}, f32[128,512]{1,0:T(8,128)S(1)}, u32[]{:S(2)}, u32[]{:S(2)}) collective-permute-start(f32[128,512]{1,0:T(8,128)} %collective-permute-done.1), channel_id=1, source_target_pairs={{8,0},{12,4},{16,24},{20,28},{9,1},{13,5},{17,25},{21,29},{10,2},{... | collective-permute-start | bytes 786440 | tf_op jit(solution)/shard_map/ppermute | solution.py:35
  17.7 2.1 %collective-permute-done.3 = f32[128,512]{1,0:T(8,128)} collective-permute-done((f32[128,512]{1,0:T(8,128)}, f32[128,512]{1,0:T(8,128)}, u32[]{:S(2)}, u32[]{:S(2)}) %collective-permute-start.3) | collective-permute-done | bytes 262176 | tf_op jit(solution)/shard_map/ppermute | solution.py:35
  19.8 6.6 %collective-permute-done.6 = f32[128,512]{1,0:T(8,128)S(1)} collective-permute-done((f32[128,512]{1,0:T(8,128)}, f32[128,512]{1,0:T(8,128)S(1)}, u32[]{:S(2)}, u32[]{:S(2)}) %collective-permute-start.6) | collective-permute-done | bytes 262176 | tf_op jit(solution)/shard_map/ppermute | solution.py:35
  26.5 1.0 %broadcast_select_fusion.6 = (f32[128,512]{1,0:T(8,128)S(1)}, f32[128,512]{1,0:T(8,128)S(1)}) fusion(f32[128,512]{1,0:T(8,128)} %collective-permute-done.1, f32[128,512]{1,0:T(8,128)S(1)} %collective-permute-done.2, pred[]{:T(512)S(6)} %eq.4), kind=kLoop, calls=%fused_computation.29 | loop fusion | flops 131072 | bytes 1048577 | tf_op jit(solution)/shard_map/jit(_where)/select_n | solution.py:41
  27.5 0.6 %fusion.3 = f32[512,256]{0,1:T(8,128)S(1)} fusion(f32[512,512]{1,0:T(8,128)S(1)} %copy-done, f32[512,1,256]{0,2,1:T(8,128)S(1)} %copy.3, f32[128,512]{1,0:T(8,128)S(1)} %get-tuple-element.18, f32[128,512]{1,0:T(8,128)S(1)} %get-tuple-element.17), kind=kOutput, calls=%fused_computation.8 | convolution fusion | flops 402915328 | bytes 2621440 | tf_op jit(solution)/shard_map/dot_general | solution.py:10
  29.4 0.6 %convolution_add_fusion.1 = f32[512,512]{1,0:T(8,128)S(1)} fusion(f32[512,512]{1,0:T(8,128)S(1)} %fusion.6, f32[512,256]{0,1:T(8,128)S(1)} %fusion.3, f32[128,512]{1,0:T(8,128)S(1)} %get-tuple-element.18, f32[128,512]{1,0:T(8,128)S(1)} %get-tuple-element.17), kind=kOutput, calls=%fused_computation.2 | convolution fusion | flops 403046400 | bytes 3145728 | tf_op jit(solution)/shard_map/dot_general | solution.py:10
  30.0 1.0 %broadcast_select_fusion.4 = (f32[128,512]{1,0:T(8,128)S(1)}, f32[128,512]{1,0:T(8,128)S(1)}) fusion(f32[128,512]{1,0:T(8,128)} %collective-permute-done.3, f32[128,512]{1,0:T(8,128)S(1)} %collective-permute-done.4, pred[]{:T(512)S(6)} %eq.4), kind=kLoop, calls=%fused_computation.27 | loop fusion | flops 131072 | bytes 1048577 | tf_op jit(solution)/shard_map/jit(_where)/select_n | solution.py:41
  31.0 0.6 %fusion.2 = f32[512,256]{1,0:T(8,128)S(1)} fusion(f32[512,512]{1,0:T(8,128)S(1)} %copy-done, f32[512,1,256]{2,1,0:T(1,128)S(1)} %get-tuple-element.5, f32[128,512]{1,0:T(8,128)S(1)} %get-tuple-element.12, f32[128,512]{1,0:T(8,128)S(1)} %get-tuple-element.11), kind=kOutput, calls=%fused_computation.6 | convolution fusion | flops 402915328 | bytes 2621440 | tf_op jit(solution)/shard_map/dot_general | solution.py:10
  32.9 0.6 %fusion = f32[512,512]{1,0:T(8,128)S(1)} fusion(f32[512,512]{1,0:T(8,128)S(1)} %fusion.5, f32[512,512]{1,0:T(8,128)S(1)} %convolution_add_fusion.1, f32[512,256]{1,0:T(8,128)S(1)} %fusion.2, f32[128,512]{1,0:T(8,128)S(1)} %get-tuple-element.12, f32[128,512]{1,0:T(8,128)S(1)} %get-tuple-element.11), kind=kOutput, calls=%fused_computation.1 | convolution fusion | flops 403308544 | bytes 4194304 | tf_op jit(solution)/shard_map/dot_general | solution.py:10
  33.7 1.6 %collective-permute-start.8 = (f32[2,1,128,256]{3,2,1,0:T(8,128)S(1)}, f32[2,1,128,256]{3,2,1,0:T(8,128)S(1)}, u32[]{:S(2)}, u32[]{:S(2)}) collective-permute-start(f32[2,1,128,256]{3,2,1,0:T(8,128)S(1)} %constant_dynamic-slice_fusion.4), channel_id=1, source_target_pairs={{0,1},{1,0},{2,3},{3,2},{4,5},{5,4},{6,7},{7,6},{8,9},{9,8},{10,11... | collective-permute-start | bytes 786440 | tf_op jit(solution)/shard_map/ppermute | solution.py:91
  35.2 1.6 %collective-permute-start.10 = (f32[1,2,128,256]{3,2,1,0:T(8,128)S(1)}, f32[1,2,128,256]{3,2,1,0:T(8,128)S(1)}, u32[]{:S(2)}, u32[]{:S(2)}) collective-permute-start(f32[1,2,128,256]{3,2,1,0:T(8,128)S(1)} %constant_dynamic-slice_fusion.2), channel_id=1, source_target_pairs={{0,2},{1,3},{2,0},{3,1},{4,6},{5,7},{6,4},{7,5},{8,10},{9,11},{10,... | collective-permute-start | bytes 786440 | tf_op jit(solution)/shard_map/ppermute | solution.py:91
  36.9 1.3 %collective-permute-start.13 = (f32[128,512]{1,0:T(8,128)S(1)}, f32[128,512]{1,0:T(8,128)S(1)}, u32[]{:S(2)}, u32[]{:S(2)}) collective-permute-start(f32[128,512]{1,0:T(8,128)S(1)} %dynamic-slice_add_fusion), channel_id=1, source_target_pairs={{8,24},{12,28},{16,0},{20,4},{9,25},{13,29},{17,1},{21,5},{10,26},... | collective-permute-start | bytes 786440 | tf_op jit(solution)/shard_map/ppermute | solution.py:35
  38.2 3.8 %collective-permute-done.8 = f32[2,1,128,256]{3,2,1,0:T(8,128)S(1)} collective-permute-done((f32[2,1,128,256]{3,2,1,0:T(8,128)S(1)}, f32[2,1,128,256]{3,2,1,0:T(8,128)S(1)}, u32[]{:S(2)}, u32[]{:S(2)}) %collective-permute-start.8) | collective-permute-done | bytes 262176 | tf_op jit(solution)/shard_map/ppermute | solution.py:91
  42.0 1.6 %collective-permute-start.9 = (f32[1,1,128,256]{3,2,1,0:T(8,128)S(1)}, f32[1,1,128,256]{3,2,1,0:T(8,128)S(1)}, u32[]{:S(2)}, u32[]{:S(2)}) collective-permute-start(f32[1,1,128,256]{3,2,1,0:T(8,128)S(1)} %constant_dynamic-slice_fusion.3), channel_id=1, source_target_pairs={{0,2},{1,3},{2,0},{3,1},{4,6},{5,7},{6,4},{7,5},{8,10},{9,11},{10,... | collective-permute-start | bytes 393224 | tf_op jit(solution)/shard_map/ppermute | solution.py:91
  43.7 1.5 %collective-permute-start.11 = (f32[1,1,128,256]{3,2,1,0:T(8,128)S(1)}, f32[1,1,128,256]{3,2,1,0:T(8,128)S(1)}, u32[]{:S(2)}, u32[]{:S(2)}) collective-permute-start(f32[1,1,128,256]{3,2,1,0:T(8,128)S(1)} %constant_dynamic-slice_fusion.1), channel_id=1, source_target_pairs={{0,1},{1,0},{2,3},{3,2},{4,5},{5,4},{6,7},{7,6},{8,9},{9,8},{10,11... | collective-permute-start | bytes 393224 | tf_op jit(solution)/shard_map/ppermute | solution.py:91
  45.2 1.8 %collective-permute-done.9 = f32[1,1,128,256]{3,2,1,0:T(8,128)S(1)} collective-permute-done((f32[1,1,128,256]{3,2,1,0:T(8,128)S(1)}, f32[1,1,128,256]{3,2,1,0:T(8,128)S(1)}, u32[]{:S(2)}, u32[]{:S(2)}) %collective-permute-start.9) | collective-permute-done | bytes 131104 | tf_op jit(solution)/shard_map/ppermute | solution.py:91
  47.1 1.6 %collective-permute-done.11 = f32[1,1,128,256]{3,2,1,0:T(8,128)S(1)} collective-permute-done((f32[1,1,128,256]{3,2,1,0:T(8,128)S(1)}, f32[1,1,128,256]{3,2,1,0:T(8,128)S(1)}, u32[]{:S(2)}, u32[]{:S(2)}) %collective-permute-start.11) | collective-permute-done | bytes 131104 | tf_op jit(solution)/shard_map/ppermute | solution.py:91
  48.8 0.7 %maximum_add_fusion = f32[128,512]{1,0:T(8,128)} fusion(f32[128,512]{1,0:T(8,128)S(1)} %collective-permute-done.13, f32[128,256]{1,0:T(8,128)S(1)} %add_bitcast_fusion, f32[128,256]{1,0:T(8,128)S(1)} %add_bitcast_fusion.1), kind=kLoop, calls=%fused_computation.17 | loop fusion | flops 131072 | bytes 786432 | tf_op jit(solution)/shard_map/add | solution.py:94
  (35 shorter events, 4.3 us)
Async XLA Ops:
  1.7 13.1 %collective-permute-start = (f32[128,512]{1,0:T(8,128)}, f32[128,512]{1,0:T(8,128)S(1)}, u32[]{:S(2)}, u32[]{:S(2)}) collective-permute-start(f32[128,512]{1,0:T(8,128)} %constant_dynamic-slice_fusion.8), channel_id=1, source_target_pairs={{0,4},{4,0},{8,12},{12,8},{16,20},{20,16},{24,28},{28,24},{1,5},{5... | collective-permute-start | bytes 786440 | tf_op jit(solution)/shard_map/ppermute | solution.py:38
  2.1 13.4 %collective-permute-start.1 = (f32[128,512]{1,0:T(8,128)}, f32[128,512]{1,0:T(8,128)}, u32[]{:S(2)}, u32[]{:S(2)}) collective-permute-start(f32[128,512]{1,0:T(8,128)} %constant_dynamic-slice_fusion.8), channel_id=1, source_target_pairs={{0,16},{4,20},{24,8},{28,12},{1,17},{5,21},{25,9},{29,13},{2,18},{... | collective-permute-start | bytes 786440 | tf_op jit(solution)/shard_map/ppermute | solution.py:35
  8.3 11.5 %collective-permute-start.5 = (f32[128,512]{1,0:T(8,128)}, f32[128,512]{1,0:T(8,128)}, u32[]{:S(2)}, u32[]{:S(2)}) collective-permute-start(f32[128,512]{1,0:T(8,128)} %constant_dynamic-slice_fusion.8), channel_id=1, source_target_pairs={{8,16},{12,20},{16,8},{20,12},{9,17},{13,21},{17,9},{21,13},{10,18... | collective-permute-start | bytes 786440 | tf_op jit(solution)/shard_map/ppermute | solution.py:35
  9.7 10.1 %collective-permute-start.3 = (f32[128,512]{1,0:T(8,128)}, f32[128,512]{1,0:T(8,128)}, u32[]{:S(2)}, u32[]{:S(2)}) collective-permute-start(f32[128,512]{1,0:T(8,128)} %constant_dynamic-slice_fusion.8), channel_id=1, source_target_pairs={{0,8},{4,12},{8,0},{12,4},{16,24},{20,28},{24,16},{28,20},{1,9},{5... | collective-permute-start | bytes 786440 | tf_op jit(solution)/shard_map/ppermute | solution.py:35
  9.7 5.1 %copy-start = (f32[512,512]{1,0:T(8,128)S(1)}, f32[512,512]{1,0:T(8,128)}, u32[]{:S(2)}) copy-start(f32[512,512]{1,0:T(8,128)} %param.2) | copy-start | bytes 3145732
  15.5 11.0 %collective-permute-start.2 = (f32[128,512]{1,0:T(8,128)}, f32[128,512]{1,0:T(8,128)S(1)}, u32[]{:S(2)}, u32[]{:S(2)}) collective-permute-start(f32[128,512]{1,0:T(8,128)} %collective-permute-done.1), channel_id=1, source_target_pairs={{0,4},{4,0},{8,12},{12,8},{16,20},{20,16},{24,28},{28,24},{1,5},{5... | collective-permute-start | bytes 786440 | tf_op jit(solution)/shard_map/ppermute | solution.py:38
  15.8 10.6 %collective-permute-start.6 = (f32[128,512]{1,0:T(8,128)}, f32[128,512]{1,0:T(8,128)S(1)}, u32[]{:S(2)}, u32[]{:S(2)}) collective-permute-start(f32[128,512]{1,0:T(8,128)} %collective-permute-done.1), channel_id=1, source_target_pairs={{8,0},{12,4},{16,24},{20,28},{9,1},{13,5},{17,25},{21,29},{10,2},{... | collective-permute-start | bytes 786440 | tf_op jit(solution)/shard_map/ppermute | solution.py:35
  19.8 10.2 %collective-permute-start.4 = (f32[128,512]{1,0:T(8,128)}, f32[128,512]{1,0:T(8,128)S(1)}, u32[]{:S(2)}, u32[]{:S(2)}) collective-permute-start(f32[128,512]{1,0:T(8,128)} %collective-permute-done.3), channel_id=1, source_target_pairs={{0,4},{4,0},{8,12},{12,8},{16,20},{20,16},{24,28},{28,24},{1,5},{5... | collective-permute-start | bytes 786440 | tf_op jit(solution)/shard_map/ppermute | solution.py:38
  26.4 5.2 %collective-permute-start.7 = (f32[128,512]{1,0:T(8,128)S(1)}, f32[128,512]{1,0:T(8,128)S(1)}, u32[]{:S(2)}, u32[]{:S(2)}) collective-permute-start(f32[128,512]{1,0:T(8,128)S(1)} %broadcast_select_fusion), channel_id=1, source_target_pairs={{0,4},{4,0},{8,12},{12,8},{16,20},{20,16},{24,28},{28,24},{1,5},{5... | collective-permute-start | bytes 786440 | tf_op jit(solution)/shard_map/ppermute | solution.py:38
  28.8 8.0 %collective-permute-start.12 = (f32[128,512]{1,0:T(8,128)S(1)}, f32[128,512]{1,0:T(8,128)S(1)}, u32[]{:S(2)}, u32[]{:S(2)}) collective-permute-start(f32[128,512]{1,0:T(8,128)S(1)} %constant_dynamic-slice_fusion), channel_id=1, source_target_pairs={{0,4},{4,0},{8,12},{12,8},{16,20},{20,16},{24,28},{28,24},{1,5},{5... | collective-permute-start | bytes 786440 | tf_op jit(solution)/shard_map/ppermute | solution.py:38
  33.7 8.3 %collective-permute-start.8 = (f32[2,1,128,256]{3,2,1,0:T(8,128)S(1)}, f32[2,1,128,256]{3,2,1,0:T(8,128)S(1)}, u32[]{:S(2)}, u32[]{:S(2)}) collective-permute-start(f32[2,1,128,256]{3,2,1,0:T(8,128)S(1)} %constant_dynamic-slice_fusion.4), channel_id=1, source_target_pairs={{0,1},{1,0},{2,3},{3,2},{4,5},{5,4},{6,7},{7,6},{8,9},{9,8},{10,11... | collective-permute-start | bytes 786440 | tf_op jit(solution)/shard_map/ppermute | solution.py:91
  35.2 8.4 %collective-permute-start.10 = (f32[1,2,128,256]{3,2,1,0:T(8,128)S(1)}, f32[1,2,128,256]{3,2,1,0:T(8,128)S(1)}, u32[]{:S(2)}, u32[]{:S(2)}) collective-permute-start(f32[1,2,128,256]{3,2,1,0:T(8,128)S(1)} %constant_dynamic-slice_fusion.2), channel_id=1, source_target_pairs={{0,2},{1,3},{2,0},{3,1},{4,6},{5,7},{6,4},{7,5},{8,10},{9,11},{10,... | collective-permute-start | bytes 786440 | tf_op jit(solution)/shard_map/ppermute | solution.py:91
  36.9 11.9 %collective-permute-start.13 = (f32[128,512]{1,0:T(8,128)S(1)}, f32[128,512]{1,0:T(8,128)S(1)}, u32[]{:S(2)}, u32[]{:S(2)}) collective-permute-start(f32[128,512]{1,0:T(8,128)S(1)} %dynamic-slice_add_fusion), channel_id=1, source_target_pairs={{8,24},{12,28},{16,0},{20,4},{9,25},{13,29},{17,1},{21,5},{10,26},... | collective-permute-start | bytes 786440 | tf_op jit(solution)/shard_map/ppermute | solution.py:35
  42.0 5.0 %collective-permute-start.9 = (f32[1,1,128,256]{3,2,1,0:T(8,128)S(1)}, f32[1,1,128,256]{3,2,1,0:T(8,128)S(1)}, u32[]{:S(2)}, u32[]{:S(2)}) collective-permute-start(f32[1,1,128,256]{3,2,1,0:T(8,128)S(1)} %constant_dynamic-slice_fusion.3), channel_id=1, source_target_pairs={{0,2},{1,3},{2,0},{3,1},{4,6},{5,7},{6,4},{7,5},{8,10},{9,11},{10,... | collective-permute-start | bytes 393224 | tf_op jit(solution)/shard_map/ppermute | solution.py:91
  43.7 5.0 %collective-permute-start.11 = (f32[1,1,128,256]{3,2,1,0:T(8,128)S(1)}, f32[1,1,128,256]{3,2,1,0:T(8,128)S(1)}, u32[]{:S(2)}, u32[]{:S(2)}) collective-permute-start(f32[1,1,128,256]{3,2,1,0:T(8,128)S(1)} %constant_dynamic-slice_fusion.1), channel_id=1, source_target_pairs={{0,1},{1,0},{2,3},{3,2},{4,5},{5,4},{6,7},{7,6},{8,9},{9,8},{10,11... | collective-permute-start | bytes 393224 | tf_op jit(solution)/shard_map/ppermute | solution.py:91

commit v2 on v0

v2 whole, which is shorter than its diff:
```python
import jax
import jax.numpy as jnp
from jax import lax
from jax.experimental import pallas as pl
from jax.experimental.pallas import tpu as pltpu
from jax.sharding import PartitionSpec as P

CORES = 2
LANES = 128
MIB = 1 << 20


def product(a, b, dims):
    return lax.dot_general(
        a, b, (dims, ((), ())), precision=lax.Precision.HIGH, preferred_element_type=jnp.float32
    )


def pick_body(at_ref, kernel_ref, *out_refs):
    share = out_refs[0].shape[1] // CORES
    for i, out_ref in enumerate(out_refs):
        for c in range(CORES):
            start = pl.multiple_of(at_ref[i * CORES + c] * share, share)
            out_ref[:, c * share : (c + 1) * share] = kernel_ref[:, 0, pl.ds(start, share)]


def pick_columns(kernel, blocks, share):
    rows, count = kernel.shape[0], len(blocks) // CORES
    if share % LANES:
        flat = kernel[:, 0, :]
        parts = [lax.dynamic_slice_in_dim(flat, b * share, share, 1) for b in blocks]
        return [jnp.concatenate(parts[i * CORES : (i + 1) * CORES], axis=1) for i in range(count)]
    return pl.pallas_call(
        pick_body,
        in_specs=[
            pl.BlockSpec(memory_space=pltpu.SMEM),
            pl.BlockSpec(memory_space=pltpu.VMEM),
        ],
        out_specs=[pl.BlockSpec(memory_space=pltpu.VMEM)] * count,
        out_shape=[jax.ShapeDtypeStruct((rows, CORES * share), jnp.float32)] * count,
        compiler_params=pltpu.CompilerParams(vmem_limit_bytes=16 * MIB),
        cost_estimate=pl.CostEstimate(flops=0, bytes_accessed=4 * kernel.size, transcendentals=0),
    )(jnp.stack(blocks).astype(jnp.int32), kernel)


def per_device(orbitals, kernel):
    nchips = lax.axis_size("blk") // CORES
    nshares = lax.axis_size("split")
    q = lax.axis_index("blk")
    share_id = lax.axis_index("split")
    chip = q // CORES
    share = orbitals.shape[0] // nshares
    half, near = nchips // 2, nchips // 4
    across = half ^ near

    def is_inner(c):
        return (c // half) != (c // near) % 2

    inner_chips = [c for c in range(nchips) if is_inner(c)]
    outer_chips = [c for c in range(nchips) if not is_inner(c)]
    inner = (chip // half) != (chip // near) % 2

    def along(value, pairs):
        full = [(CORES * a + c, CORES * b + c) for a, b in pairs for c in range(CORES)]
        return lax.ppermute(value, "blk", full)

    def other_core(value):
        return lax.ppermute(value, "blk", [(i, i ^ 1) for i in range(nchips * CORES)])

    own = lax.dynamic_slice_in_dim(orbitals, share_id * share, share, 0)
    pair_own = other_core(own)
    x = along(own, [(c, c ^ half) for c in outer_chips] + [(c, c ^ near) for c in inner_chips])

    others = [k for k in range(1, nchips) if k not in (near, half, across)]
    blocks = []
    for k in [0, jnp.where(inner, half, near), across] + others:
        blocks += [q ^ (CORES * k), q ^ (CORES * k + 1)]
    z_own, z_x, z_late, *z_others = pick_columns(kernel, blocks, share)

    def weighted(z_part, points):
        return z_part * product(orbitals, points, ((1,), (1,)))

    def rows_of(weights, points):
        return product(weights, points, ((1,), (0,)))

    points = jnp.concatenate([own, pair_own], axis=0)
    total = rows_of(weighted(z_own, points), points)

    own_late, z_x, z_late = lax.optimization_barrier((own, z_x, z_late))
    swapped = along(own_late, [(c, c ^ across) for c in inner_chips])

    for k, z_k in zip(others, z_others):
        more = along(own_late, [(c, c ^ k) for c in range(nchips)])
        points = jnp.concatenate([more, other_core(more)], axis=0)
        total += rows_of(weighted(z_k, points), points)

    passed = along(x, [(c, c ^ near) for c in range(nchips)])
    points = jnp.concatenate([x, other_core(x)], axis=0)
    weights = weighted(z_x, points)
    back = product(weights, orbitals, ((0,), (0,)))
    back = back[:share] + other_core(back[share:])
    total += rows_of(weights, points)

    total, back, passed, swapped = lax.optimization_barrier((total, back, passed, swapped))
    late = jnp.where(inner, swapped, passed)
    late, back = lax.optimization_barrier((late, back))
    points = jnp.concatenate([late, other_core(late)], axis=0)
    returned = along(
        back, [(c, c ^ half) for c in inner_chips] + [(c, c ^ near) for c in outer_chips]
    )
    total += rows_of(weighted(z_late, points), points)

    def for_share(at):
        return lax.dynamic_slice_in_dim(total, at * share, share, 0)

    out = for_share(share_id) + returned
    masks = sorted(range(1, nshares), key=lambda mask: -mask.bit_count())
    for mask in masks:
        out += lax.ppermute(
            for_share(share_id ^ mask), "split", [(i, i ^ mask) for i in range(nshares)]
        )
    return out


def solution(mesh):
    placed = (P("blk", None), P("blk", "split", None))
    return jax.shard_map(
        per_device, mesh=mesh, in_specs=placed, out_specs=P(("blk", "split"), None), check_vma=False
    )
```

time: 85.1 us -> 40 us (0.47)
  waiting for transfers between devices: 59.6 us -> 17.3 us
  between operations: 13.4 us -> 0.2 us
  starting transfers between devices: 0.04 us -> 12.8 us
  matrix products: 9.96 us -> 4.24 us
  local copies, waits for them, and re-layouts: 1.95 us -> 3.08 us
  other arithmetic: 0 us -> 1.09 us
  Pallas kernels: 0 us -> 1.06 us
    all_gather x1 -> x0, waiting for transfers between devices: 32.2 us -> none  [per_device(): piece = lax.all_gather(own, 'blk', axis=0, tiled=True)]
    reduce_scatter x1 -> x0, waiting for transfers between devices: 27.3 us -> none  [per_device(): folded = lax.psum_scatter(home, 'split', scatter_dimension=0, tiled=True)]
    ppermute x0 -> x11, waiting for transfers between devices: none -> 17.3 us  [the longest x3 8.9 us: per_device(): lax.ppermute(for_share(share_id ^ mask), 'split', [(i, i ^ mask) for i in...]
    ppermute x0 -> x11, starting transfers between devices: none -> 12.8 us  [the longest x4 8.93 us: along(): return lax.ppermute(value, 'blk', full)]
    dot_general x2 -> x7, matrix products: 9.96 us -> 4.24 us  [product(): lax.dot_general(a, b, (dims, ((), ())), precision=lax.Precision.HIGH, pre...]
    unnamed x6, local copies, waits for them, and re-layouts: 1.23 us -> 2.85 us
    add x0 -> x3, other arithmetic: none -> 1.06 us  [the longest x1 0.81 us: per_device(): out += lax.ppermute(for_share(share_id ^ mask), 'split', [(i, i ^ mask) f...]
    pallas_call x0 -> x1, Pallas kernels: none -> 1.06 us  [pick_columns(): pl.pallas_call(pick_body, in_specs=[pl.BlockSpec(memory_space=pltpu.SMEM)...]
  transfers between devices with their start and end apart: 2 -> 11, of which waited for: 2 -> 7; matrix products, arithmetic and copies ran while one was open for 0% -> 12% of each run, Pallas kernels for 0% -> 3%
where the time goes in v2:
time: 40 us; the launch traced here: 39.8 us
  waiting for transfers between devices  17.3 us (43%)
  starting transfers between devices  12.8 us (32%)
  matrix products  4.24 us (11%)
  local copies, waits for them, and re-layouts  3.08 us (8%)
  other arithmetic  1.09 us (3%)
  Pallas kernels  1.06 us (3%)
    ppermute x4, starting transfers between devices, along(): return lax.ppermute(value, 'blk', full)  8.93 us
    ppermute x3, waiting for transfers between devices, per_device(): lax.ppermute(for_share(share_id ^ mask), 'split', [(i, i ^ mask) for i in...  8.9 us
    ppermute x4, waiting for transfers between devices, along(): return lax.ppermute(value, 'blk', full)  7.66 us
    dot_general x7, matrix products, product(): lax.dot_general(a, b, (dims, ((), ())), precision=lax.Precision.HIGH, pre...  4.24 us
    ppermute x3, starting transfers between devices, per_device(): lax.ppermute(for_share(share_id ^ mask), 'split', [(i, i ^ mask) for i in...  3.55 us
    unnamed x6, local copies, waits for them, and re-layouts  2.85 us
    pallas_call x1, Pallas kernels, pick_columns(): pl.pallas_call(pick_body, in_specs=[pl.BlockSpec(memory_space=pltpu.SMEM)...  1.06 us
    add x1, other arithmetic, per_device(): out += lax.ppermute(for_share(share_id ^ mask), 'split', [(i, i ^ mask) f...  0.81 us
  transfers between devices with their start and end apart: 11, of which 7 were waited for; matrix products, arithmetic and copies ran while one was open for 12% of the time, Pallas kernels for 3%

profile of v2, /device:TPU:0, one launch (start us, length us, event | category | flops | bytes accessed | tf_op | source)
XLA Modules:
  0.0 39.8 jit_solution(17387543140520168598)
XLA Ops:
  0.0 1.2 %copy-done = f32[512,512]{1,0:T(8,128)S(1)} copy-done((f32[512,512]{1,0:T(8,128)S(1)}, f32[512,512]{1,0:T(8,128)}, u32[]{:S(2)}) %copy-start) | copy-done | bytes 1048600
  1.2 4.1 %collective-permute-start.1 = (f32[128,512]{1,0:T(8,128)S(1)}, f32[128,512]{1,0:T(8,128)S(1)}, u32[]{:S(2)}, u32[]{:S(2)}) collective-permute-start(f32[128,512]{1,0:T(8,128)S(1)} %constant_dynamic-slice_fusion.3), channel_id=1, source_target_pairs={{0,16},{4,20},{24,8},{28,12},{8,0},{12,4},{16,24},{20,28},{1,17},{... | collective-permute-start | bytes 786440 | tf_op jit(solution)/shard_map/ppermute | solution.py:65
  5.4 1.6 %copy-done.1 = f32[512,1,1024]{2,1,0:T(1,128)S(1)} copy-done((f32[512,1,1024]{2,1,0:T(1,128)S(1)}, f32[512,1,1024]{2,1,0:T(1,128)}, u32[]{:S(2)}) %copy-start.1) | copy-done | bytes 2097176
  7.0 1.1 %shard_map.28 = (f32[512,256]{1,0:T(8,128)S(1)}, f32[512,256]{1,0:T(8,128)S(1)}, f32[512,256]{1,0:T(8,128)S(1)}) custom-call(s32[6]{0:T(128)S(1)} %stack.27.at_ref, f32[512,1,1024]{2,1,0:T(1,128)S(1)} %copy-done.1), custom_call_target="tpu_custom_call" | custom-call | bytes 2097152 | tf_op jit(solution)/shard_map/pallas_call | solution.py:33
  8.1 0.7 %collective-permute-start.5 = (f32[128,512]{1,0:T(8,128)S(1)}, f32[128,512]{1,0:T(8,128)S(1)}, u32[]{:S(2)}, u32[]{:S(2)}) collective-permute-start(f32[128,512]{1,0:T(8,128)S(1)} %constant_dynamic-slice_fusion.3), channel_id=1, source_target_pairs={{8,16},{12,20},{16,8},{20,12},{9,17},{13,21},{17,9},{21,13},{10,18... | collective-permute-start | bytes 786440 | tf_op jit(solution)/shard_map/ppermute | solution.py:65
  8.8 2.1 %collective-permute-done.1 = f32[128,512]{1,0:T(8,128)S(1)} collective-permute-done((f32[128,512]{1,0:T(8,128)S(1)}, f32[128,512]{1,0:T(8,128)S(1)}, u32[]{:S(2)}, u32[]{:S(2)}) %collective-permute-start.1) | collective-permute-done | bytes 262176 | tf_op jit(solution)/shard_map/ppermute | solution.py:65
  10.9 2.4 %collective-permute-start.4 = (f32[128,512]{1,0:T(8,128)S(1)}, f32[128,512]{1,0:T(8,128)S(1)}, u32[]{:S(2)}, u32[]{:S(2)}) collective-permute-start(f32[128,512]{1,0:T(8,128)S(1)} %collective-permute-done.1), channel_id=1, source_target_pairs={{0,8},{4,12},{8,0},{12,4},{16,24},{20,28},{24,16},{28,20},{1,9},{5... | collective-permute-start | bytes 786440 | tf_op jit(solution)/shard_map/ppermute | solution.py:65
  13.3 0.6 %fusion.2 = f32[512,256]{1,0:T(8,128)S(1)} fusion(f32[512,256]{1,0:T(8,128)S(1)} %get-tuple-element.17, f32[512,512]{1,0:T(8,128)S(1)} %copy-done, f32[128,512]{1,0:T(8,128)S(1)} %collective-permute-done, f32[128,512]{1,0:T(8,128)S(1)} %constant_dynamic-slice_fusion.3), kind=kOutput, calls=%fused_computation.6 | convolution fusion | flops 402915328 | bytes 2621440 | tf_op jit(solution)/shard_map/dot_general | solution.py:14
  13.9 0.6 %fusion.3 = f32[512,512]{1,0:T(8,128)S(1)} fusion(f32[512,256]{1,0:T(8,128)S(1)} %fusion.2, f32[128,512]{1,0:T(8,128)S(1)} %collective-permute-done, f32[128,512]{1,0:T(8,128)S(1)} %constant_dynamic-slice_fusion.3), kind=kOutput, calls=%fused_computation.8 | convolution fusion | flops 402784256 | bytes 2097152 | tf_op jit(solution)/shard_map/dot_general | solution.py:14
  14.6 0.6 %fusion.1 = f32[512,256]{1,0:T(8,128)S(1)} fusion(f32[512,256]{1,0:T(8,128)S(1)} %get-tuple-element.20, f32[256,512]{1,0:T(8,128)S(1)} %constant_dynamic-update-slice_fusion, f32[512,512]{1,0:T(8,128)S(1)} %copy-done), kind=kOutput, calls=%fused_computation.4 | convolution fusion | flops 402784256 | bytes 2621440 | tf_op jit(solution)/shard_map/dot_general | solution.py:14
  15.2 0.6 %fusion.6 = f32[256,512]{1,0:T(8,128)S(1)} fusion(f32[512,256]{1,0:T(8,128)S(1)} %fusion.1, f32[512,512]{1,0:T(8,128)S(1)} %copy-done), kind=kOutput, calls=%fused_computation.22 | convolution fusion | flops 402653184 | bytes 2097152 | tf_op jit(solution)/shard_map/dot_general | solution.py:14
  16.1 0.6 %convolution_add_fusion = f32[512,512]{1,0:T(8,128)S(1)} fusion(f32[512,512]{1,0:T(8,128)S(1)} %fusion.3, f32[512,256]{1,0:T(8,128)S(1)} %fusion.1, f32[256,512]{1,0:T(8,128)S(1)} %constant_dynamic-update-slice_fusion), kind=kOutput, calls=%fused_computation | convolution fusion | flops 402915328 | bytes 3145728 | tf_op jit(solution)/shard_map/dot_general | solution.py:14
  16.7 0.7 %collective-permute-done.3 = f32[128,512]{1,0:T(8,128)S(1)} collective-permute-done((f32[128,512]{1,0:T(8,128)S(1)}, f32[128,512]{1,0:T(8,128)S(1)}, u32[]{:S(2)}, u32[]{:S(2)}) %collective-permute-start.3) | collective-permute-done | bytes 262176 | tf_op jit(solution)/shard_map/ppermute | solution.py:68
  17.5 2.7 %collective-permute-done.4 = f32[128,512]{1,0:T(8,128)S(1)} collective-permute-done((f32[128,512]{1,0:T(8,128)S(1)}, f32[128,512]{1,0:T(8,128)S(1)}, u32[]{:S(2)}, u32[]{:S(2)}) %collective-permute-start.4) | collective-permute-done | bytes 262176 | tf_op jit(solution)/shard_map/ppermute | solution.py:65
  20.4 1.8 %collective-permute-start.7 = (f32[128,512]{1,0:T(8,128)S(1)}, f32[128,512]{1,0:T(8,128)S(1)}, u32[]{:S(2)}, u32[]{:S(2)}) collective-permute-start(f32[128,512]{1,0:T(8,128)S(1)} %slice_add_fusion), channel_id=1, source_target_pairs={{8,24},{12,28},{16,0},{20,4},{0,8},{4,12},{24,16},{28,20},{9,25},{... | collective-permute-start | bytes 786440 | tf_op jit(solution)/shard_map/ppermute | solution.py:65
  22.2 0.6 %fusion = f32[512,256]{1,0:T(8,128)S(1)} fusion(f32[512,256]{1,0:T(8,128)S(1)} %get-tuple-element.23, f32[256,512]{1,0:T(8,128)S(1)} %constant_dynamic-update-slice_fusion.2, f32[512,512]{1,0:T(8,128)S(1)} %copy-done), kind=kOutput, calls=%fused_computation.2 | convolution fusion | flops 402784256 | bytes 2621440 | tf_op jit(solution)/shard_map/dot_general | solution.py:14
  22.9 0.6 %fusion.7 = f32[512,512]{1,0:T(8,128)S(1)} fusion(f32[512,256]{1,0:T(8,128)S(1)} %fusion, f32[256,512]{1,0:T(8,128)S(1)} %constant_dynamic-update-slice_fusion.2), kind=kOutput, calls=%fused_computation.23 | convolution fusion | flops 402653184 | bytes 2097152 | tf_op jit(solution)/shard_map/dot_general | solution.py:14
  23.8 1.6 %collective-permute-start.10 = (f32[128,512]{1,0:T(8,128)S(1)}, f32[128,512]{1,0:T(8,128)S(1)}, u32[]{:S(2)}, u32[]{:S(2)}) collective-permute-start(f32[128,512]{1,0:T(8,128)S(1)} %get-tuple-element.30), channel_id=1, source_target_pairs={{0,2},{1,3},{2,0},{3,1},{4,6},{5,7},{6,4},{7,5},{8,10},{9,11},{10,... | collective-permute-start | bytes 786440 | tf_op jit(solution)/shard_map/ppermute | solution.py:119
  25.3 1.5 %collective-permute-start.9 = (f32[128,512]{1,0:T(8,128)S(1)}, f32[128,512]{1,0:T(8,128)S(1)}, u32[]{:S(2)}, u32[]{:S(2)}) collective-permute-start(f32[128,512]{1,0:T(8,128)S(1)} %get-tuple-element.31), channel_id=1, source_target_pairs={{0,1},{1,0},{2,3},{3,2},{4,5},{5,4},{6,7},{7,6},{8,9},{9,8},{10,11... | collective-permute-start | bytes 786440 | tf_op jit(solution)/shard_map/ppermute | solution.py:119
  27.3 2.8 %collective-permute-done.7 = f32[128,512]{1,0:T(8,128)S(1)} collective-permute-done((f32[128,512]{1,0:T(8,128)S(1)}, f32[128,512]{1,0:T(8,128)S(1)}, u32[]{:S(2)}, u32[]{:S(2)}) %collective-permute-start.7) | collective-permute-done | bytes 262176 | tf_op jit(solution)/shard_map/ppermute | solution.py:65
  30.1 2.1 %collective-permute-done.10 = f32[128,512]{1,0:T(8,128)S(1)} collective-permute-done((f32[128,512]{1,0:T(8,128)S(1)}, f32[128,512]{1,0:T(8,128)S(1)}, u32[]{:S(2)}, u32[]{:S(2)}) %collective-permute-start.10) | collective-permute-done | bytes 262176 | tf_op jit(solution)/shard_map/ppermute | solution.py:119
  32.2 2.3 %collective-permute-done.9 = f32[128,512]{1,0:T(8,128)S(1)} collective-permute-done((f32[128,512]{1,0:T(8,128)S(1)}, f32[128,512]{1,0:T(8,128)S(1)}, u32[]{:S(2)}, u32[]{:S(2)}) %collective-permute-start.9) | collective-permute-done | bytes 262176 | tf_op jit(solution)/shard_map/ppermute | solution.py:119
  34.5 4.5 %collective-permute-done.8 = f32[128,512]{1,0:T(8,128)S(1)} collective-permute-done((f32[128,512]{1,0:T(8,128)S(1)}, f32[128,512]{1,0:T(8,128)S(1)}, u32[]{:S(2)}, u32[]{:S(2)}) %collective-permute-start.8) | collective-permute-done | bytes 262176 | tf_op jit(solution)/shard_map/ppermute | solution.py:119
  39.0 0.8 %add_add_fusion = f32[128,512]{1,0:T(8,128)} fusion(f32[128,512]{1,0:T(8,128)S(1)} %collective-permute-done.10, f32[128,512]{1,0:T(8,128)S(1)} %collective-permute-done.9, f32[128,512]{1,0:T(8,128)S(1)} %collective-permute-done.8, f32[128,512]{1,0:T(8,128)S(1)} %collective-permute-done.7, f32[512,512]{1,0:T(8,128)S(1)} %add.49, s32[]{:T(128)S(6)} %select_n.44), kind=kLoop, calls=%fused_computation.10 | loop fusion | flops 262144 | bytes 1572868 | tf_op jit(solution)/shard_map/add | solution.py:119
  (22 shorter events, 1.4 us)
Async XLA Ops:
  0.0 1.2 %copy-start = (f32[512,512]{1,0:T(8,128)S(1)}, f32[512,512]{1,0:T(8,128)}, u32[]{:S(2)}) copy-start(f32[512,512]{1,0:T(8,128)} %param.2) | copy-start | bytes 3145732
  1.2 9.7 %collective-permute-start.1 = (f32[128,512]{1,0:T(8,128)S(1)}, f32[128,512]{1,0:T(8,128)S(1)}, u32[]{:S(2)}, u32[]{:S(2)}) collective-permute-start(f32[128,512]{1,0:T(8,128)S(1)} %constant_dynamic-slice_fusion.3), channel_id=1, source_target_pairs={{0,16},{4,20},{24,8},{28,12},{8,0},{12,4},{16,24},{20,28},{1,17},{... | collective-permute-start | bytes 786440 | tf_op jit(solution)/shard_map/ppermute | solution.py:65
  5.3 8.0 %collective-permute-start = (f32[128,512]{1,0:T(8,128)S(1)}, f32[128,512]{1,0:T(8,128)S(1)}, u32[]{:S(2)}, u32[]{:S(2)}) collective-permute-start(f32[128,512]{1,0:T(8,128)S(1)} %constant_dynamic-slice_fusion.3), channel_id=1, source_target_pairs={{0,4},{4,0},{8,12},{12,8},{16,20},{20,16},{24,28},{28,24},{1,5},{5... | collective-permute-start | bytes 786440 | tf_op jit(solution)/shard_map/ppermute | solution.py:68
  5.4 1.6 %copy-start.1 = (f32[512,1,1024]{2,1,0:T(1,128)S(1)}, f32[512,1,1024]{2,1,0:T(1,128)}, u32[]{:S(2)}) copy-start(f32[512,1,1024]{2,1,0:T(1,128)} %kernel_ref.1) | copy-start | bytes 6291460
  8.1 9.4 %collective-permute-start.5 = (f32[128,512]{1,0:T(8,128)S(1)}, f32[128,512]{1,0:T(8,128)S(1)}, u32[]{:S(2)}, u32[]{:S(2)}) collective-permute-start(f32[128,512]{1,0:T(8,128)S(1)} %constant_dynamic-slice_fusion.3), channel_id=1, source_target_pairs={{8,16},{12,20},{16,8},{20,12},{9,17},{13,21},{17,9},{21,13},{10,18... | collective-permute-start | bytes 786440 | tf_op jit(solution)/shard_map/ppermute | solution.py:65
  10.9 3.6 %collective-permute-start.2 = (f32[128,512]{1,0:T(8,128)S(1)}, f32[128,512]{1,0:T(8,128)S(1)}, u32[]{:S(2)}, u32[]{:S(2)}) collective-permute-start(f32[128,512]{1,0:T(8,128)S(1)} %collective-permute-done.1), channel_id=1, source_target_pairs={{0,4},{4,0},{8,12},{12,8},{16,20},{20,16},{24,28},{28,24},{1,5},{5... | collective-permute-start | bytes 786440 | tf_op jit(solution)/shard_map/ppermute | solution.py:68
  10.9 9.3 %collective-permute-start.4 = (f32[128,512]{1,0:T(8,128)S(1)}, f32[128,512]{1,0:T(8,128)S(1)}, u32[]{:S(2)}, u32[]{:S(2)}) collective-permute-start(f32[128,512]{1,0:T(8,128)S(1)} %collective-permute-done.1), channel_id=1, source_target_pairs={{0,8},{4,12},{8,0},{12,4},{16,24},{20,28},{24,16},{28,20},{1,9},{5... | collective-permute-start | bytes 786440 | tf_op jit(solution)/shard_map/ppermute | solution.py:65
  15.8 1.6 %collective-permute-start.3 = (f32[128,512]{1,0:T(8,128)S(1)}, f32[128,512]{1,0:T(8,128)S(1)}, u32[]{:S(2)}, u32[]{:S(2)}) collective-permute-start(f32[128,512]{1,0:T(8,128)S(1)} %slice.9), channel_id=1, source_target_pairs={{0,4},{4,0},{8,12},{12,8},{16,20},{20,16},{24,28},{28,24},{1,5},{5... | collective-permute-start | bytes 786440 | tf_op jit(solution)/shard_map/ppermute | solution.py:68
  20.3 1.9 %collective-permute-start.6 = (f32[128,512]{1,0:T(8,128)S(1)}, f32[128,512]{1,0:T(8,128)S(1)}, u32[]{:S(2)}, u32[]{:S(2)}) collective-permute-start(f32[128,512]{1,0:T(8,128)S(1)} %broadcast_select_fusion), channel_id=1, source_target_pairs={{0,4},{4,0},{8,12},{12,8},{16,20},{20,16},{24,28},{28,24},{1,5},{5... | collective-permute-start | bytes 786440 | tf_op jit(solution)/shard_map/ppermute | solution.py:68
  20.4 9.7 %collective-permute-start.7 = (f32[128,512]{1,0:T(8,128)S(1)}, f32[128,512]{1,0:T(8,128)S(1)}, u32[]{:S(2)}, u32[]{:S(2)}) collective-permute-start(f32[128,512]{1,0:T(8,128)S(1)} %slice_add_fusion), channel_id=1, source_target_pairs={{8,24},{12,28},{16,0},{20,4},{0,8},{4,12},{24,16},{28,20},{9,25},{... | collective-permute-start | bytes 786440 | tf_op jit(solution)/shard_map/ppermute | solution.py:65
  23.8 8.4 %collective-permute-start.10 = (f32[128,512]{1,0:T(8,128)S(1)}, f32[128,512]{1,0:T(8,128)S(1)}, u32[]{:S(2)}, u32[]{:S(2)}) collective-permute-start(f32[128,512]{1,0:T(8,128)S(1)} %get-tuple-element.30), channel_id=1, source_target_pairs={{0,2},{1,3},{2,0},{3,1},{4,6},{5,7},{6,4},{7,5},{8,10},{9,11},{10,... | collective-permute-start | bytes 786440 | tf_op jit(solution)/shard_map/ppermute | solution.py:119
  25.3 9.2 %collective-permute-start.9 = (f32[128,512]{1,0:T(8,128)S(1)}, f32[128,512]{1,0:T(8,128)S(1)}, u32[]{:S(2)}, u32[]{:S(2)}) collective-permute-start(f32[128,512]{1,0:T(8,128)S(1)} %get-tuple-element.31), channel_id=1, source_target_pairs={{0,1},{1,0},{2,3},{3,2},{4,5},{5,4},{6,7},{7,6},{8,9},{9,8},{10,11... | collective-permute-start | bytes 786440 | tf_op jit(solution)/shard_map/ppermute | solution.py:119
  26.8 12.2 %collective-permute-start.8 = (f32[128,512]{1,0:T(8,128)S(1)}, f32[128,512]{1,0:T(8,128)S(1)}, u32[]{:S(2)}, u32[]{:S(2)}) collective-permute-start(f32[128,512]{1,0:T(8,128)S(1)} %get-tuple-element.29), channel_id=1, source_target_pairs={{0,3},{1,2},{2,1},{3,0},{4,7},{5,6},{6,5},{7,4},{8,11},{9,10},{10,... | collective-permute-start | bytes 786440 | tf_op jit(solution)/shard_map/ppermute | solution.py:119

commit v3 on v2

v3 whole, which is shorter than its diff:
```python
import jax
import jax.numpy as jnp
from jax import lax
from jax.experimental import pallas as pl
from jax.experimental.pallas import tpu as pltpu
from jax.sharding import PartitionSpec as P

CORES = 2
CHUNKS = 2
LANES = 128
MIB = 1 << 20


def product(a, b, dims):
    return lax.dot_general(
        a, b, (dims, ((), ())), precision=lax.Precision.HIGH, preferred_element_type=jnp.float32
    )


def pick_body(at_ref, kernel_ref, *out_refs):
    share = out_refs[0].shape[1] // CORES
    for i, out_ref in enumerate(out_refs):
        for c in range(CORES):
            start = pl.multiple_of(at_ref[i * CORES + c] * share, share)
            out_ref[:, c * share : (c + 1) * share] = kernel_ref[:, 0, pl.ds(start, share)]


def pick_columns(kernel, blocks, share):
    rows, count = kernel.shape[0], len(blocks) // CORES
    if share % LANES:
        flat = kernel[:, 0, :]
        parts = [lax.dynamic_slice_in_dim(flat, b * share, share, 1) for b in blocks]
        return [jnp.concatenate(parts[i * CORES : (i + 1) * CORES], axis=1) for i in range(count)]
    return pl.pallas_call(
        pick_body,
        in_specs=[
            pl.BlockSpec(memory_space=pltpu.SMEM),
            pl.BlockSpec(memory_space=pltpu.VMEM),
        ],
        out_specs=[pl.BlockSpec(memory_space=pltpu.VMEM)] * count,
        out_shape=[jax.ShapeDtypeStruct((rows, CORES * share), jnp.float32)] * count,
        compiler_params=pltpu.CompilerParams(vmem_limit_bytes=16 * MIB),
        cost_estimate=pl.CostEstimate(flops=0, bytes_accessed=4 * kernel.size, transcendentals=0),
    )(jnp.stack(blocks).astype(jnp.int32), kernel)


def per_device(orbitals, kernel):
    nchips = lax.axis_size("blk") // CORES
    nshares = lax.axis_size("split")
    q = lax.axis_index("blk")
    share_id = lax.axis_index("split")
    chip, core = q // CORES, q % CORES
    share = orbitals.shape[0] // nshares
    steps = nchips // 2

    ring = list(range(0, nchips, 2)) + list(range(1, nchips, 2))[::-1]

    def shift(value, by):
        pairs = [
            (CORES * c + i, CORES * ring[(at + by) % nchips] + i)
            for at, c in enumerate(ring)
            for i in range(CORES)
        ]
        return lax.ppermute(value, "blk", pairs)

    def chip_behind(t):
        at = jnp.where(chip % 2 == 0, chip // 2, nchips - 1 - chip // 2)
        at = (at - t + nchips) % nchips
        return jnp.where(2 * at < nchips, 2 * at, 2 * (nchips - 1 - at) + 1)

    def other_core(value):
        return lax.ppermute(value, "blk", [(i, i ^ 1) for i in range(nchips * CORES)])

    def weighted(z_part, points):
        return z_part * product(orbitals, points, ((1,), (1,)))

    def rows_of(weights, points):
        return product(weights, points, ((1,), (0,)))

    own = lax.dynamic_slice_in_dim(orbitals, share_id * share, share, 0)
    pair_own = other_core(own)
    held = shift(own, 1)

    blocks = []
    for t in range(steps + 1):
        there = CORES * chip_behind(t)
        blocks += [there + core, there + 1 - core]
    z_parts = pick_columns(kernel, blocks, share)

    points = jnp.concatenate([own, pair_own], axis=0)
    total = rows_of(weighted(z_parts[0], points), points)

    backs = []
    for t in range(1, steps):
        points = jnp.concatenate([held, other_core(held)], axis=0)
        ahead = shift(held, 1)
        weights = weighted(z_parts[t], points)
        back = product(weights, orbitals, ((0,), (0,)))
        backs.append(back[:share] + other_core(back[share:]))
        total += rows_of(weights, points)
        held = ahead
    total, backs, held = lax.optimization_barrier((total, backs, held))

    pair_held = other_core(held)
    z_last = z_parts[steps]
    total += rows_of(weighted(z_last[:, :share], held), held)
    total, pair_held = lax.optimization_barrier((total, pair_held))
    total += rows_of(weighted(z_last[:, share:], pair_held), pair_held)
    total, backs = lax.optimization_barrier((total, backs))
    returned = sum(shift(back, -t) for t, back in enumerate(backs, 1))

    bits = nshares.bit_length() - 1

    def bit_at(step, on_core):
        return (step + on_core * (bits // 2)) % bits

    def share_mask(place, on_core):
        return sum(((place >> (bits - 1 - t)) & 1) << bit_at(t, on_core) for t in range(bits))

    masks = [jnp.where(core == 0, share_mask(p, 0), share_mask(p, 1)) for p in range(nshares)]
    cut = orbitals.shape[1] // CHUNKS

    def blocks_of(places, chunk):
        found = [
            lax.dynamic_slice(total, ((share_id ^ masks[p]) * share, chunk * cut), (share, cut))
            for p in places
        ]
        return jnp.concatenate(found, axis=0)

    def halve(keep, send, step):
        pairs = [
            (b * nshares + s, b * nshares + (s ^ (1 << bit_at(step, b % CORES))))
            for b in range(nchips * CORES)
            for s in range(nshares)
        ]
        return keep + lax.ppermute(send, ("blk", "split"), pairs)

    places, middle = list(range(nshares)), nshares // 2
    parts = [halve(blocks_of(places[:middle], k), blocks_of(places[middle:], k), 0) for k in range(CHUNKS)]
    for step in range(1, bits):
        size = parts[0].shape[0] // 2
        parts = [halve(part[:size], part[size:], step) for part in parts]
    return jnp.concatenate(parts, axis=1) + returned


def solution(mesh):
    placed = (P("blk", None), P("blk", "split", None))
    return jax.shard_map(
        per_device, mesh=mesh, in_specs=placed, out_specs=P(("blk", "split"), None), check_vma=False
    )
```

time: 40 us -> 39.4 us (0.985)
  waiting for transfers between devices: 17.3 us -> 12.7 us
  starting transfers between devices: 12.8 us -> 15.5 us
  matrix products: 4.24 us -> 5.32 us
    ppermute x7, waiting for transfers between devices: 16.6 us -> 11.8 us  [the longest x4 6.99 us: halve(): return keep + lax.ppermute(send, ('blk', 'split'), pairs)]
    ppermute x7, starting transfers between devices: 12.5 us -> 15.2 us  [the longest x3 9.84 us: shift(): return lax.ppermute(value, 'blk', pairs)]
    dot_general x7 -> x9, matrix products: 4.24 us -> 5.32 us  [product(): lax.dot_general(a, b, (dims, ((), ())), precision=lax.Precision.HIGH, pre...]
    add x3 -> x8, other arithmetic: 1.06 us -> 1.29 us  [the longest x1 0.73 us: per_device(): return jnp.concatenate(parts, axis=1) + returned]
    unnamed x6 -> x5, local copies, waits for them, and re-layouts: 2.85 us -> 2.84 us
  transfers between devices with their start and end apart: 11 -> 11, of which waited for: 7 -> 8; matrix products, arithmetic and copies ran while one was open for 12% -> 12% of each run, Pallas kernels for 3% -> 3%
where the time goes in v3:
time: 39.4 us; the launch traced here: 39.2 us
  starting transfers between devices  15.5 us (39%)
  waiting for transfers between devices  12.7 us (32%)
  matrix products  5.32 us (14%)
  local copies, waits for them, and re-layouts  3.11 us (8%)
  other arithmetic  1.33 us (3%)
  Pallas kernels  1.06 us (3%)
    ppermute x3, starting transfers between devices, shift(): return lax.ppermute(value, 'blk', pairs)  9.84 us
    ppermute x4, waiting for transfers between devices, halve(): return keep + lax.ppermute(send, ('blk', 'split'), pairs)  6.99 us
    ppermute x4, starting transfers between devices, halve(): return keep + lax.ppermute(send, ('blk', 'split'), pairs)  5.33 us
    dot_general x9, matrix products, product(): lax.dot_general(a, b, (dims, ((), ())), precision=lax.Precision.HIGH, pre...  5.32 us
    ppermute x3, waiting for transfers between devices, shift(): return lax.ppermute(value, 'blk', pairs)  4.83 us
    unnamed x5, local copies, waits for them, and re-layouts  2.84 us
    pallas_call x1, Pallas kernels, pick_columns(): pl.pallas_call(pick_body, in_specs=[pl.BlockSpec(memory_space=pltpu.SMEM)...  1.06 us
    ppermute x4, waiting for transfers between devices, other_core(): lax.ppermute(value, 'blk', [(i, i ^ 1) for i in range(nchips * CORES)])  0.88 us
  transfers between devices with their start and end apart: 11, of which 8 were waited for; matrix products, arithmetic and copies ran while one was open for 12% of the time, Pallas kernels for 3%

profile of v3, /device:TPU:0, one launch (start us, length us, event | category | flops | bytes accessed | tf_op | source)
XLA Modules:
  0.0 39.2 jit_solution(4777586466247587974)
XLA Ops:
  0.0 1.2 %copy-done = f32[512,512]{1,0:T(8,128)S(1)} copy-done((f32[512,512]{1,0:T(8,128)S(1)}, f32[512,512]{1,0:T(8,128)}, u32[]{:S(2)}) %copy-start) | copy-done | bytes 1048600
  1.2 4.1 %collective-permute-start.1 = (f32[128,512]{1,0:T(8,128)S(1)}, f32[128,512]{1,0:T(8,128)S(1)}, u32[]{:S(2)}, u32[]{:S(2)}) collective-permute-start(f32[128,512]{1,0:T(8,128)S(1)} %constant_dynamic-slice_fusion.8), channel_id=1, source_target_pairs={{0,16},{4,20},{16,24},{20,28},{24,8},{28,12},{8,0},{12,4},{1,17},{... | collective-permute-start | bytes 786440 | tf_op jit(solution)/shard_map/ppermute | solution.py:64
  5.4 1.6 %copy-done.1 = f32[512,1,1024]{2,1,0:T(1,128)S(1)} copy-done((f32[512,1,1024]{2,1,0:T(1,128)S(1)}, f32[512,1,1024]{2,1,0:T(1,128)}, u32[]{:S(2)}) %copy-start.1) | copy-done | bytes 2097176
  7.0 1.1 %shard_map.28 = (f32[512,256]{1,0:T(8,128)S(1)}, f32[512,256]{1,0:T(8,128)S(1)}, f32[512,256]{1,0:T(8,128)S(1)}) custom-call(s32[6]{0:T(128)S(1)} %stack.27.at_ref, f32[512,1,1024]{2,1,0:T(1,128)S(1)} %copy-done.1), custom_call_target="tpu_custom_call" | custom-call | bytes 2097152 | tf_op jit(solution)/shard_map/pallas_call | solution.py:34
  8.1 2.8 %collective-permute-done.1 = f32[128,512]{1,0:T(8,128)S(1)} collective-permute-done((f32[128,512]{1,0:T(8,128)S(1)}, f32[128,512]{1,0:T(8,128)S(1)}, u32[]{:S(2)}, u32[]{:S(2)}) %collective-permute-start.1) | collective-permute-done | bytes 262176 | tf_op jit(solution)/shard_map/ppermute | solution.py:64
  10.9 3.4 %collective-permute-start.4 = (f32[128,512]{1,0:T(8,128)S(1)}, f32[128,512]{1,0:T(8,128)S(1)}, u32[]{:S(2)}, u32[]{:S(2)}) collective-permute-start(f32[128,512]{1,0:T(8,128)S(1)} %collective-permute-done.1), channel_id=1, source_target_pairs={{0,16},{4,20},{16,24},{20,28},{24,8},{28,12},{8,0},{12,4},{1,17},{... | collective-permute-start | bytes 786440 | tf_op jit(solution)/shard_map/ppermute | solution.py:64
  14.3 0.6 %fusion.1 = f32[512,256]{1,0:T(8,128)S(1)} fusion(f32[512,256]{1,0:T(8,128)S(1)} %get-tuple-element.15, f32[512,512]{1,0:T(8,128)S(1)} %copy-done, f32[128,512]{1,0:T(8,128)S(1)} %collective-permute-done, f32[128,512]{1,0:T(8,128)S(1)} %constant_dynamic-slice_fusion.8), kind=kOutput, calls=%fused_computation.4 | convolution fusion | flops 402915328 | bytes 2621440 | tf_op jit(solution)/shard_map/dot_general | solution.py:15
  14.9 0.6 %fusion.4 = f32[512,512]{1,0:T(8,128)S(1)} fusion(f32[512,256]{1,0:T(8,128)S(1)} %fusion.1, f32[128,512]{1,0:T(8,128)S(1)} %collective-permute-done, f32[128,512]{1,0:T(8,128)S(1)} %constant_dynamic-slice_fusion.8), kind=kOutput, calls=%fused_computation.10 | convolution fusion | flops 402784256 | bytes 2097152 | tf_op jit(solution)/shard_map/dot_general | solution.py:15
  15.6 0.6 %fusion = f32[512,256]{1,0:T(8,128)S(1)} fusion(f32[512,256]{1,0:T(8,128)S(1)} %get-tuple-element.16, f32[256,512]{1,0:T(8,128)S(1)} %constant_dynamic-update-slice_fusion, f32[512,512]{1,0:T(8,128)S(1)} %copy-done), kind=kOutput, calls=%fused_computation.2 | convolution fusion | flops 402784256 | bytes 2621440 | tf_op jit(solution)/shard_map/dot_general | solution.py:15
  16.2 0.6 %fusion.7 = f32[256,512]{1,0:T(8,128)S(1)} fusion(f32[512,256]{1,0:T(8,128)S(1)} %fusion, f32[512,512]{1,0:T(8,128)S(1)} %copy-done), kind=kOutput, calls=%fused_computation.32 | convolution fusion | flops 402653184 | bytes 2097152 | tf_op jit(solution)/shard_map/dot_general | solution.py:15
  17.1 0.6 %convolution_add_fusion = f32[512,512]{1,0:T(8,128)S(1)} fusion(f32[512,512]{1,0:T(8,128)S(1)} %fusion.4, f32[512,256]{1,0:T(8,128)S(1)} %fusion, f32[256,512]{1,0:T(8,128)S(1)} %constant_dynamic-update-slice_fusion), kind=kOutput, calls=%fused_computation | convolution fusion | flops 402915328 | bytes 3145728 | tf_op jit(solution)/shard_map/dot_general | solution.py:15
  17.7 0.7 %collective-permute-done.3 = f32[128,512]{1,0:T(8,128)S(1)} collective-permute-done((f32[128,512]{1,0:T(8,128)S(1)}, f32[128,512]{1,0:T(8,128)S(1)}, u32[]{:S(2)}, u32[]{:S(2)}) %collective-permute-start.3) | collective-permute-done | bytes 262176 | tf_op jit(solution)/shard_map/ppermute | solution.py:72
  18.5 2.0 %collective-permute-done.4 = f32[128,512]{1,0:T(8,128)S(1)} collective-permute-done((f32[128,512]{1,0:T(8,128)S(1)}, f32[128,512]{1,0:T(8,128)S(1)}, u32[]{:S(2)}, u32[]{:S(2)}) %collective-permute-start.4) | collective-permute-done | bytes 262176 | tf_op jit(solution)/shard_map/ppermute | solution.py:64
  20.5 0.6 %fusion.2 = f32[512,128]{1,0:T(8,128)S(1)} fusion(f32[128,512]{1,0:T(8,128)S(1)} %collective-permute-done.4, f32[512,512]{1,0:T(8,128)S(1)} %copy-done, f32[512,256]{1,0:T(8,128)S(1)} %get-tuple-element.18), kind=kOutput, calls=%fused_computation.7 | convolution fusion | flops 201392128 | bytes 1835008 | tf_op jit(solution)/shard_map/dot_general | solution.py:15
  22.1 0.6 %fusion.3 = f32[512,128]{1,0:T(8,128)S(1)} fusion(f32[128,512]{1,0:T(8,128)S(1)} %collective-permute-done.5, f32[512,512]{1,0:T(8,128)S(1)} %copy-done, f32[512,256]{1,0:T(8,128)S(1)} %get-tuple-element.18), kind=kOutput, calls=%fused_computation.8 | convolution fusion | flops 201392128 | bytes 1835008 | tf_op jit(solution)/shard_map/dot_general | solution.py:15
  23.6 1.6 %collective-permute-start.8 = (f32[256,256]{1,0:T(8,128)S(1)}, f32[256,256]{1,0:T(8,128)S(1)}, u32[]{:S(2)}, u32[]{:S(2)}) collective-permute-start(f32[256,256]{1,0:T(8,128)S(1)} %pad_maximum_fusion.4), channel_id=1, source_target_pairs={{0,1},{1,0},{2,3},{3,2},{4,6},{5,7},{6,4},{7,5},{8,9},{9,8},{10,11... | collective-permute-start | bytes 786440 | tf_op jit(solution)/shard_map/ppermute | solution.py:136
  25.2 0.6 %collective-permute-start.6 = (f32[256,256]{1,0:T(8,128)S(1)}, f32[256,256]{1,0:T(8,128)S(1)}, u32[]{:S(2)}, u32[]{:S(2)}) collective-permute-start(f32[256,256]{1,0:T(8,128)S(1)} %pad_maximum_fusion.3), channel_id=1, source_target_pairs={{0,1},{1,0},{2,3},{3,2},{4,6},{5,7},{6,4},{7,5},{8,9},{9,8},{10,11... | collective-permute-start | bytes 786440 | tf_op jit(solution)/shard_map/ppermute | solution.py:136
  25.8 2.4 %collective-permute-start.10 = (f32[128,512]{1,0:T(8,128)S(1)}, f32[128,512]{1,0:T(8,128)S(1)}, u32[]{:S(2)}, u32[]{:S(2)}) collective-permute-start(f32[128,512]{1,0:T(8,128)S(1)} %slice_add_fusion), channel_id=1, source_target_pairs={{0,8},{4,12},{16,0},{20,4},{24,16},{28,20},{8,24},{12,28},{1,9},{5... | collective-permute-start | bytes 786440 | tf_op jit(solution)/shard_map/ppermute | solution.py:64
  28.1 1.9 %collective-permute-done.8 = f32[256,256]{1,0:T(8,128)S(1)} collective-permute-done((f32[256,256]{1,0:T(8,128)S(1)}, f32[256,256]{1,0:T(8,128)S(1)}, u32[]{:S(2)}, u32[]{:S(2)}) %collective-permute-start.8) | collective-permute-done | bytes 262176 | tf_op jit(solution)/shard_map/ppermute | solution.py:136
  30.1 1.6 %collective-permute-start.9 = (f32[128,256]{1,0:T(8,128)S(1)}, f32[128,256]{1,0:T(8,128)S(1)}, u32[]{:S(2)}, u32[]{:S(2)}) collective-permute-start(f32[128,256]{1,0:T(8,128)S(1)} %slice.37), channel_id=1, source_target_pairs={{0,2},{1,3},{2,0},{3,1},{4,5},{5,4},{6,7},{7,6},{8,10},{9,11},{10,... | collective-permute-start | bytes 393224 | tf_op jit(solution)/shard_map/ppermute | solution.py:136
  31.7 1.7 %collective-permute-done.6 = f32[256,256]{1,0:T(8,128)S(1)} collective-permute-done((f32[256,256]{1,0:T(8,128)S(1)}, f32[256,256]{1,0:T(8,128)S(1)}, u32[]{:S(2)}, u32[]{:S(2)}) %collective-permute-start.6) | collective-permute-done | bytes 262176 | tf_op jit(solution)/shard_map/ppermute | solution.py:136
  33.4 1.6 %collective-permute-start.7 = (f32[128,256]{1,0:T(8,128)S(1)}, f32[128,256]{1,0:T(8,128)S(1)}, u32[]{:S(2)}, u32[]{:S(2)}) collective-permute-start(f32[128,256]{1,0:T(8,128)S(1)} %slice.35), channel_id=1, source_target_pairs={{0,2},{1,3},{2,0},{3,1},{4,5},{5,4},{6,7},{7,6},{8,10},{9,11},{10,... | collective-permute-start | bytes 393224 | tf_op jit(solution)/shard_map/ppermute | solution.py:136
  35.1 3.3 %collective-permute-done.7 = f32[128,256]{1,0:T(8,128)S(1)} collective-permute-done((f32[128,256]{1,0:T(8,128)S(1)}, f32[128,256]{1,0:T(8,128)S(1)}, u32[]{:S(2)}, u32[]{:S(2)}) %collective-permute-start.7) | collective-permute-done | bytes 131104 | tf_op jit(solution)/shard_map/ppermute | solution.py:136
  38.5 0.7 %maximum_add_fusion.2 = f32[128,512]{1,0:T(8,128)} fusion(f32[128,512]{1,0:T(8,128)S(1)} %collective-permute-done.10, f32[128,256]{1,0:T(8,128)S(1)} %slice_add_fusion.1, f32[128,256]{1,0:T(8,128)S(1)} %slice_add_fusion.2), kind=kLoop, calls=%fused_computation.16 | loop fusion | flops 131072 | bytes 786432 | tf_op jit(solution)/shard_map/add | solution.py:143
  (30 shorter events, 2.6 us)
Async XLA Ops:
  0.0 1.2 %copy-start = (f32[512,512]{1,0:T(8,128)S(1)}, f32[512,512]{1,0:T(8,128)}, u32[]{:S(2)}) copy-start(f32[512,512]{1,0:T(8,128)} %param.2) | copy-start | bytes 3145732
  1.2 9.7 %collective-permute-start.1 = (f32[128,512]{1,0:T(8,128)S(1)}, f32[128,512]{1,0:T(8,128)S(1)}, u32[]{:S(2)}, u32[]{:S(2)}) collective-permute-start(f32[128,512]{1,0:T(8,128)S(1)} %constant_dynamic-slice_fusion.8), channel_id=1, source_target_pairs={{0,16},{4,20},{16,24},{20,28},{24,8},{28,12},{8,0},{12,4},{1,17},{... | collective-permute-start | bytes 786440 | tf_op jit(solution)/shard_map/ppermute | solution.py:64
  5.3 9.0 %collective-permute-start = (f32[128,512]{1,0:T(8,128)S(1)}, f32[128,512]{1,0:T(8,128)S(1)}, u32[]{:S(2)}, u32[]{:S(2)}) collective-permute-start(f32[128,512]{1,0:T(8,128)S(1)} %constant_dynamic-slice_fusion.8), channel_id=1, source_target_pairs={{0,4},{4,0},{8,12},{12,8},{16,20},{20,16},{24,28},{28,24},{1,5},{5... | collective-permute-start | bytes 786440 | tf_op jit(solution)/shard_map/ppermute | solution.py:72
  5.4 1.6 %copy-start.1 = (f32[512,1,1024]{2,1,0:T(1,128)S(1)}, f32[512,1,1024]{2,1,0:T(1,128)}, u32[]{:S(2)}) copy-start(f32[512,1,1024]{2,1,0:T(1,128)} %kernel_ref.1) | copy-start | bytes 6291460
  10.9 4.6 %collective-permute-start.2 = (f32[128,512]{1,0:T(8,128)S(1)}, f32[128,512]{1,0:T(8,128)S(1)}, u32[]{:S(2)}, u32[]{:S(2)}) collective-permute-start(f32[128,512]{1,0:T(8,128)S(1)} %collective-permute-done.1), channel_id=1, source_target_pairs={{0,4},{4,0},{8,12},{12,8},{16,20},{20,16},{24,28},{28,24},{1,5},{5... | collective-permute-start | bytes 786440 | tf_op jit(solution)/shard_map/ppermute | solution.py:72
  10.9 9.6 %collective-permute-start.4 = (f32[128,512]{1,0:T(8,128)S(1)}, f32[128,512]{1,0:T(8,128)S(1)}, u32[]{:S(2)}, u32[]{:S(2)}) collective-permute-start(f32[128,512]{1,0:T(8,128)S(1)} %collective-permute-done.1), channel_id=1, source_target_pairs={{0,16},{4,20},{16,24},{20,28},{24,8},{28,12},{8,0},{12,4},{1,17},{... | collective-permute-start | bytes 786440 | tf_op jit(solution)/shard_map/ppermute | solution.py:64
  16.9 1.6 %collective-permute-start.3 = (f32[128,512]{1,0:T(8,128)S(1)}, f32[128,512]{1,0:T(8,128)S(1)}, u32[]{:S(2)}, u32[]{:S(2)}) collective-permute-start(f32[128,512]{1,0:T(8,128)S(1)} %slice.33), channel_id=1, source_target_pairs={{0,4},{4,0},{8,12},{12,8},{16,20},{20,16},{24,28},{28,24},{1,5},{5... | collective-permute-start | bytes 786440 | tf_op jit(solution)/shard_map/ppermute | solution.py:72
  20.5 1.5 %collective-permute-start.5 = (f32[128,512]{1,0:T(8,128)S(1)}, f32[128,512]{1,0:T(8,128)S(1)}, u32[]{:S(2)}, u32[]{:S(2)}) collective-permute-start(f32[128,512]{1,0:T(8,128)S(1)} %collective-permute-done.4), channel_id=1, source_target_pairs={{0,4},{4,0},{8,12},{12,8},{16,20},{20,16},{24,28},{28,24},{1,5},{5... | collective-permute-start | bytes 786440 | tf_op jit(solution)/shard_map/ppermute | solution.py:72
  23.6 6.4 %collective-permute-start.8 = (f32[256,256]{1,0:T(8,128)S(1)}, f32[256,256]{1,0:T(8,128)S(1)}, u32[]{:S(2)}, u32[]{:S(2)}) collective-permute-start(f32[256,256]{1,0:T(8,128)S(1)} %pad_maximum_fusion.4), channel_id=1, source_target_pairs={{0,1},{1,0},{2,3},{3,2},{4,6},{5,7},{6,4},{7,5},{8,9},{9,8},{10,11... | collective-permute-start | bytes 786440 | tf_op jit(solution)/shard_map/ppermute | solution.py:136
  25.2 8.2 %collective-permute-start.6 = (f32[256,256]{1,0:T(8,128)S(1)}, f32[256,256]{1,0:T(8,128)S(1)}, u32[]{:S(2)}, u32[]{:S(2)}) collective-permute-start(f32[256,256]{1,0:T(8,128)S(1)} %pad_maximum_fusion.3), channel_id=1, source_target_pairs={{0,1},{1,0},{2,3},{3,2},{4,6},{5,7},{6,4},{7,5},{8,9},{9,8},{10,11... | collective-permute-start | bytes 786440 | tf_op jit(solution)/shard_map/ppermute | solution.py:136
  25.8 12.7 %collective-permute-start.10 = (f32[128,512]{1,0:T(8,128)S(1)}, f32[128,512]{1,0:T(8,128)S(1)}, u32[]{:S(2)}, u32[]{:S(2)}) collective-permute-start(f32[128,512]{1,0:T(8,128)S(1)} %slice_add_fusion), channel_id=1, source_target_pairs={{0,8},{4,12},{16,0},{20,4},{24,16},{28,20},{8,24},{12,28},{1,9},{5... | collective-permute-start | bytes 786440 | tf_op jit(solution)/shard_map/ppermute | solution.py:64
  30.1 5.0 %collective-permute-start.9 = (f32[128,256]{1,0:T(8,128)S(1)}, f32[128,256]{1,0:T(8,128)S(1)}, u32[]{:S(2)}, u32[]{:S(2)}) collective-permute-start(f32[128,256]{1,0:T(8,128)S(1)} %slice.37), channel_id=1, source_target_pairs={{0,2},{1,3},{2,0},{3,1},{4,5},{5,4},{6,7},{7,6},{8,10},{9,11},{10,... | collective-permute-start | bytes 393224 | tf_op jit(solution)/shard_map/ppermute | solution.py:136
  33.4 5.0 %collective-permute-start.7 = (f32[128,256]{1,0:T(8,128)S(1)}, f32[128,256]{1,0:T(8,128)S(1)}, u32[]{:S(2)}, u32[]{:S(2)}) collective-permute-start(f32[128,256]{1,0:T(8,128)S(1)} %slice.35), channel_id=1, source_target_pairs={{0,2},{1,3},{2,0},{3,1},{4,5},{5,4},{6,7},{7,6},{8,10},{9,11},{10,... | collective-permute-start | bytes 393224 | tf_op jit(solution)/shard_map/ppermute | solution.py:136

commit v4 on v2

--- a/solution.py
+++ b/solution.py
@@ -6,6 +6,7 @@
 from jax.sharding import PartitionSpec as P
 
 CORES = 2
+CHUNKS = 2
 LANES = 128
 MIB = 1 << 20
 
@@ -102,24 +103,49 @@
     total += rows_of(weights, points)
 
     total, back, passed, swapped = lax.optimization_barrier((total, back, passed, swapped))
-    late = jnp.where(inner, swapped, passed)
-    late, back = lax.optimization_barrier((late, back))
-    points = jnp.concatenate([late, other_core(late)], axis=0)
+    held = jnp.where(inner, swapped, passed)
+    pair_held = other_core(held)
+    z_last = z_late
+    total += rows_of(weighted(z_last[:, :share], held), held)
+    total, pair_held = lax.optimization_barrier((total, pair_held))
+    total += rows_of(weighted(z_last[:, share:], pair_held), pair_held)
+    total, back = lax.optimization_barrier((total, back))
     returned = along(
         back, [(c, c ^ half) for c in inner_chips] + [(c, c ^ near) for c in outer_chips]
     )
-    total += rows_of(weighted(z_late, points), points)
 
-    def for_share(at):
-        return lax.dynamic_slice_in_dim(total, at * share, share, 0)
+    bits = nshares.bit_length() - 1
 
-    out = for_share(share_id) + returned
-    masks = sorted(range(1, nshares), key=lambda mask: -mask.bit_count())
-    for mask in masks:
-        out += lax.ppermute(
-            for_share(share_id ^ mask), "split", [(i, i ^ mask) for i in range(nshares)]
-        )
-    return out
+    def bit_at(step, on_core):
+        return (step + on_core * (bits // 2)) % bits
+
+    def share_mask(place, on_core):
+        return sum(((place >> (bits - 1 - t)) & 1) << bit_at(t, on_core) for t in range(bits))
+
+    masks = [jnp.where(q % CORES == 0, share_mask(p, 0), share_mask(p, 1)) for p in range(nshares)]
+    cut = orbitals.shape[1] // CHUNKS
+
+    def blocks_of(places, chunk):
+        found = [
+            lax.dynamic_slice(total, ((share_id ^ masks[p]) * share, chunk * cut), (share, cut))
+            for p in places
+        ]
+        return jnp.concatenate(found, axis=0)
+
+    def halve(keep, send, step):
+        pairs = [
+            (b * nshares + s, b * nshares + (s ^ (1 << bit_at(step, b % CORES))))
+            for b in range(nchips * CORES)
+            for s in range(nshares)
+        ]
+        return keep + lax.ppermute(send, ("blk", "split"), pairs)
+
+    places, middle = list(range(nshares)), nshares // 2
+    parts = [halve(blocks_of(places[:middle], k), blocks_of(places[middle:], k), 0) for k in range(CHUNKS)]
+    for step in range(1, bits):
+        size = parts[0].shape[0] // 2
+        parts = [halve(part[:size], part[size:], step) for part in parts]
+    return jnp.concatenate(parts, axis=1) + returned
 
 
 def solution(mesh):

time: 40 us -> 37.9 us (0.948)
  waiting for transfers between devices: 17.3 us -> 10.4 us
  starting transfers between devices: 12.8 us -> 16.2 us
  matrix products: 4.24 us -> 5.32 us
    ppermute x4, waiting for transfers between devices: 7.66 us -> 2.65 us  [along(): return lax.ppermute(value, 'blk', full)]
    ppermute x3 -> x4, waiting for transfers between devices: 8.9 us -> 6.68 us  [halve(): return keep + lax.ppermute(send, ('blk', 'split'), pairs)]
    ppermute x3 -> x4, starting transfers between devices: 3.55 us -> 5.33 us  [halve(): return keep + lax.ppermute(send, ('blk', 'split'), pairs)]
    ppermute x4, starting transfers between devices: 8.93 us -> 10.5 us  [along(): return lax.ppermute(value, 'blk', full)]
    dot_general x7 -> x9, matrix products: 4.24 us -> 5.32 us  [product(): lax.dot_general(a, b, (dims, ((), ())), precision=lax.Precision.HIGH, pre...]
    add x2 -> x7, other arithmetic: 1.02 us -> 1.26 us  [the longest x1 0.73 us: per_device(): return jnp.concatenate(parts, axis=1) + returned]
    unnamed x6 -> x5, local copies, waits for them, and re-layouts: 2.85 us -> 2.84 us
  transfers between devices with their start and end apart: 11 -> 12, of which waited for: 7 -> 9; matrix products, arithmetic and copies ran while one was open for 12% -> 12% of each run, Pallas kernels for 3% -> 3%
where the time goes in v4:
time: 37.9 us; the launch traced here: 37.7 us
  starting transfers between devices  16.2 us (43%)
  waiting for transfers between devices  10.4 us (27%)
  matrix products  5.32 us (14%)
  local copies, waits for them, and re-layouts  3.11 us (8%)
  other arithmetic  1.37 us (4%)
  Pallas kernels  1.06 us (3%)
    ppermute x4, starting transfers between devices, along(): return lax.ppermute(value, 'blk', full)  10.5 us
    ppermute x4, waiting for transfers between devices, halve(): return keep + lax.ppermute(send, ('blk', 'split'), pairs)  6.68 us
    ppermute x4, starting transfers between devices, halve(): return keep + lax.ppermute(send, ('blk', 'split'), pairs)  5.33 us
    dot_general x9, matrix products, product(): lax.dot_general(a, b, (dims, ((), ())), precision=lax.Precision.HIGH, pre...  5.32 us
    unnamed x5, local copies, waits for them, and re-layouts  2.84 us
    ppermute x4, waiting for transfers between devices, along(): return lax.ppermute(value, 'blk', full)  2.65 us
    ppermute x4, waiting for transfers between devices, other_core(): lax.ppermute(value, 'blk', [(i, i ^ 1) for i in range(nchips * CORES)])  1.11 us
    pallas_call x1, Pallas kernels, pick_columns(): pl.pallas_call(pick_body, in_specs=[pl.BlockSpec(memory_space=pltpu.SMEM)...  1.06 us
  transfers between devices with their start and end apart: 12, of which 9 were waited for; matrix products, arithmetic and copies ran while one was open for 12% of the time, Pallas kernels for 3%

profile of v4, /device:TPU:0, one launch (start us, length us, event | category | flops | bytes accessed | tf_op | source)
XLA Modules:
  0.0 37.7 jit_solution(2852528775210473605)
XLA Ops:
  0.0 1.2 %copy-done = f32[512,512]{1,0:T(8,128)S(1)} copy-done((f32[512,512]{1,0:T(8,128)S(1)}, f32[512,512]{1,0:T(8,128)}, u32[]{:S(2)}) %copy-start) | copy-done | bytes 1048600
  1.2 4.1 %collective-permute-start.1 = (f32[128,512]{1,0:T(8,128)S(1)}, f32[128,512]{1,0:T(8,128)S(1)}, u32[]{:S(2)}, u32[]{:S(2)}) collective-permute-start(f32[128,512]{1,0:T(8,128)S(1)} %constant_dynamic-slice_fusion.8), channel_id=1, source_target_pairs={{0,16},{4,20},{24,8},{28,12},{8,0},{12,4},{16,24},{20,28},{1,17},{... | collective-permute-start | bytes 786440 | tf_op jit(solution)/shard_map/ppermute | solution.py:66
  5.4 1.6 %copy-done.1 = f32[512,1,1024]{2,1,0:T(1,128)S(1)} copy-done((f32[512,1,1024]{2,1,0:T(1,128)S(1)}, f32[512,1,1024]{2,1,0:T(1,128)}, u32[]{:S(2)}) %copy-start.1) | copy-done | bytes 2097176
  7.0 1.1 %shard_map.28 = (f32[512,256]{1,0:T(8,128)S(1)}, f32[512,256]{1,0:T(8,128)S(1)}, f32[512,256]{1,0:T(8,128)S(1)}) custom-call(s32[6]{0:T(128)S(1)} %stack.27.at_ref, f32[512,1,1024]{2,1,0:T(1,128)S(1)} %copy-done.1), custom_call_target="tpu_custom_call" | custom-call | bytes 2097152 | tf_op jit(solution)/shard_map/pallas_call | solution.py:34
  8.1 1.4 %collective-permute-start.5 = (f32[128,512]{1,0:T(8,128)S(1)}, f32[128,512]{1,0:T(8,128)}, u32[]{:S(2)}, u32[]{:S(2)}) collective-permute-start(f32[128,512]{1,0:T(8,128)S(1)} %constant_dynamic-slice_fusion.8), channel_id=1, source_target_pairs={{8,16},{12,20},{16,8},{20,12},{9,17},{13,21},{17,9},{21,13},{10,18... | collective-permute-start | bytes 786440 | tf_op jit(solution)/shard_map/ppermute | solution.py:66
  9.5 1.5 %collective-permute-done.1 = f32[128,512]{1,0:T(8,128)S(1)} collective-permute-done((f32[128,512]{1,0:T(8,128)S(1)}, f32[128,512]{1,0:T(8,128)S(1)}, u32[]{:S(2)}, u32[]{:S(2)}) %collective-permute-start.1) | collective-permute-done | bytes 262176 | tf_op jit(solution)/shard_map/ppermute | solution.py:66
  10.9 2.4 %collective-permute-start.4 = (f32[128,512]{1,0:T(8,128)S(1)}, f32[128,512]{1,0:T(8,128)S(1)}, u32[]{:S(2)}, u32[]{:S(2)}) collective-permute-start(f32[128,512]{1,0:T(8,128)S(1)} %collective-permute-done.1), channel_id=1, source_target_pairs={{0,8},{4,12},{8,0},{12,4},{16,24},{20,28},{24,16},{28,20},{1,9},{5... | collective-permute-start | bytes 786440 | tf_op jit(solution)/shard_map/ppermute | solution.py:66
  13.3 0.6 %fusion.1 = f32[512,256]{1,0:T(8,128)S(1)} fusion(f32[512,256]{1,0:T(8,128)S(1)} %get-tuple-element.19, f32[512,512]{1,0:T(8,128)S(1)} %copy-done, f32[128,512]{1,0:T(8,128)S(1)} %collective-permute-done, f32[128,512]{1,0:T(8,128)S(1)} %constant_dynamic-slice_fusion.8), kind=kOutput, calls=%fused_computation.4 | convolution fusion | flops 402915328 | bytes 2621440 | tf_op jit(solution)/shard_map/dot_general | solution.py:15
  13.9 0.6 %fusion.4 = f32[512,512]{1,0:T(8,128)S(1)} fusion(f32[512,256]{1,0:T(8,128)S(1)} %fusion.1, f32[128,512]{1,0:T(8,128)S(1)} %collective-permute-done, f32[128,512]{1,0:T(8,128)S(1)} %constant_dynamic-slice_fusion.8), kind=kOutput, calls=%fused_computation.10 | convolution fusion | flops 402784256 | bytes 2097152 | tf_op jit(solution)/shard_map/dot_general | solution.py:15
  14.8 0.6 %fusion = f32[512,256]{1,0:T(8,128)S(1)} fusion(f32[512,256]{1,0:T(8,128)S(1)} %get-tuple-element.22, f32[256,512]{1,0:T(8,128)S(1)} %constant_dynamic-update-slice_fusion, f32[512,512]{1,0:T(8,128)S(1)} %copy-done), kind=kOutput, calls=%fused_computation.2 | convolution fusion | flops 402784256 | bytes 2621440 | tf_op jit(solution)/shard_map/dot_general | solution.py:15
  15.5 0.6 %fusion.7 = f32[256,512]{1,0:T(8,128)S(1)} fusion(f32[512,256]{1,0:T(8,128)S(1)} %fusion, f32[512,512]{1,0:T(8,128)S(1)} %copy-done), kind=kOutput, calls=%fused_computation.33 | convolution fusion | flops 402653184 | bytes 2097152 | tf_op jit(solution)/shard_map/dot_general | solution.py:15
  16.4 0.6 %convolution_add_fusion = f32[512,512]{1,0:T(8,128)S(1)} fusion(f32[512,512]{1,0:T(8,128)S(1)} %fusion.4, f32[512,256]{1,0:T(8,128)S(1)} %fusion, f32[256,512]{1,0:T(8,128)S(1)} %constant_dynamic-update-slice_fusion), kind=kOutput, calls=%fused_computation | convolution fusion | flops 402915328 | bytes 3145728 | tf_op jit(solution)/shard_map/dot_general | solution.py:15
  17.0 0.7 %collective-permute-done.3 = f32[128,512]{1,0:T(8,128)S(1)} collective-permute-done((f32[128,512]{1,0:T(8,128)S(1)}, f32[128,512]{1,0:T(8,128)S(1)}, u32[]{:S(2)}, u32[]{:S(2)}) %collective-permute-start.3) | collective-permute-done | bytes 262176 | tf_op jit(solution)/shard_map/ppermute | solution.py:69
  17.8 1.2 %collective-permute-done.4 = f32[128,512]{1,0:T(8,128)S(1)} collective-permute-done((f32[128,512]{1,0:T(8,128)S(1)}, f32[128,512]{1,0:T(8,128)S(1)}, u32[]{:S(2)}, u32[]{:S(2)}) %collective-permute-start.4) | collective-permute-done | bytes 262176 | tf_op jit(solution)/shard_map/ppermute | solution.py:66
  19.1 0.6 %fusion.2 = f32[512,128]{1,0:T(8,128)S(1)} fusion(f32[128,512]{1,0:T(8,128)S(1)} %broadcast_select_fusion, f32[512,512]{1,0:T(8,128)S(1)} %copy-done, f32[512,256]{1,0:T(8,128)S(1)} %get-tuple-element.25), kind=kOutput, calls=%fused_computation.7 | convolution fusion | flops 201392128 | bytes 1835008 | tf_op jit(solution)/shard_map/dot_general | solution.py:15
  22.1 1.6 %collective-permute-start.7 = (f32[256,256]{1,0:T(8,128)S(1)}, f32[256,256]{1,0:T(8,128)S(1)}, u32[]{:S(2)}, u32[]{:S(2)}) collective-permute-start(f32[256,256]{1,0:T(8,128)S(1)} %pad_maximum_fusion.3), channel_id=1, source_target_pairs={{0,1},{1,0},{2,3},{3,2},{4,6},{5,7},{6,4},{7,5},{8,9},{9,8},{10,11... | collective-permute-start | bytes 786440 | tf_op jit(solution)/shard_map/ppermute | solution.py:141
  23.7 0.6 %collective-permute-start.9 = (f32[256,256]{1,0:T(8,128)S(1)}, f32[256,256]{1,0:T(8,128)S(1)}, u32[]{:S(2)}, u32[]{:S(2)}) collective-permute-start(f32[256,256]{1,0:T(8,128)S(1)} %pad_maximum_fusion.4), channel_id=1, source_target_pairs={{0,1},{1,0},{2,3},{3,2},{4,6},{5,7},{6,4},{7,5},{8,9},{9,8},{10,11... | collective-permute-start | bytes 786440 | tf_op jit(solution)/shard_map/ppermute | solution.py:141
  24.3 2.7 %collective-permute-start.11 = (f32[128,512]{1,0:T(8,128)S(1)}, f32[128,512]{1,0:T(8,128)S(1)}, u32[]{:S(2)}, u32[]{:S(2)}) collective-permute-start(f32[128,512]{1,0:T(8,128)S(1)} %slice_add_fusion), channel_id=1, source_target_pairs={{8,24},{12,28},{16,0},{20,4},{0,8},{4,12},{24,16},{28,20},{9,25},{... | collective-permute-start | bytes 786440 | tf_op jit(solution)/shard_map/ppermute | solution.py:66
  27.0 1.6 %collective-permute-done.7 = f32[256,256]{1,0:T(8,128)S(1)} collective-permute-done((f32[256,256]{1,0:T(8,128)S(1)}, f32[256,256]{1,0:T(8,128)S(1)}, u32[]{:S(2)}, u32[]{:S(2)}) %collective-permute-start.7) | collective-permute-done | bytes 262176 | tf_op jit(solution)/shard_map/ppermute | solution.py:141
  28.6 1.6 %collective-permute-start.8 = (f32[128,256]{1,0:T(8,128)S(1)}, f32[128,256]{1,0:T(8,128)S(1)}, u32[]{:S(2)}, u32[]{:S(2)}) collective-permute-start(f32[128,256]{1,0:T(8,128)S(1)} %slice.35), channel_id=1, source_target_pairs={{0,2},{1,3},{2,0},{3,1},{4,5},{5,4},{6,7},{7,6},{8,10},{9,11},{10,... | collective-permute-start | bytes 393224 | tf_op jit(solution)/shard_map/ppermute | solution.py:141
  30.2 1.7 %collective-permute-done.9 = f32[256,256]{1,0:T(8,128)S(1)} collective-permute-done((f32[256,256]{1,0:T(8,128)S(1)}, f32[256,256]{1,0:T(8,128)S(1)}, u32[]{:S(2)}, u32[]{:S(2)}) %collective-permute-start.9) | collective-permute-done | bytes 262176 | tf_op jit(solution)/shard_map/ppermute | solution.py:141
  31.9 1.6 %collective-permute-start.10 = (f32[128,256]{1,0:T(8,128)S(1)}, f32[128,256]{1,0:T(8,128)S(1)}, u32[]{:S(2)}, u32[]{:S(2)}) collective-permute-start(f32[128,256]{1,0:T(8,128)S(1)} %slice.37), channel_id=1, source_target_pairs={{0,2},{1,3},{2,0},{3,1},{4,5},{5,4},{6,7},{7,6},{8,10},{9,11},{10,... | collective-permute-start | bytes 393224 | tf_op jit(solution)/shard_map/ppermute | solution.py:141
  33.7 3.3 %collective-permute-done.10 = f32[128,256]{1,0:T(8,128)S(1)} collective-permute-done((f32[128,256]{1,0:T(8,128)S(1)}, f32[128,256]{1,0:T(8,128)S(1)}, u32[]{:S(2)}, u32[]{:S(2)}) %collective-permute-start.10) | collective-permute-done | bytes 131104 | tf_op jit(solution)/shard_map/ppermute | solution.py:141
  37.0 0.7 %maximum_add_fusion.2 = f32[128,512]{1,0:T(8,128)} fusion(f32[128,512]{1,0:T(8,128)S(1)} %collective-permute-done.11, f32[128,256]{1,0:T(8,128)S(1)} %slice_add_fusion.1, f32[128,256]{1,0:T(8,128)S(1)} %slice_add_fusion.2), kind=kLoop, calls=%fused_computation.16 | loop fusion | flops 131072 | bytes 786432 | tf_op jit(solution)/shard_map/add | solution.py:148
  (33 shorter events, 3.6 us)
Async XLA Ops:
  0.0 1.2 %copy-start = (f32[512,512]{1,0:T(8,128)S(1)}, f32[512,512]{1,0:T(8,128)}, u32[]{:S(2)}) copy-start(f32[512,512]{1,0:T(8,128)} %param.2) | copy-start | bytes 3145732
  1.2 9.7 %collective-permute-start.1 = (f32[128,512]{1,0:T(8,128)S(1)}, f32[128,512]{1,0:T(8,128)S(1)}, u32[]{:S(2)}, u32[]{:S(2)}) collective-permute-start(f32[128,512]{1,0:T(8,128)S(1)} %constant_dynamic-slice_fusion.8), channel_id=1, source_target_pairs={{0,16},{4,20},{24,8},{28,12},{8,0},{12,4},{16,24},{20,28},{1,17},{... | collective-permute-start | bytes 786440 | tf_op jit(solution)/shard_map/ppermute | solution.py:66
  5.3 8.0 %collective-permute-start = (f32[128,512]{1,0:T(8,128)S(1)}, f32[128,512]{1,0:T(8,128)S(1)}, u32[]{:S(2)}, u32[]{:S(2)}) collective-permute-start(f32[128,512]{1,0:T(8,128)S(1)} %constant_dynamic-slice_fusion.8), channel_id=1, source_target_pairs={{0,4},{4,0},{8,12},{12,8},{16,20},{20,16},{24,28},{28,24},{1,5},{5... | collective-permute-start | bytes 786440 | tf_op jit(solution)/shard_map/ppermute | solution.py:69
  5.4 1.6 %copy-start.1 = (f32[512,1,1024]{2,1,0:T(1,128)S(1)}, f32[512,1,1024]{2,1,0:T(1,128)}, u32[]{:S(2)}) copy-start(f32[512,1,1024]{2,1,0:T(1,128)} %kernel_ref.1) | copy-start | bytes 6291460
  8.1 9.7 %collective-permute-start.5 = (f32[128,512]{1,0:T(8,128)S(1)}, f32[128,512]{1,0:T(8,128)}, u32[]{:S(2)}, u32[]{:S(2)}) collective-permute-start(f32[128,512]{1,0:T(8,128)S(1)} %constant_dynamic-slice_fusion.8), channel_id=1, source_target_pairs={{8,16},{12,20},{16,8},{20,12},{9,17},{13,21},{17,9},{21,13},{10,18... | collective-permute-start | bytes 786440 | tf_op jit(solution)/shard_map/ppermute | solution.py:66
  10.9 8.0 %collective-permute-start.4 = (f32[128,512]{1,0:T(8,128)S(1)}, f32[128,512]{1,0:T(8,128)S(1)}, u32[]{:S(2)}, u32[]{:S(2)}) collective-permute-start(f32[128,512]{1,0:T(8,128)S(1)} %collective-permute-done.1), channel_id=1, source_target_pairs={{0,8},{4,12},{8,0},{12,4},{16,24},{20,28},{24,16},{28,20},{1,9},{5... | collective-permute-start | bytes 786440 | tf_op jit(solution)/shard_map/ppermute | solution.py:66
  13.3 1.5 %collective-permute-start.2 = (f32[128,512]{1,0:T(8,128)S(1)}, f32[128,512]{1,0:T(8,128)S(1)}, u32[]{:S(2)}, u32[]{:S(2)}) collective-permute-start(f32[128,512]{1,0:T(8,128)S(1)} %collective-permute-done.1), channel_id=1, source_target_pairs={{0,4},{4,0},{8,12},{12,8},{16,20},{20,16},{24,28},{28,24},{1,5},{5... | collective-permute-start | bytes 786440 | tf_op jit(solution)/shard_map/ppermute | solution.py:69
  16.1 1.6 %collective-permute-start.3 = (f32[128,512]{1,0:T(8,128)S(1)}, f32[128,512]{1,0:T(8,128)S(1)}, u32[]{:S(2)}, u32[]{:S(2)}) collective-permute-start(f32[128,512]{1,0:T(8,128)S(1)} %slice.33), channel_id=1, source_target_pairs={{0,4},{4,0},{8,12},{12,8},{16,20},{20,16},{24,28},{28,24},{1,5},{5... | collective-permute-start | bytes 786440 | tf_op jit(solution)/shard_map/ppermute | solution.py:69
  19.0 1.6 %collective-permute-start.6 = (f32[128,512]{1,0:T(8,128)S(1)}, f32[128,512]{1,0:T(8,128)S(1)}, u32[]{:S(2)}, u32[]{:S(2)}) collective-permute-start(f32[128,512]{1,0:T(8,128)S(1)} %broadcast_select_fusion), channel_id=1, source_target_pairs={{0,4},{4,0},{8,12},{12,8},{16,20},{20,16},{24,28},{28,24},{1,5},{5... | collective-permute-start | bytes 786440 | tf_op jit(solution)/shard_map/ppermute | solution.py:69
  22.1 6.4 %collective-permute-start.7 = (f32[256,256]{1,0:T(8,128)S(1)}, f32[256,256]{1,0:T(8,128)S(1)}, u32[]{:S(2)}, u32[]{:S(2)}) collective-permute-start(f32[256,256]{1,0:T(8,128)S(1)} %pad_maximum_fusion.3), channel_id=1, source_target_pairs={{0,1},{1,0},{2,3},{3,2},{4,6},{5,7},{6,4},{7,5},{8,9},{9,8},{10,11... | collective-permute-start | bytes 786440 | tf_op jit(solution)/shard_map/ppermute | solution.py:141
  23.7 8.2 %collective-permute-start.9 = (f32[256,256]{1,0:T(8,128)S(1)}, f32[256,256]{1,0:T(8,128)S(1)}, u32[]{:S(2)}, u32[]{:S(2)}) collective-permute-start(f32[256,256]{1,0:T(8,128)S(1)} %pad_maximum_fusion.4), channel_id=1, source_target_pairs={{0,1},{1,0},{2,3},{3,2},{4,6},{5,7},{6,4},{7,5},{8,9},{9,8},{10,11... | collective-permute-start | bytes 786440 | tf_op jit(solution)/shard_map/ppermute | solution.py:141
  24.3 12.7 %collective-permute-start.11 = (f32[128,512]{1,0:T(8,128)S(1)}, f32[128,512]{1,0:T(8,128)S(1)}, u32[]{:S(2)}, u32[]{:S(2)}) collective-permute-start(f32[128,512]{1,0:T(8,128)S(1)} %slice_add_fusion), channel_id=1, source_target_pairs={{8,24},{12,28},{16,0},{20,4},{0,8},{4,12},{24,16},{28,20},{9,25},{... | collective-permute-start | bytes 786440 | tf_op jit(solution)/shard_map/ppermute | solution.py:66
  28.6 5.0 %collective-permute-start.8 = (f32[128,256]{1,0:T(8,128)S(1)}, f32[128,256]{1,0:T(8,128)S(1)}, u32[]{:S(2)}, u32[]{:S(2)}) collective-permute-start(f32[128,256]{1,0:T(8,128)S(1)} %slice.35), channel_id=1, source_target_pairs={{0,2},{1,3},{2,0},{3,1},{4,5},{5,4},{6,7},{7,6},{8,10},{9,11},{10,... | collective-permute-start | bytes 393224 | tf_op jit(solution)/shard_map/ppermute | solution.py:141
  31.9 5.0 %collective-permute-start.10 = (f32[128,256]{1,0:T(8,128)S(1)}, f32[128,256]{1,0:T(8,128)S(1)}, u32[]{:S(2)}, u32[]{:S(2)}) collective-permute-start(f32[128,256]{1,0:T(8,128)S(1)} %slice.37), channel_id=1, source_target_pairs={{0,2},{1,3},{2,0},{3,1},{4,5},{5,4},{6,7},{7,6},{8,10},{9,11},{10,... | collective-permute-start | bytes 393224 | tf_op jit(solution)/shard_map/ppermute | solution.py:141

commit v5 on v4

--- a/solution.py
+++ b/solution.py
@@ -102,14 +102,16 @@
     back = back[:share] + other_core(back[share:])
     total += rows_of(weights, points)
 
+    total, back, swapped = lax.optimization_barrier((total, back, swapped))
+    swapped = jnp.where(inner, swapped, own)
     total, back, passed, swapped = lax.optimization_barrier((total, back, passed, swapped))
     held = jnp.where(inner, swapped, passed)
     pair_held = other_core(held)
     z_last = z_late
     total += rows_of(weighted(z_last[:, :share], held), held)
     total, pair_held = lax.optimization_barrier((total, pair_held))
-    total += rows_of(weighted(z_last[:, share:], pair_held), pair_held)
-    total, back = lax.optimization_barrier((total, back))
+    last = rows_of(weighted(z_last[:, share:], pair_held), pair_held)
+    total, last, back = lax.optimization_barrier((total, last, back))
     returned = along(
         back, [(c, c ^ half) for c in inner_chips] + [(c, c ^ near) for c in outer_chips]
     )
@@ -125,11 +127,12 @@
     masks = [jnp.where(q % CORES == 0, share_mask(p, 0), share_mask(p, 1)) for p in range(nshares)]
     cut = orbitals.shape[1] // CHUNKS
 
+    def block_of(value, place, chunk):
+        start = ((share_id ^ masks[place]) * share, chunk * cut)
+        return lax.dynamic_slice(value, start, (share, cut))
+
     def blocks_of(places, chunk):
-        found = [
-            lax.dynamic_slice(total, ((share_id ^ masks[p]) * share, chunk * cut), (share, cut))
-            for p in places
-        ]
+        found = [block_of(total, p, chunk) + block_of(last, p, chunk) for p in places]
         return jnp.concatenate(found, axis=0)
 
     def halve(keep, send, step):

time: 37.9 us -> 37.5 us (0.989)
  waiting for transfers between devices: 10.4 us -> 11.3 us
  starting transfers between devices: 16.2 us -> 15.3 us
  local copies, waits for them, and re-layouts: 3.11 us -> 2.72 us
    unnamed x5, local copies, waits for them, and re-layouts: 2.84 us -> 1.61 us
    ppermute x4, waiting for transfers between devices: 6.68 us -> 7.65 us  [halve(): return keep + lax.ppermute(send, ('blk', 'split'), pairs)]
    ppermute x4, starting transfers between devices: 10.5 us -> 9.56 us  [along(): return lax.ppermute(value, 'blk', full)]
    dynamic_slice x1, local copies, waits for them, and re-layouts: 0.02 us -> 0.97 us  [per_device(): own = lax.dynamic_slice_in_dim(orbitals, share_id * share, share, 0)]
  transfers between devices with their start and end apart: 12 -> 12, of which waited for: 9 -> 9; matrix products, arithmetic and copies ran while one was open for 12% -> 13% of each run, Pallas kernels for 3% -> 3%
where the time goes in v5:
time: 37.5 us; the launch traced here: 37.3 us
  starting transfers between devices  15.3 us (41%)
  waiting for transfers between devices  11.3 us (30%)
  matrix products  5.39 us (14%)
  local copies, waits for them, and re-layouts  2.72 us (7%)
  other arithmetic  1.37 us (4%)
  Pallas kernels  1.06 us (3%)
    ppermute x4, starting transfers between devices, along(): return lax.ppermute(value, 'blk', full)  9.56 us
    ppermute x4, waiting for transfers between devices, halve(): return keep + lax.ppermute(send, ('blk', 'split'), pairs)  7.65 us
    dot_general x9, matrix products, product(): lax.dot_general(a, b, (dims, ((), ())), precision=lax.Precision.HIGH, pre...  5.39 us
    ppermute x4, starting transfers between devices, halve(): return keep + lax.ppermute(send, ('blk', 'split'), pairs)  5.31 us
    ppermute x4, waiting for transfers between devices, along(): return lax.ppermute(value, 'blk', full)  2.54 us
    unnamed x5, local copies, waits for them, and re-layouts  1.61 us
    ppermute x4, waiting for transfers between devices, other_core(): lax.ppermute(value, 'blk', [(i, i ^ 1) for i in range(nchips * CORES)])  1.08 us
    pallas_call x1, Pallas kernels, pick_columns(): pl.pallas_call(pick_body, in_specs=[pl.BlockSpec(memory_space=pltpu.SMEM)...  1.06 us
  transfers between devices with their start and end apart: 12, of which 9 were waited for; matrix products, arithmetic and copies ran while one was open for 13% of the time, Pallas kernels for 3%

profile of v5, /device:TPU:0, one launch (start us, length us, event | category | flops | bytes accessed | tf_op | source)
XLA Modules:
  0.0 37.3 jit_solution(12675255837020111748)
XLA Ops:
  0.0 1.0 %constant_dynamic-slice_fusion = f32[128,512]{1,0:T(8,128)S(1)} fusion(f32[512,512]{1,0:T(8,128)} %param.2, s32[]{:T(128)S(6)} %select_n.78), kind=kLoop, calls=%fused_computation.31 | loop fusion | bytes 524292 | tf_op jit(solution)/shard_map/dynamic_slice | solution.py:71
  1.0 4.1 %collective-permute-start.1 = (f32[128,512]{1,0:T(8,128)S(1)}, f32[128,512]{1,0:T(8,128)S(1)}, u32[]{:S(2)}, u32[]{:S(2)}) collective-permute-start(f32[128,512]{1,0:T(8,128)S(1)} %constant_dynamic-slice_fusion), channel_id=1, source_target_pairs={{0,16},{4,20},{24,8},{28,12},{8,0},{12,4},{16,24},{20,28},{1,17},{... | collective-permute-start | bytes 786440 | tf_op jit(solution)/shard_map/ppermute | solution.py:66
  5.1 1.6 %copy-done = f32[512,1,1024]{2,1,0:T(1,128)S(1)} copy-done((f32[512,1,1024]{2,1,0:T(1,128)S(1)}, f32[512,1,1024]{2,1,0:T(1,128)}, u32[]{:S(2)}) %copy-start) | copy-done | bytes 2097176
  6.7 1.1 %shard_map.28 = (f32[512,256]{1,0:T(8,128)S(1)}, f32[512,256]{1,0:T(8,128)S(1)}, f32[512,256]{1,0:T(8,128)S(1)}) custom-call(s32[6]{0:T(128)S(1)} %stack.27.at_ref, f32[512,1,1024]{2,1,0:T(1,128)S(1)} %copy-done), custom_call_target="tpu_custom_call" | custom-call | bytes 2097152 | tf_op jit(solution)/shard_map/pallas_call | solution.py:34
  7.8 1.4 %collective-permute-start.4 = (f32[128,512]{1,0:T(8,128)S(1)}, f32[128,512]{1,0:T(8,128)}, u32[]{:S(2)}, u32[]{:S(2)}) collective-permute-start(f32[128,512]{1,0:T(8,128)S(1)} %constant_dynamic-slice_fusion), channel_id=1, source_target_pairs={{8,16},{12,20},{16,8},{20,12},{9,17},{13,21},{17,9},{21,13},{10,18... | collective-permute-start | bytes 786440 | tf_op jit(solution)/shard_map/ppermute | solution.py:66
  9.2 1.4 %collective-permute-done.1 = f32[128,512]{1,0:T(8,128)S(1)} collective-permute-done((f32[128,512]{1,0:T(8,128)S(1)}, f32[128,512]{1,0:T(8,128)S(1)}, u32[]{:S(2)}, u32[]{:S(2)}) %collective-permute-start.1) | collective-permute-done | bytes 262176 | tf_op jit(solution)/shard_map/ppermute | solution.py:66
  10.6 2.4 %collective-permute-start.5 = (f32[128,512]{1,0:T(8,128)S(1)}, f32[128,512]{1,0:T(8,128)S(1)}, u32[]{:S(2)}, u32[]{:S(2)}) collective-permute-start(f32[128,512]{1,0:T(8,128)S(1)} %collective-permute-done.1), channel_id=1, source_target_pairs={{0,8},{4,12},{8,0},{12,4},{16,24},{20,28},{24,16},{28,20},{1,9},{5... | collective-permute-start | bytes 786440 | tf_op jit(solution)/shard_map/ppermute | solution.py:66
  13.0 0.6 %fusion.1 = f32[512,256]{1,0:T(8,128)S(1)} fusion(f32[512,256]{1,0:T(8,128)S(1)} %get-tuple-element.23, f32[512,512]{1,0:T(8,128)S(1)} %copy-done.1, f32[128,512]{1,0:T(8,128)S(1)} %collective-permute-done, f32[128,512]{1,0:T(8,128)S(1)} %constant_dynamic-slice_fusion), kind=kOutput, calls=%fused_computation.4 | convolution fusion | flops 402915328 | bytes 2621440 | tf_op jit(solution)/shard_map/dot_general | solution.py:15
  13.7 0.6 %fusion.4 = f32[512,512]{1,0:T(8,128)S(1)} fusion(f32[512,256]{1,0:T(8,128)S(1)} %fusion.1, f32[128,512]{1,0:T(8,128)S(1)} %collective-permute-done, f32[128,512]{1,0:T(8,128)S(1)} %constant_dynamic-slice_fusion), kind=kOutput, calls=%fused_computation.10 | convolution fusion | flops 402784256 | bytes 2097152 | tf_op jit(solution)/shard_map/dot_general | solution.py:15
  14.6 0.6 %fusion = f32[512,256]{1,0:T(8,128)S(1)} fusion(f32[512,256]{1,0:T(8,128)S(1)} %get-tuple-element.26, f32[256,512]{1,0:T(8,128)S(1)} %constant_dynamic-update-slice_fusion, f32[512,512]{1,0:T(8,128)S(1)} %copy-done.1), kind=kOutput, calls=%fused_computation.2 | convolution fusion | flops 402784256 | bytes 2621440 | tf_op jit(solution)/shard_map/dot_general | solution.py:15
  15.2 0.7 %fusion.7 = f32[256,512]{1,0:T(8,128)S(1)} fusion(f32[512,256]{1,0:T(8,128)S(1)} %fusion, f32[512,512]{1,0:T(8,128)S(1)} %copy-done.1), kind=kOutput, calls=%fused_computation.34 | convolution fusion | flops 402653184 | bytes 2097152 | tf_op jit(solution)/shard_map/dot_general | solution.py:15
  16.2 0.6 %convolution_add_fusion = f32[512,512]{1,0:T(8,128)S(1)} fusion(f32[512,512]{1,0:T(8,128)S(1)} %fusion.4, f32[512,256]{1,0:T(8,128)S(1)} %fusion, f32[256,512]{1,0:T(8,128)S(1)} %constant_dynamic-update-slice_fusion), kind=kOutput, calls=%fused_computation | convolution fusion | flops 402915328 | bytes 3145728 | tf_op jit(solution)/shard_map/dot_general | solution.py:15
  16.8 0.7 %collective-permute-done.3 = f32[128,512]{1,0:T(8,128)S(1)} collective-permute-done((f32[128,512]{1,0:T(8,128)S(1)}, f32[128,512]{1,0:T(8,128)S(1)}, u32[]{:S(2)}, u32[]{:S(2)}) %collective-permute-start.3) | collective-permute-done | bytes 262176 | tf_op jit(solution)/shard_map/ppermute | solution.py:69
  17.6 1.1 %collective-permute-done.5 = f32[128,512]{1,0:T(8,128)S(1)} collective-permute-done((f32[128,512]{1,0:T(8,128)S(1)}, f32[128,512]{1,0:T(8,128)S(1)}, u32[]{:S(2)}, u32[]{:S(2)}) %collective-permute-start.5) | collective-permute-done | bytes 262176 | tf_op jit(solution)/shard_map/ppermute | solution.py:66
  20.3 0.6 %fusion.3 = f32[512,128]{1,0:T(8,128)S(1)} fusion(f32[128,512]{1,0:T(8,128)S(1)} %collective-permute-done.6, f32[512,512]{1,0:T(8,128)S(1)} %copy-done.1, f32[512,256]{1,0:T(8,128)S(1)} %get-tuple-element.32), kind=kOutput, calls=%fused_computation.8 | convolution fusion | flops 201392128 | bytes 1835008 | tf_op jit(solution)/shard_map/dot_general | solution.py:15
  21.7 1.5 %collective-permute-start.7 = (f32[256,256]{1,0:T(8,128)S(1)}, f32[256,256]{1,0:T(8,128)S(1)}, u32[]{:S(2)}, u32[]{:S(2)}) collective-permute-start(f32[256,256]{1,0:T(8,128)S(1)} %pad_maximum_fusion.3), channel_id=1, source_target_pairs={{0,1},{1,0},{2,3},{3,2},{4,6},{5,7},{6,4},{7,5},{8,9},{9,8},{10,11... | collective-permute-start | bytes 786440 | tf_op jit(solution)/shard_map/ppermute | solution.py:144
  23.2 0.6 %collective-permute-start.9 = (f32[256,256]{1,0:T(8,128)S(1)}, f32[256,256]{1,0:T(8,128)S(1)}, u32[]{:S(2)}, u32[]{:S(2)}) collective-permute-start(f32[256,256]{1,0:T(8,128)S(1)} %pad_maximum_fusion.4), channel_id=1, source_target_pairs={{0,1},{1,0},{2,3},{3,2},{4,6},{5,7},{6,4},{7,5},{8,9},{9,8},{10,11... | collective-permute-start | bytes 786440 | tf_op jit(solution)/shard_map/ppermute | solution.py:144
  23.8 1.7 %collective-permute-start.11 = (f32[128,512]{1,0:T(8,128)S(1)}, f32[128,512]{1,0:T(8,128)S(1)}, u32[]{:S(2)}, u32[]{:S(2)}) collective-permute-start(f32[128,512]{1,0:T(8,128)S(1)} %slice_add_fusion), channel_id=1, source_target_pairs={{8,24},{12,28},{16,0},{20,4},{0,8},{4,12},{24,16},{28,20},{9,25},{... | collective-permute-start | bytes 786440 | tf_op jit(solution)/shard_map/ppermute | solution.py:66
  25.6 2.5 %collective-permute-done.7 = f32[256,256]{1,0:T(8,128)S(1)} collective-permute-done((f32[256,256]{1,0:T(8,128)S(1)}, f32[256,256]{1,0:T(8,128)S(1)}, u32[]{:S(2)}, u32[]{:S(2)}) %collective-permute-start.7) | collective-permute-done | bytes 262176 | tf_op jit(solution)/shard_map/ppermute | solution.py:144
  28.2 1.6 %collective-permute-start.8 = (f32[128,256]{1,0:T(8,128)S(1)}, f32[128,256]{1,0:T(8,128)S(1)}, u32[]{:S(2)}, u32[]{:S(2)}) collective-permute-start(f32[128,256]{1,0:T(8,128)S(1)} %slice.35), channel_id=1, source_target_pairs={{0,2},{1,3},{2,0},{3,1},{4,5},{5,4},{6,7},{7,6},{8,10},{9,11},{10,... | collective-permute-start | bytes 393224 | tf_op jit(solution)/shard_map/ppermute | solution.py:144
  29.7 1.7 %collective-permute-done.9 = f32[256,256]{1,0:T(8,128)S(1)} collective-permute-done((f32[256,256]{1,0:T(8,128)S(1)}, f32[256,256]{1,0:T(8,128)S(1)}, u32[]{:S(2)}, u32[]{:S(2)}) %collective-permute-start.9) | collective-permute-done | bytes 262176 | tf_op jit(solution)/shard_map/ppermute | solution.py:144
  31.5 1.6 %collective-permute-start.10 = (f32[128,256]{1,0:T(8,128)S(1)}, f32[128,256]{1,0:T(8,128)S(1)}, u32[]{:S(2)}, u32[]{:S(2)}) collective-permute-start(f32[128,256]{1,0:T(8,128)S(1)} %slice.37), channel_id=1, source_target_pairs={{0,2},{1,3},{2,0},{3,1},{4,5},{5,4},{6,7},{7,6},{8,10},{9,11},{10,... | collective-permute-start | bytes 393224 | tf_op jit(solution)/shard_map/ppermute | solution.py:144
  33.2 3.3 %collective-permute-done.10 = f32[128,256]{1,0:T(8,128)S(1)} collective-permute-done((f32[128,256]{1,0:T(8,128)S(1)}, f32[128,256]{1,0:T(8,128)S(1)}, u32[]{:S(2)}, u32[]{:S(2)}) %collective-permute-start.10) | collective-permute-done | bytes 131104 | tf_op jit(solution)/shard_map/ppermute | solution.py:144
  36.5 0.7 %maximum_add_fusion.2 = f32[128,512]{1,0:T(8,128)} fusion(f32[128,512]{1,0:T(8,128)S(1)} %collective-permute-done.11, f32[128,256]{1,0:T(8,128)S(1)} %slice_add_fusion.1, f32[128,256]{1,0:T(8,128)S(1)} %slice_add_fusion.2), kind=kLoop, calls=%fused_computation.16 | loop fusion | flops 131072 | bytes 786432 | tf_op jit(solution)/shard_map/add | solution.py:151
  (33 shorter events, 3.5 us)
Async XLA Ops:
  1.0 9.7 %collective-permute-start.1 = (f32[128,512]{1,0:T(8,128)S(1)}, f32[128,512]{1,0:T(8,128)S(1)}, u32[]{:S(2)}, u32[]{:S(2)}) collective-permute-start(f32[128,512]{1,0:T(8,128)S(1)} %constant_dynamic-slice_fusion), channel_id=1, source_target_pairs={{0,16},{4,20},{24,8},{28,12},{8,0},{12,4},{16,24},{20,28},{1,17},{... | collective-permute-start | bytes 786440 | tf_op jit(solution)/shard_map/ppermute | solution.py:66
  5.1 8.0 %collective-permute-start = (f32[128,512]{1,0:T(8,128)S(1)}, f32[128,512]{1,0:T(8,128)S(1)}, u32[]{:S(2)}, u32[]{:S(2)}) collective-permute-start(f32[128,512]{1,0:T(8,128)S(1)} %constant_dynamic-slice_fusion), channel_id=1, source_target_pairs={{0,4},{4,0},{8,12},{12,8},{16,20},{20,16},{24,28},{28,24},{1,5},{5... | collective-permute-start | bytes 786440 | tf_op jit(solution)/shard_map/ppermute | solution.py:69
  5.1 1.6 %copy-start = (f32[512,1,1024]{2,1,0:T(1,128)S(1)}, f32[512,1,1024]{2,1,0:T(1,128)}, u32[]{:S(2)}) copy-start(f32[512,1,1024]{2,1,0:T(1,128)} %kernel_ref.1) | copy-start | bytes 6291460
  6.7 6.3 %copy-start.1 = (f32[512,512]{1,0:T(8,128)S(1)}, f32[512,512]{1,0:T(8,128)}, u32[]{:S(2)}) copy-start(f32[512,512]{1,0:T(8,128)} %param.2) | copy-start | bytes 3145732
  7.8 9.7 %collective-permute-start.4 = (f32[128,512]{1,0:T(8,128)S(1)}, f32[128,512]{1,0:T(8,128)}, u32[]{:S(2)}, u32[]{:S(2)}) collective-permute-start(f32[128,512]{1,0:T(8,128)S(1)} %constant_dynamic-slice_fusion), channel_id=1, source_target_pairs={{8,16},{12,20},{16,8},{20,12},{9,17},{13,21},{17,9},{21,13},{10,18... | collective-permute-start | bytes 786440 | tf_op jit(solution)/shard_map/ppermute | solution.py:66
  10.6 8.0 %collective-permute-start.5 = (f32[128,512]{1,0:T(8,128)S(1)}, f32[128,512]{1,0:T(8,128)S(1)}, u32[]{:S(2)}, u32[]{:S(2)}) collective-permute-start(f32[128,512]{1,0:T(8,128)S(1)} %collective-permute-done.1), channel_id=1, source_target_pairs={{0,8},{4,12},{8,0},{12,4},{16,24},{20,28},{24,16},{28,20},{1,9},{5... | collective-permute-start | bytes 786440 | tf_op jit(solution)/shard_map/ppermute | solution.py:66
  13.0 1.5 %collective-permute-start.2 = (f32[128,512]{1,0:T(8,128)S(1)}, f32[128,512]{1,0:T(8,128)S(1)}, u32[]{:S(2)}, u32[]{:S(2)}) collective-permute-start(f32[128,512]{1,0:T(8,128)S(1)} %collective-permute-done.1), channel_id=1, source_target_pairs={{0,4},{4,0},{8,12},{12,8},{16,20},{20,16},{24,28},{28,24},{1,5},{5... | collective-permute-start | bytes 786440 | tf_op jit(solution)/shard_map/ppermute | solution.py:69
  15.9 1.6 %collective-permute-start.3 = (f32[128,512]{1,0:T(8,128)S(1)}, f32[128,512]{1,0:T(8,128)S(1)}, u32[]{:S(2)}, u32[]{:S(2)}) collective-permute-start(f32[128,512]{1,0:T(8,128)S(1)} %slice.33), channel_id=1, source_target_pairs={{0,4},{4,0},{8,12},{12,8},{16,20},{20,16},{24,28},{28,24},{1,5},{5... | collective-permute-start | bytes 786440 | tf_op jit(solution)/shard_map/ppermute | solution.py:69
  18.7 1.6 %collective-permute-start.6 = (f32[128,512]{1,0:T(8,128)S(1)}, f32[128,512]{1,0:T(8,128)S(1)}, u32[]{:S(2)}, u32[]{:S(2)}) collective-permute-start(f32[128,512]{1,0:T(8,128)S(1)} %broadcast_select_fusion), channel_id=1, source_target_pairs={{0,4},{4,0},{8,12},{12,8},{16,20},{20,16},{24,28},{28,24},{1,5},{5... | collective-permute-start | bytes 786440 | tf_op jit(solution)/shard_map/ppermute | solution.py:69
  21.7 6.4 %collective-permute-start.7 = (f32[256,256]{1,0:T(8,128)S(1)}, f32[256,256]{1,0:T(8,128)S(1)}, u32[]{:S(2)}, u32[]{:S(2)}) collective-permute-start(f32[256,256]{1,0:T(8,128)S(1)} %pad_maximum_fusion.3), channel_id=1, source_target_pairs={{0,1},{1,0},{2,3},{3,2},{4,6},{5,7},{6,4},{7,5},{8,9},{9,8},{10,11... | collective-permute-start | bytes 786440 | tf_op jit(solution)/shard_map/ppermute | solution.py:144
  23.2 8.2 %collective-permute-start.9 = (f32[256,256]{1,0:T(8,128)S(1)}, f32[256,256]{1,0:T(8,128)S(1)}, u32[]{:S(2)}, u32[]{:S(2)}) collective-permute-start(f32[256,256]{1,0:T(8,128)S(1)} %pad_maximum_fusion.4), channel_id=1, source_target_pairs={{0,1},{1,0},{2,3},{3,2},{4,6},{5,7},{6,4},{7,5},{8,9},{9,8},{10,11... | collective-permute-start | bytes 786440 | tf_op jit(solution)/shard_map/ppermute | solution.py:144
  23.8 12.7 %collective-permute-start.11 = (f32[128,512]{1,0:T(8,128)S(1)}, f32[128,512]{1,0:T(8,128)S(1)}, u32[]{:S(2)}, u32[]{:S(2)}) collective-permute-start(f32[128,512]{1,0:T(8,128)S(1)} %slice_add_fusion), channel_id=1, source_target_pairs={{8,24},{12,28},{16,0},{20,4},{0,8},{4,12},{24,16},{28,20},{9,25},{... | collective-permute-start | bytes 786440 | tf_op jit(solution)/shard_map/ppermute | solution.py:66
  28.2 5.0 %collective-permute-start.8 = (f32[128,256]{1,0:T(8,128)S(1)}, f32[128,256]{1,0:T(8,128)S(1)}, u32[]{:S(2)}, u32[]{:S(2)}) collective-permute-start(f32[128,256]{1,0:T(8,128)S(1)} %slice.35), channel_id=1, source_target_pairs={{0,2},{1,3},{2,0},{3,1},{4,5},{5,4},{6,7},{7,6},{8,10},{9,11},{10,... | collective-permute-start | bytes 393224 | tf_op jit(solution)/shard_map/ppermute | solution.py:144
  31.5 5.0 %collective-permute-start.10 = (f32[128,256]{1,0:T(8,128)S(1)}, f32[128,256]{1,0:T(8,128)S(1)}, u32[]{:S(2)}, u32[]{:S(2)}) collective-permute-start(f32[128,256]{1,0:T(8,128)S(1)} %slice.37), channel_id=1, source_target_pairs={{0,2},{1,3},{2,0},{3,1},{4,5},{5,4},{6,7},{7,6},{8,10},{9,11},{10,... | collective-permute-start | bytes 393224 | tf_op jit(solution)/shard_map/ppermute | solution.py:144

commit v6 on v5

--- a/solution.py
+++ b/solution.py
@@ -125,29 +125,33 @@
         return sum(((place >> (bits - 1 - t)) & 1) << bit_at(t, on_core) for t in range(bits))
 
     masks = [jnp.where(q % CORES == 0, share_mask(p, 0), share_mask(p, 1)) for p in range(nshares)]
-    cut = orbitals.shape[1] // CHUNKS
+    cut = orbitals.shape[1] * 1 // 2
+    cuts = [(0, cut), (cut, orbitals.shape[1] - cut)]
 
-    def block_of(value, place, chunk):
-        start = ((share_id ^ masks[place]) * share, chunk * cut)
-        return lax.dynamic_slice(value, start, (share, cut))
+    def block_of(value, place, start, size):
+        start = ((share_id ^ masks[place]) * share, start)
+        return lax.dynamic_slice(value, start, (share, size))
 
-    def blocks_of(places, chunk):
-        found = [block_of(total, p, chunk) + block_of(last, p, chunk) for p in places]
+    def blocks_of(places, where):
+        found = [block_of(total, p, *where) + block_of(last, p, *where) for p in places]
         return jnp.concatenate(found, axis=0)
 
-    def halve(keep, send, step):
+    def exchange(send, step):
         pairs = [
             (b * nshares + s, b * nshares + (s ^ (1 << bit_at(step, b % CORES))))
             for b in range(nchips * CORES)
             for s in range(nshares)
         ]
-        return keep + lax.ppermute(send, ("blk", "split"), pairs)
+        return lax.ppermute(send, ("blk", "split"), pairs)
 
     places, middle = list(range(nshares)), nshares // 2
-    parts = [halve(blocks_of(places[:middle], k), blocks_of(places[middle:], k), 0) for k in range(CHUNKS)]
+    gots = [exchange(blocks_of(places[middle:], where), 0) for where in cuts]
+    wide = blocks_of(places[:middle], cuts[0]) + gots[0]
+    got, _ = lax.optimization_barrier((gots[1], wide))
+    parts = [wide, blocks_of(places[:middle], cuts[1]) + got]
     for step in range(1, bits):
         size = parts[0].shape[0] // 2
-        parts = [halve(part[:size], part[size:], step) for part in parts]
+        parts = [part[:size] + exchange(part[size:], step) for part in parts]
     return jnp.concatenate(parts, axis=1) + returned
 
 

time: 37.5 us -> 37.5 us (level)
  no operation moved by 1% of the time
where the time goes in v6:
time: 37.5 us; the launch traced here: 37.3 us
  starting transfers between devices  15.3 us (41%)
  waiting for transfers between devices  11.3 us (30%)
  matrix products  5.39 us (14%)
  local copies, waits for them, and re-layouts  2.72 us (7%)
  other arithmetic  1.37 us (4%)
  Pallas kernels  1.06 us (3%)
    ppermute x4, starting transfers between devices, along(): return lax.ppermute(value, 'blk', full)  9.56 us
    ppermute x4, waiting for transfers between devices, exchange(): return lax.ppermute(send, ('blk', 'split'), pairs)  7.65 us
    dot_general x9, matrix products, product(): lax.dot_general(a, b, (dims, ((), ())), precision=lax.Precision.HIGH, pre...  5.39 us
    ppermute x4, starting transfers between devices, exchange(): return lax.ppermute(send, ('blk', 'split'), pairs)  5.31 us
    ppermute x4, waiting for transfers between devices, along(): return lax.ppermute(value, 'blk', full)  2.54 us
    unnamed x5, local copies, waits for them, and re-layouts  1.61 us
    ppermute x4, waiting for transfers between devices, other_core(): lax.ppermute(value, 'blk', [(i, i ^ 1) for i in range(nchips * CORES)])  1.08 us
    pallas_call x1, Pallas kernels, pick_columns(): pl.pallas_call(pick_body, in_specs=[pl.BlockSpec(memory_space=pltpu.SMEM)...  1.06 us
  transfers between devices with their start and end apart: 12, of which 9 were waited for; matrix products, arithmetic and copies ran while one was open for 13% of the time, Pallas kernels for 3%

profile of v6, /device:TPU:0, one launch (start us, length us, event | category | flops | bytes accessed | tf_op | source)
XLA Modules:
  0.0 37.3 jit_solution(7364526132543740161)
XLA Ops:
  0.0 1.0 %constant_dynamic-slice_fusion = f32[128,512]{1,0:T(8,128)S(1)} fusion(f32[512,512]{1,0:T(8,128)} %param.2, s32[]{:T(128)S(6)} %select_n.78), kind=kLoop, calls=%fused_computation.31 | loop fusion | bytes 524292 | tf_op jit(solution)/shard_map/dynamic_slice | solution.py:71
  1.0 4.1 %collective-permute-start.1 = (f32[128,512]{1,0:T(8,128)S(1)}, f32[128,512]{1,0:T(8,128)S(1)}, u32[]{:S(2)}, u32[]{:S(2)}) collective-permute-start(f32[128,512]{1,0:T(8,128)S(1)} %constant_dynamic-slice_fusion), channel_id=1, source_target_pairs={{0,16},{4,20},{24,8},{28,12},{8,0},{12,4},{16,24},{20,28},{1,17},{... | collective-permute-start | bytes 786440 | tf_op jit(solution)/shard_map/ppermute | solution.py:66
  5.1 1.6 %copy-done = f32[512,1,1024]{2,1,0:T(1,128)S(1)} copy-done((f32[512,1,1024]{2,1,0:T(1,128)S(1)}, f32[512,1,1024]{2,1,0:T(1,128)}, u32[]{:S(2)}) %copy-start) | copy-done | bytes 2097176
  6.7 1.1 %shard_map.28 = (f32[512,256]{1,0:T(8,128)S(1)}, f32[512,256]{1,0:T(8,128)S(1)}, f32[512,256]{1,0:T(8,128)S(1)}) custom-call(s32[6]{0:T(128)S(1)} %stack.27.at_ref, f32[512,1,1024]{2,1,0:T(1,128)S(1)} %copy-done), custom_call_target="tpu_custom_call" | custom-call | bytes 2097152 | tf_op jit(solution)/shard_map/pallas_call | solution.py:34
  7.8 1.4 %collective-permute-start.4 = (f32[128,512]{1,0:T(8,128)S(1)}, f32[128,512]{1,0:T(8,128)}, u32[]{:S(2)}, u32[]{:S(2)}) collective-permute-start(f32[128,512]{1,0:T(8,128)S(1)} %constant_dynamic-slice_fusion), channel_id=1, source_target_pairs={{8,16},{12,20},{16,8},{20,12},{9,17},{13,21},{17,9},{21,13},{10,18... | collective-permute-start | bytes 786440 | tf_op jit(solution)/shard_map/ppermute | solution.py:66
  9.2 1.4 %collective-permute-done.1 = f32[128,512]{1,0:T(8,128)S(1)} collective-permute-done((f32[128,512]{1,0:T(8,128)S(1)}, f32[128,512]{1,0:T(8,128)S(1)}, u32[]{:S(2)}, u32[]{:S(2)}) %collective-permute-start.1) | collective-permute-done | bytes 262176 | tf_op jit(solution)/shard_map/ppermute | solution.py:66
  10.6 2.4 %collective-permute-start.5 = (f32[128,512]{1,0:T(8,128)S(1)}, f32[128,512]{1,0:T(8,128)S(1)}, u32[]{:S(2)}, u32[]{:S(2)}) collective-permute-start(f32[128,512]{1,0:T(8,128)S(1)} %collective-permute-done.1), channel_id=1, source_target_pairs={{0,8},{4,12},{8,0},{12,4},{16,24},{20,28},{24,16},{28,20},{1,9},{5... | collective-permute-start | bytes 786440 | tf_op jit(solution)/shard_map/ppermute | solution.py:66
  13.0 0.6 %fusion.1 = f32[512,256]{1,0:T(8,128)S(1)} fusion(f32[512,256]{1,0:T(8,128)S(1)} %get-tuple-element.24, f32[512,512]{1,0:T(8,128)S(1)} %copy-done.1, f32[128,512]{1,0:T(8,128)S(1)} %collective-permute-done, f32[128,512]{1,0:T(8,128)S(1)} %constant_dynamic-slice_fusion), kind=kOutput, calls=%fused_computation.4 | convolution fusion | flops 402915328 | bytes 2621440 | tf_op jit(solution)/shard_map/dot_general | solution.py:15
  13.7 0.6 %fusion.4 = f32[512,512]{1,0:T(8,128)S(1)} fusion(f32[512,256]{1,0:T(8,128)S(1)} %fusion.1, f32[128,512]{1,0:T(8,128)S(1)} %collective-permute-done, f32[128,512]{1,0:T(8,128)S(1)} %constant_dynamic-slice_fusion), kind=kOutput, calls=%fused_computation.10 | convolution fusion | flops 402784256 | bytes 2097152 | tf_op jit(solution)/shard_map/dot_general | solution.py:15
  14.6 0.6 %fusion = f32[512,256]{1,0:T(8,128)S(1)} fusion(f32[512,256]{1,0:T(8,128)S(1)} %get-tuple-element.27, f32[256,512]{1,0:T(8,128)S(1)} %constant_dynamic-update-slice_fusion, f32[512,512]{1,0:T(8,128)S(1)} %copy-done.1), kind=kOutput, calls=%fused_computation.2 | convolution fusion | flops 402784256 | bytes 2621440 | tf_op jit(solution)/shard_map/dot_general | solution.py:15
  15.2 0.7 %fusion.7 = f32[256,512]{1,0:T(8,128)S(1)} fusion(f32[512,256]{1,0:T(8,128)S(1)} %fusion, f32[512,512]{1,0:T(8,128)S(1)} %copy-done.1), kind=kOutput, calls=%fused_computation.34 | convolution fusion | flops 402653184 | bytes 2097152 | tf_op jit(solution)/shard_map/dot_general | solution.py:15
  16.2 0.6 %convolution_add_fusion = f32[512,512]{1,0:T(8,128)S(1)} fusion(f32[512,512]{1,0:T(8,128)S(1)} %fusion.4, f32[512,256]{1,0:T(8,128)S(1)} %fusion, f32[256,512]{1,0:T(8,128)S(1)} %constant_dynamic-update-slice_fusion), kind=kOutput, calls=%fused_computation | convolution fusion | flops 402915328 | bytes 3145728 | tf_op jit(solution)/shard_map/dot_general | solution.py:15
  16.8 0.7 %collective-permute-done.3 = f32[128,512]{1,0:T(8,128)S(1)} collective-permute-done((f32[128,512]{1,0:T(8,128)S(1)}, f32[128,512]{1,0:T(8,128)S(1)}, u32[]{:S(2)}, u32[]{:S(2)}) %collective-permute-start.3) | collective-permute-done | bytes 262176 | tf_op jit(solution)/shard_map/ppermute | solution.py:69
  17.6 1.1 %collective-permute-done.5 = f32[128,512]{1,0:T(8,128)S(1)} collective-permute-done((f32[128,512]{1,0:T(8,128)S(1)}, f32[128,512]{1,0:T(8,128)S(1)}, u32[]{:S(2)}, u32[]{:S(2)}) %collective-permute-start.5) | collective-permute-done | bytes 262176 | tf_op jit(solution)/shard_map/ppermute | solution.py:66
  20.3 0.6 %fusion.3 = f32[512,128]{1,0:T(8,128)S(1)} fusion(f32[128,512]{1,0:T(8,128)S(1)} %collective-permute-done.6, f32[512,512]{1,0:T(8,128)S(1)} %copy-done.1, f32[512,256]{1,0:T(8,128)S(1)} %get-tuple-element.33), kind=kOutput, calls=%fused_computation.8 | convolution fusion | flops 201392128 | bytes 1835008 | tf_op jit(solution)/shard_map/dot_general | solution.py:15
  21.7 1.5 %collective-permute-start.7 = (f32[256,256]{1,0:T(8,128)S(1)}, f32[256,256]{1,0:T(8,128)S(1)}, u32[]{:S(2)}, u32[]{:S(2)}) collective-permute-start(f32[256,256]{1,0:T(8,128)S(1)} %pad_maximum_fusion.3), channel_id=1, source_target_pairs={{0,1},{1,0},{2,3},{3,2},{4,6},{5,7},{6,4},{7,5},{8,9},{9,8},{10,11... | collective-permute-start | bytes 786440 | tf_op jit(solution)/shard_map/ppermute | solution.py:145
  23.2 0.6 %collective-permute-start.9 = (f32[256,256]{1,0:T(8,128)S(1)}, f32[256,256]{1,0:T(8,128)S(1)}, u32[]{:S(2)}, u32[]{:S(2)}) collective-permute-start(f32[256,256]{1,0:T(8,128)S(1)} %pad_maximum_fusion.4), channel_id=1, source_target_pairs={{0,1},{1,0},{2,3},{3,2},{4,6},{5,7},{6,4},{7,5},{8,9},{9,8},{10,11... | collective-permute-start | bytes 786440 | tf_op jit(solution)/shard_map/ppermute | solution.py:145
  23.8 1.7 %collective-permute-start.11 = (f32[128,512]{1,0:T(8,128)S(1)}, f32[128,512]{1,0:T(8,128)S(1)}, u32[]{:S(2)}, u32[]{:S(2)}) collective-permute-start(f32[128,512]{1,0:T(8,128)S(1)} %slice_add_fusion), channel_id=1, source_target_pairs={{8,24},{12,28},{16,0},{20,4},{0,8},{4,12},{24,16},{28,20},{9,25},{... | collective-permute-start | bytes 786440 | tf_op jit(solution)/shard_map/ppermute | solution.py:66
  25.6 2.5 %collective-permute-done.7 = f32[256,256]{1,0:T(8,128)S(1)} collective-permute-done((f32[256,256]{1,0:T(8,128)S(1)}, f32[256,256]{1,0:T(8,128)S(1)}, u32[]{:S(2)}, u32[]{:S(2)}) %collective-permute-start.7) | collective-permute-done | bytes 262176 | tf_op jit(solution)/shard_map/ppermute | solution.py:145
  28.2 1.6 %collective-permute-start.8 = (f32[128,256]{1,0:T(8,128)S(1)}, f32[128,256]{1,0:T(8,128)S(1)}, u32[]{:S(2)}, u32[]{:S(2)}) collective-permute-start(f32[128,256]{1,0:T(8,128)S(1)} %slice.35), channel_id=1, source_target_pairs={{0,2},{1,3},{2,0},{3,1},{4,5},{5,4},{6,7},{7,6},{8,10},{9,11},{10,... | collective-permute-start | bytes 393224 | tf_op jit(solution)/shard_map/ppermute | solution.py:145
  29.7 1.7 %collective-permute-done.9 = f32[256,256]{1,0:T(8,128)S(1)} collective-permute-done((f32[256,256]{1,0:T(8,128)S(1)}, f32[256,256]{1,0:T(8,128)S(1)}, u32[]{:S(2)}, u32[]{:S(2)}) %collective-permute-start.9) | collective-permute-done | bytes 262176 | tf_op jit(solution)/shard_map/ppermute | solution.py:145
  31.5 1.6 %collective-permute-start.10 = (f32[128,256]{1,0:T(8,128)S(1)}, f32[128,256]{1,0:T(8,128)S(1)}, u32[]{:S(2)}, u32[]{:S(2)}) collective-permute-start(f32[128,256]{1,0:T(8,128)S(1)} %slice.37), channel_id=1, source_target_pairs={{0,2},{1,3},{2,0},{3,1},{4,5},{5,4},{6,7},{7,6},{8,10},{9,11},{10,... | collective-permute-start | bytes 393224 | tf_op jit(solution)/shard_map/ppermute | solution.py:145
  33.2 3.3 %collective-permute-done.10 = f32[128,256]{1,0:T(8,128)S(1)} collective-permute-done((f32[128,256]{1,0:T(8,128)S(1)}, f32[128,256]{1,0:T(8,128)S(1)}, u32[]{:S(2)}, u32[]{:S(2)}) %collective-permute-start.10) | collective-permute-done | bytes 131104 | tf_op jit(solution)/shard_map/ppermute | solution.py:145
  36.5 0.7 %maximum_add_fusion.2 = f32[128,512]{1,0:T(8,128)} fusion(f32[128,512]{1,0:T(8,128)S(1)} %collective-permute-done.11, f32[128,256]{1,0:T(8,128)S(1)} %slice_add_fusion.1, f32[128,256]{1,0:T(8,128)S(1)} %slice_add_fusion.2), kind=kLoop, calls=%fused_computation.16 | loop fusion | flops 131072 | bytes 786432 | tf_op jit(solution)/shard_map/add | solution.py:155
  (33 shorter events, 3.5 us)
Async XLA Ops:
  1.0 9.7 %collective-permute-start.1 = (f32[128,512]{1,0:T(8,128)S(1)}, f32[128,512]{1,0:T(8,128)S(1)}, u32[]{:S(2)}, u32[]{:S(2)}) collective-permute-start(f32[128,512]{1,0:T(8,128)S(1)} %constant_dynamic-slice_fusion), channel_id=1, source_target_pairs={{0,16},{4,20},{24,8},{28,12},{8,0},{12,4},{16,24},{20,28},{1,17},{... | collective-permute-start | bytes 786440 | tf_op jit(solution)/shard_map/ppermute | solution.py:66
  5.1 8.0 %collective-permute-start = (f32[128,512]{1,0:T(8,128)S(1)}, f32[128,512]{1,0:T(8,128)S(1)}, u32[]{:S(2)}, u32[]{:S(2)}) collective-permute-start(f32[128,512]{1,0:T(8,128)S(1)} %constant_dynamic-slice_fusion), channel_id=1, source_target_pairs={{0,4},{4,0},{8,12},{12,8},{16,20},{20,16},{24,28},{28,24},{1,5},{5... | collective-permute-start | bytes 786440 | tf_op jit(solution)/shard_map/ppermute | solution.py:69
  5.1 1.6 %copy-start = (f32[512,1,1024]{2,1,0:T(1,128)S(1)}, f32[512,1,1024]{2,1,0:T(1,128)}, u32[]{:S(2)}) copy-start(f32[512,1,1024]{2,1,0:T(1,128)} %kernel_ref.1) | copy-start | bytes 6291460
  6.7 6.3 %copy-start.1 = (f32[512,512]{1,0:T(8,128)S(1)}, f32[512,512]{1,0:T(8,128)}, u32[]{:S(2)}) copy-start(f32[512,512]{1,0:T(8,128)} %param.2) | copy-start | bytes 3145732
  7.8 9.7 %collective-permute-start.4 = (f32[128,512]{1,0:T(8,128)S(1)}, f32[128,512]{1,0:T(8,128)}, u32[]{:S(2)}, u32[]{:S(2)}) collective-permute-start(f32[128,512]{1,0:T(8,128)S(1)} %constant_dynamic-slice_fusion), channel_id=1, source_target_pairs={{8,16},{12,20},{16,8},{20,12},{9,17},{13,21},{17,9},{21,13},{10,18... | collective-permute-start | bytes 786440 | tf_op jit(solution)/shard_map/ppermute | solution.py:66
  10.6 8.0 %collective-permute-start.5 = (f32[128,512]{1,0:T(8,128)S(1)}, f32[128,512]{1,0:T(8,128)S(1)}, u32[]{:S(2)}, u32[]{:S(2)}) collective-permute-start(f32[128,512]{1,0:T(8,128)S(1)} %collective-permute-done.1), channel_id=1, source_target_pairs={{0,8},{4,12},{8,0},{12,4},{16,24},{20,28},{24,16},{28,20},{1,9},{5... | collective-permute-start | bytes 786440 | tf_op jit(solution)/shard_map/ppermute | solution.py:66
  13.0 1.5 %collective-permute-start.2 = (f32[128,512]{1,0:T(8,128)S(1)}, f32[128,512]{1,0:T(8,128)S(1)}, u32[]{:S(2)}, u32[]{:S(2)}) collective-permute-start(f32[128,512]{1,0:T(8,128)S(1)} %collective-permute-done.1), channel_id=1, source_target_pairs={{0,4},{4,0},{8,12},{12,8},{16,20},{20,16},{24,28},{28,24},{1,5},{5... | collective-permute-start | bytes 786440 | tf_op jit(solution)/shard_map/ppermute | solution.py:69
  15.9 1.6 %collective-permute-start.3 = (f32[128,512]{1,0:T(8,128)S(1)}, f32[128,512]{1,0:T(8,128)S(1)}, u32[]{:S(2)}, u32[]{:S(2)}) collective-permute-start(f32[128,512]{1,0:T(8,128)S(1)} %slice.33), channel_id=1, source_target_pairs={{0,4},{4,0},{8,12},{12,8},{16,20},{20,16},{24,28},{28,24},{1,5},{5... | collective-permute-start | bytes 786440 | tf_op jit(solution)/shard_map/ppermute | solution.py:69
  18.7 1.6 %collective-permute-start.6 = (f32[128,512]{1,0:T(8,128)S(1)}, f32[128,512]{1,0:T(8,128)S(1)}, u32[]{:S(2)}, u32[]{:S(2)}) collective-permute-start(f32[128,512]{1,0:T(8,128)S(1)} %broadcast_select_fusion), channel_id=1, source_target_pairs={{0,4},{4,0},{8,12},{12,8},{16,20},{20,16},{24,28},{28,24},{1,5},{5... | collective-permute-start | bytes 786440 | tf_op jit(solution)/shard_map/ppermute | solution.py:69
  21.7 6.4 %collective-permute-start.7 = (f32[256,256]{1,0:T(8,128)S(1)}, f32[256,256]{1,0:T(8,128)S(1)}, u32[]{:S(2)}, u32[]{:S(2)}) collective-permute-start(f32[256,256]{1,0:T(8,128)S(1)} %pad_maximum_fusion.3), channel_id=1, source_target_pairs={{0,1},{1,0},{2,3},{3,2},{4,6},{5,7},{6,4},{7,5},{8,9},{9,8},{10,11... | collective-permute-start | bytes 786440 | tf_op jit(solution)/shard_map/ppermute | solution.py:145
  23.2 8.2 %collective-permute-start.9 = (f32[256,256]{1,0:T(8,128)S(1)}, f32[256,256]{1,0:T(8,128)S(1)}, u32[]{:S(2)}, u32[]{:S(2)}) collective-permute-start(f32[256,256]{1,0:T(8,128)S(1)} %pad_maximum_fusion.4), channel_id=1, source_target_pairs={{0,1},{1,0},{2,3},{3,2},{4,6},{5,7},{6,4},{7,5},{8,9},{9,8},{10,11... | collective-permute-start | bytes 786440 | tf_op jit(solution)/shard_map/ppermute | solution.py:145
  23.8 12.7 %collective-permute-start.11 = (f32[128,512]{1,0:T(8,128)S(1)}, f32[128,512]{1,0:T(8,128)S(1)}, u32[]{:S(2)}, u32[]{:S(2)}) collective-permute-start(f32[128,512]{1,0:T(8,128)S(1)} %slice_add_fusion), channel_id=1, source_target_pairs={{8,24},{12,28},{16,0},{20,4},{0,8},{4,12},{24,16},{28,20},{9,25},{... | collective-permute-start | bytes 786440 | tf_op jit(solution)/shard_map/ppermute | solution.py:66
  28.2 5.0 %collective-permute-start.8 = (f32[128,256]{1,0:T(8,128)S(1)}, f32[128,256]{1,0:T(8,128)S(1)}, u32[]{:S(2)}, u32[]{:S(2)}) collective-permute-start(f32[128,256]{1,0:T(8,128)S(1)} %slice.35), channel_id=1, source_target_pairs={{0,2},{1,3},{2,0},{3,1},{4,5},{5,4},{6,7},{7,6},{8,10},{9,11},{10,... | collective-permute-start | bytes 393224 | tf_op jit(solution)/shard_map/ppermute | solution.py:145
  31.5 5.0 %collective-permute-start.10 = (f32[128,256]{1,0:T(8,128)S(1)}, f32[128,256]{1,0:T(8,128)S(1)}, u32[]{:S(2)}, u32[]{:S(2)}) collective-permute-start(f32[128,256]{1,0:T(8,128)S(1)} %slice.37), channel_id=1, source_target_pairs={{0,2},{1,3},{2,0},{3,1},{4,5},{5,4},{6,7},{7,6},{8,10},{9,11},{10,... | collective-permute-start | bytes 393224 | tf_op jit(solution)/shard_map/ppermute | solution.py:145

commit v7 on v6

--- a/solution.py
+++ b/solution.py
@@ -15,6 +15,15 @@
     return lax.dot_general(
         a, b, (dims, ((), ())), precision=lax.Precision.HIGH, preferred_element_type=jnp.float32
     )
+
+
+def split(value):
+    high = lax.reduce_precision(value, exponent_bits=8, mantissa_bits=7)
+    return high.astype(jnp.bfloat16), (value - high).astype(jnp.bfloat16)
+
+
+def single(a, b, dims):
+    return lax.dot_general(a, b, (dims, ((), ())), preferred_element_type=jnp.float32)
 
 
 def pick_body(at_ref, kernel_ref, *out_refs):
@@ -110,7 +119,13 @@
     z_last = z_late
     total += rows_of(weighted(z_last[:, :share], held), held)
     total, pair_held = lax.optimization_barrier((total, pair_held))
-    last = rows_of(weighted(z_last[:, share:], pair_held), pair_held)
+    high, low = split(pair_held)
+    w_high, w_low = split(weighted(z_last[:, share:], pair_held))
+    last = single(
+        jnp.concatenate([w_high, w_low, w_high], axis=1),
+        jnp.concatenate([high, high, low], axis=0),
+        ((1,), (0,)),
+    )
     total, last, back = lax.optimization_barrier((total, last, back))
     returned = along(
         back, [(c, c ^ half) for c in inner_chips] + [(c, c ^ near) for c in outer_chips]
@@ -125,7 +140,7 @@
         return sum(((place >> (bits - 1 - t)) & 1) << bit_at(t, on_core) for t in range(bits))
 
     masks = [jnp.where(q % CORES == 0, share_mask(p, 0), share_mask(p, 1)) for p in range(nshares)]
-    cut = orbitals.shape[1] * 1 // 2
+    cut = orbitals.shape[1] // 2
     cuts = [(0, cut), (cut, orbitals.shape[1] - cut)]
 
     def block_of(value, place, start, size):

time: 37.5 us -> 37.4 us (level)
    dot_general x9 -> x8, matrix products: 5.39 us -> 4.83 us  [product(): lax.dot_general(a, b, (dims, ((), ())), precision=lax.Precision.HIGH, pre...]
    dot_general x0 -> x1, matrix products: none -> 0.43 us  [single(): lax.dot_general(a, b, (dims, ((), ())), preferred_element_type=jnp.float32)]
where the time goes in v7:
time: 37.4 us; the launch traced here: 37.2 us
  starting transfers between devices  15.3 us (41%)
  waiting for transfers between devices  11.3 us (30%)
  matrix products  5.25 us (14%)
  local copies, waits for them, and re-layouts  2.72 us (7%)
  other arithmetic  1.41 us (4%)
  Pallas kernels  1.06 us (3%)
    ppermute x4, starting transfers between devices, along(): return lax.ppermute(value, 'blk', full)  9.55 us
    ppermute x4, waiting for transfers between devices, exchange(): return lax.ppermute(send, ('blk', 'split'), pairs)  7.62 us
    ppermute x4, starting transfers between devices, exchange(): return lax.ppermute(send, ('blk', 'split'), pairs)  5.32 us
    dot_general x8, matrix products, product(): lax.dot_general(a, b, (dims, ((), ())), precision=lax.Precision.HIGH, pre...  4.83 us
    ppermute x4, waiting for transfers between devices, along(): return lax.ppermute(value, 'blk', full)  2.55 us
    unnamed x5, local copies, waits for them, and re-layouts  1.61 us
    ppermute x4, waiting for transfers between devices, other_core(): lax.ppermute(value, 'blk', [(i, i ^ 1) for i in range(nchips * CORES)])  1.08 us
    pallas_call x1, Pallas kernels, pick_columns(): pl.pallas_call(pick_body, in_specs=[pl.BlockSpec(memory_space=pltpu.SMEM)...  1.06 us
  transfers between devices with their start and end apart: 12, of which 9 were waited for; matrix products, arithmetic and copies ran while one was open for 13% of the time, Pallas kernels for 3%

profile of v7, /device:TPU:0, one launch (start us, length us, event | category | flops | bytes accessed | tf_op | source)
XLA Modules:
  0.0 37.2 jit_solution(6222908991945824596)
XLA Ops:
  0.0 1.0 %constant_dynamic-slice_fusion = f32[128,512]{1,0:T(8,128)S(1)} fusion(f32[512,512]{1,0:T(8,128)} %param.2, s32[]{:T(128)S(6)} %select_n.78), kind=kLoop, calls=%fused_computation.48 | loop fusion | bytes 524292 | tf_op jit(solution)/shard_map/dynamic_slice | solution.py:80
  1.0 4.1 %collective-permute-start.1 = (f32[128,512]{1,0:T(8,128)S(1)}, f32[128,512]{1,0:T(8,128)S(1)}, u32[]{:S(2)}, u32[]{:S(2)}) collective-permute-start(f32[128,512]{1,0:T(8,128)S(1)} %constant_dynamic-slice_fusion), channel_id=1, source_target_pairs={{0,16},{4,20},{24,8},{28,12},{8,0},{12,4},{16,24},{20,28},{1,17},{... | collective-permute-start | bytes 786440 | tf_op jit(solution)/shard_map/ppermute | solution.py:75
  5.1 1.6 %copy-done = f32[512,1,1024]{2,1,0:T(1,128)S(1)} copy-done((f32[512,1,1024]{2,1,0:T(1,128)S(1)}, f32[512,1,1024]{2,1,0:T(1,128)}, u32[]{:S(2)}) %copy-start) | copy-done | bytes 2097176
  6.7 1.1 %shard_map.28 = (f32[512,256]{1,0:T(8,128)S(1)}, f32[512,256]{1,0:T(8,128)S(1)}, f32[512,256]{1,0:T(8,128)S(1)}) custom-call(s32[6]{0:T(128)S(1)} %stack.27.at_ref, f32[512,1,1024]{2,1,0:T(1,128)S(1)} %copy-done), custom_call_target="tpu_custom_call" | custom-call | bytes 2097152 | tf_op jit(solution)/shard_map/pallas_call | solution.py:43
  7.8 1.4 %collective-permute-start.4 = (f32[128,512]{1,0:T(8,128)S(1)}, f32[128,512]{1,0:T(8,128)}, u32[]{:S(2)}, u32[]{:S(2)}) collective-permute-start(f32[128,512]{1,0:T(8,128)S(1)} %constant_dynamic-slice_fusion), channel_id=1, source_target_pairs={{8,16},{12,20},{16,8},{20,12},{9,17},{13,21},{17,9},{21,13},{10,18... | collective-permute-start | bytes 786440 | tf_op jit(solution)/shard_map/ppermute | solution.py:75
  9.2 1.5 %collective-permute-done.1 = f32[128,512]{1,0:T(8,128)S(1)} collective-permute-done((f32[128,512]{1,0:T(8,128)S(1)}, f32[128,512]{1,0:T(8,128)S(1)}, u32[]{:S(2)}, u32[]{:S(2)}) %collective-permute-start.1) | collective-permute-done | bytes 262176 | tf_op jit(solution)/shard_map/ppermute | solution.py:75
  10.6 2.4 %collective-permute-start.5 = (f32[128,512]{1,0:T(8,128)S(1)}, f32[128,512]{1,0:T(8,128)S(1)}, u32[]{:S(2)}, u32[]{:S(2)}) collective-permute-start(f32[128,512]{1,0:T(8,128)S(1)} %collective-permute-done.1), channel_id=1, source_target_pairs={{0,8},{4,12},{8,0},{12,4},{16,24},{20,28},{24,16},{28,20},{1,9},{5... | collective-permute-start | bytes 786440 | tf_op jit(solution)/shard_map/ppermute | solution.py:75
  13.0 0.6 %fusion.1 = f32[512,256]{1,0:T(8,128)S(1)} fusion(f32[512,256]{1,0:T(8,128)S(1)} %get-tuple-element.24, f32[512,512]{1,0:T(8,128)S(1)} %copy-done.1, f32[128,512]{1,0:T(8,128)S(1)} %collective-permute-done, f32[128,512]{1,0:T(8,128)S(1)} %constant_dynamic-slice_fusion), kind=kOutput, calls=%fused_computation.4 | convolution fusion | flops 402915328 | bytes 2621440 | tf_op jit(solution)/shard_map/dot_general | solution.py:15
  13.7 0.6 %fusion.4 = f32[512,512]{1,0:T(8,128)S(1)} fusion(f32[512,256]{1,0:T(8,128)S(1)} %fusion.1, f32[128,512]{1,0:T(8,128)S(1)} %collective-permute-done, f32[128,512]{1,0:T(8,128)S(1)} %constant_dynamic-slice_fusion), kind=kOutput, calls=%fused_computation.10 | convolution fusion | flops 402784256 | bytes 2097152 | tf_op jit(solution)/shard_map/dot_general | solution.py:15
  14.6 0.6 %fusion = f32[512,256]{1,0:T(8,128)S(1)} fusion(f32[512,256]{1,0:T(8,128)S(1)} %get-tuple-element.27, f32[256,512]{1,0:T(8,128)S(1)} %constant_dynamic-update-slice_fusion, f32[512,512]{1,0:T(8,128)S(1)} %copy-done.1), kind=kOutput, calls=%fused_computation.2 | convolution fusion | flops 402784256 | bytes 2621440 | tf_op jit(solution)/shard_map/dot_general | solution.py:15
  15.2 0.7 %fusion.21 = f32[256,512]{1,0:T(8,128)S(1)} fusion(f32[512,256]{1,0:T(8,128)S(1)} %fusion, f32[512,512]{1,0:T(8,128)S(1)} %copy-done.1), kind=kOutput, calls=%fused_computation.52 | convolution fusion | flops 402653184 | bytes 2097152 | tf_op jit(solution)/shard_map/dot_general | solution.py:15
  16.2 0.6 %convolution_add_fusion = f32[512,512]{1,0:T(8,128)S(1)} fusion(f32[512,512]{1,0:T(8,128)S(1)} %fusion.4, f32[512,256]{1,0:T(8,128)S(1)} %fusion, f32[256,512]{1,0:T(8,128)S(1)} %constant_dynamic-update-slice_fusion), kind=kOutput, calls=%fused_computation | convolution fusion | flops 402915328 | bytes 3145728 | tf_op jit(solution)/shard_map/dot_general | solution.py:15
  16.8 0.7 %collective-permute-done.3 = f32[128,512]{1,0:T(8,128)S(1)} collective-permute-done((f32[128,512]{1,0:T(8,128)S(1)}, f32[128,512]{1,0:T(8,128)S(1)}, u32[]{:S(2)}, u32[]{:S(2)}) %collective-permute-start.3) | collective-permute-done | bytes 262176 | tf_op jit(solution)/shard_map/ppermute | solution.py:78
  17.6 1.1 %collective-permute-done.5 = f32[128,512]{1,0:T(8,128)S(1)} collective-permute-done((f32[128,512]{1,0:T(8,128)S(1)}, f32[128,512]{1,0:T(8,128)S(1)}, u32[]{:S(2)}, u32[]{:S(2)}) %collective-permute-start.5) | collective-permute-done | bytes 262176 | tf_op jit(solution)/shard_map/ppermute | solution.py:75
  20.3 0.6 %fusion.16 = (bf16[512,128]{1,0:T(8,128)(2,1)S(1)}, bf16[512,128]{1,0:T(8,128)(2,1)S(1)}) fusion(f32[128,512]{1,0:T(8,128)S(1)} %collective-permute-done.6, f32[512,512]{1,0:T(8,128)S(1)} %copy-done.1, f32[512,256]{1,0:T(8,128)S(1)} %get-tuple-element.33), kind=kOutput, calls=%fused_computation.26 | convolution fusion | flops 201654272 | bytes 1835008 | tf_op jit(solution)/shard_map/dot_general | solution.py:15
  21.6 1.6 %collective-permute-start.7 = (f32[256,256]{1,0:T(8,128)S(1)}, f32[256,256]{1,0:T(8,128)S(1)}, u32[]{:S(2)}, u32[]{:S(2)}) collective-permute-start(f32[256,256]{1,0:T(8,128)S(1)} %pad_maximum_fusion.3), channel_id=1, source_target_pairs={{0,1},{1,0},{2,3},{3,2},{4,6},{5,7},{6,4},{7,5},{8,9},{9,8},{10,11... | collective-permute-start | bytes 786440 | tf_op jit(solution)/shard_map/ppermute | solution.py:160
  23.1 0.6 %collective-permute-start.9 = (f32[256,256]{1,0:T(8,128)S(1)}, f32[256,256]{1,0:T(8,128)S(1)}, u32[]{:S(2)}, u32[]{:S(2)}) collective-permute-start(f32[256,256]{1,0:T(8,128)S(1)} %pad_maximum_fusion.4), channel_id=1, source_target_pairs={{0,1},{1,0},{2,3},{3,2},{4,6},{5,7},{6,4},{7,5},{8,9},{9,8},{10,11... | collective-permute-start | bytes 786440 | tf_op jit(solution)/shard_map/ppermute | solution.py:160
  23.7 1.7 %collective-permute-start.11 = (f32[128,512]{1,0:T(8,128)S(1)}, f32[128,512]{1,0:T(8,128)S(1)}, u32[]{:S(2)}, u32[]{:S(2)}) collective-permute-start(f32[128,512]{1,0:T(8,128)S(1)} %slice_add_fusion), channel_id=1, source_target_pairs={{8,24},{12,28},{16,0},{20,4},{0,8},{4,12},{24,16},{28,20},{9,25},{... | collective-permute-start | bytes 786440 | tf_op jit(solution)/shard_map/ppermute | solution.py:75
  25.5 2.5 %collective-permute-done.7 = f32[256,256]{1,0:T(8,128)S(1)} collective-permute-done((f32[256,256]{1,0:T(8,128)S(1)}, f32[256,256]{1,0:T(8,128)S(1)}, u32[]{:S(2)}, u32[]{:S(2)}) %collective-permute-start.7) | collective-permute-done | bytes 262176 | tf_op jit(solution)/shard_map/ppermute | solution.py:160
  28.1 1.6 %collective-permute-start.8 = (f32[128,256]{1,0:T(8,128)S(1)}, f32[128,256]{1,0:T(8,128)S(1)}, u32[]{:S(2)}, u32[]{:S(2)}) collective-permute-start(f32[128,256]{1,0:T(8,128)S(1)} %slice.35), channel_id=1, source_target_pairs={{0,2},{1,3},{2,0},{3,1},{4,5},{5,4},{6,7},{7,6},{8,10},{9,11},{10,... | collective-permute-start | bytes 393224 | tf_op jit(solution)/shard_map/ppermute | solution.py:160
  29.6 1.7 %collective-permute-done.9 = f32[256,256]{1,0:T(8,128)S(1)} collective-permute-done((f32[256,256]{1,0:T(8,128)S(1)}, f32[256,256]{1,0:T(8,128)S(1)}, u32[]{:S(2)}, u32[]{:S(2)}) %collective-permute-start.9) | collective-permute-done | bytes 262176 | tf_op jit(solution)/shard_map/ppermute | solution.py:160
  31.4 1.6 %collective-permute-start.10 = (f32[128,256]{1,0:T(8,128)S(1)}, f32[128,256]{1,0:T(8,128)S(1)}, u32[]{:S(2)}, u32[]{:S(2)}) collective-permute-start(f32[128,256]{1,0:T(8,128)S(1)} %slice.37), channel_id=1, source_target_pairs={{0,2},{1,3},{2,0},{3,1},{4,5},{5,4},{6,7},{7,6},{8,10},{9,11},{10,... | collective-permute-start | bytes 393224 | tf_op jit(solution)/shard_map/ppermute | solution.py:160
  33.1 3.3 %collective-permute-done.10 = f32[128,256]{1,0:T(8,128)S(1)} collective-permute-done((f32[128,256]{1,0:T(8,128)S(1)}, f32[128,256]{1,0:T(8,128)S(1)}, u32[]{:S(2)}, u32[]{:S(2)}) %collective-permute-start.10) | collective-permute-done | bytes 131104 | tf_op jit(solution)/shard_map/ppermute | solution.py:160
  36.4 0.7 %maximum_add_fusion.2 = f32[128,512]{1,0:T(8,128)} fusion(f32[128,512]{1,0:T(8,128)S(1)} %collective-permute-done.11, f32[128,256]{1,0:T(8,128)S(1)} %slice_add_fusion.1, f32[128,256]{1,0:T(8,128)S(1)} %slice_add_fusion.2), kind=kLoop, calls=%fused_computation.33 | loop fusion | flops 131072 | bytes 786432 | tf_op jit(solution)/shard_map/add | solution.py:170
  (34 shorter events, 3.4 us)
Async XLA Ops:
  1.0 9.7 %collective-permute-start.1 = (f32[128,512]{1,0:T(8,128)S(1)}, f32[128,512]{1,0:T(8,128)S(1)}, u32[]{:S(2)}, u32[]{:S(2)}) collective-permute-start(f32[128,512]{1,0:T(8,128)S(1)} %constant_dynamic-slice_fusion), channel_id=1, source_target_pairs={{0,16},{4,20},{24,8},{28,12},{8,0},{12,4},{16,24},{20,28},{1,17},{... | collective-permute-start | bytes 786440 | tf_op jit(solution)/shard_map/ppermute | solution.py:75
  5.1 8.0 %collective-permute-start = (f32[128,512]{1,0:T(8,128)S(1)}, f32[128,512]{1,0:T(8,128)S(1)}, u32[]{:S(2)}, u32[]{:S(2)}) collective-permute-start(f32[128,512]{1,0:T(8,128)S(1)} %constant_dynamic-slice_fusion), channel_id=1, source_target_pairs={{0,4},{4,0},{8,12},{12,8},{16,20},{20,16},{24,28},{28,24},{1,5},{5... | collective-permute-start | bytes 786440 | tf_op jit(solution)/shard_map/ppermute | solution.py:78
  5.1 1.6 %copy-start = (f32[512,1,1024]{2,1,0:T(1,128)S(1)}, f32[512,1,1024]{2,1,0:T(1,128)}, u32[]{:S(2)}) copy-start(f32[512,1,1024]{2,1,0:T(1,128)} %kernel_ref.1) | copy-start | bytes 6291460
  6.7 6.3 %copy-start.1 = (f32[512,512]{1,0:T(8,128)S(1)}, f32[512,512]{1,0:T(8,128)}, u32[]{:S(2)}) copy-start(f32[512,512]{1,0:T(8,128)} %param.2) | copy-start | bytes 3145732
  7.8 9.7 %collective-permute-start.4 = (f32[128,512]{1,0:T(8,128)S(1)}, f32[128,512]{1,0:T(8,128)}, u32[]{:S(2)}, u32[]{:S(2)}) collective-permute-start(f32[128,512]{1,0:T(8,128)S(1)} %constant_dynamic-slice_fusion), channel_id=1, source_target_pairs={{8,16},{12,20},{16,8},{20,12},{9,17},{13,21},{17,9},{21,13},{10,18... | collective-permute-start | bytes 786440 | tf_op jit(solution)/shard_map/ppermute | solution.py:75
  10.6 8.0 %collective-permute-start.5 = (f32[128,512]{1,0:T(8,128)S(1)}, f32[128,512]{1,0:T(8,128)S(1)}, u32[]{:S(2)}, u32[]{:S(2)}) collective-permute-start(f32[128,512]{1,0:T(8,128)S(1)} %collective-permute-done.1), channel_id=1, source_target_pairs={{0,8},{4,12},{8,0},{12,4},{16,24},{20,28},{24,16},{28,20},{1,9},{5... | collective-permute-start | bytes 786440 | tf_op jit(solution)/shard_map/ppermute | solution.py:75
  13.0 1.5 %collective-permute-start.2 = (f32[128,512]{1,0:T(8,128)S(1)}, f32[128,512]{1,0:T(8,128)S(1)}, u32[]{:S(2)}, u32[]{:S(2)}) collective-permute-start(f32[128,512]{1,0:T(8,128)S(1)} %collective-permute-done.1), channel_id=1, source_target_pairs={{0,4},{4,0},{8,12},{12,8},{16,20},{20,16},{24,28},{28,24},{1,5},{5... | collective-permute-start | bytes 786440 | tf_op jit(solution)/shard_map/ppermute | solution.py:78
  15.9 1.6 %collective-permute-start.3 = (f32[128,512]{1,0:T(8,128)S(1)}, f32[128,512]{1,0:T(8,128)S(1)}, u32[]{:S(2)}, u32[]{:S(2)}) collective-permute-start(f32[128,512]{1,0:T(8,128)S(1)} %slice.33), channel_id=1, source_target_pairs={{0,4},{4,0},{8,12},{12,8},{16,20},{20,16},{24,28},{28,24},{1,5},{5... | collective-permute-start | bytes 786440 | tf_op jit(solution)/shard_map/ppermute | solution.py:78
  18.7 1.6 %collective-permute-start.6 = (f32[128,512]{1,0:T(8,128)S(1)}, f32[128,512]{1,0:T(8,128)S(1)}, u32[]{:S(2)}, u32[]{:S(2)}) collective-permute-start(f32[128,512]{1,0:T(8,128)S(1)} %broadcast_select_fusion), channel_id=1, source_target_pairs={{0,4},{4,0},{8,12},{12,8},{16,20},{20,16},{24,28},{28,24},{1,5},{5... | collective-permute-start | bytes 786440 | tf_op jit(solution)/shard_map/ppermute | solution.py:78
  21.6 6.4 %collective-permute-start.7 = (f32[256,256]{1,0:T(8,128)S(1)}, f32[256,256]{1,0:T(8,128)S(1)}, u32[]{:S(2)}, u32[]{:S(2)}) collective-permute-start(f32[256,256]{1,0:T(8,128)S(1)} %pad_maximum_fusion.3), channel_id=1, source_target_pairs={{0,1},{1,0},{2,3},{3,2},{4,6},{5,7},{6,4},{7,5},{8,9},{9,8},{10,11... | collective-permute-start | bytes 786440 | tf_op jit(solution)/shard_map/ppermute | solution.py:160
  23.1 8.2 %collective-permute-start.9 = (f32[256,256]{1,0:T(8,128)S(1)}, f32[256,256]{1,0:T(8,128)S(1)}, u32[]{:S(2)}, u32[]{:S(2)}) collective-permute-start(f32[256,256]{1,0:T(8,128)S(1)} %pad_maximum_fusion.4), channel_id=1, source_target_pairs={{0,1},{1,0},{2,3},{3,2},{4,6},{5,7},{6,4},{7,5},{8,9},{9,8},{10,11... | collective-permute-start | bytes 786440 | tf_op jit(solution)/shard_map/ppermute | solution.py:160
  23.7 12.7 %collective-permute-start.11 = (f32[128,512]{1,0:T(8,128)S(1)}, f32[128,512]{1,0:T(8,128)S(1)}, u32[]{:S(2)}, u32[]{:S(2)}) collective-permute-start(f32[128,512]{1,0:T(8,128)S(1)} %slice_add_fusion), channel_id=1, source_target_pairs={{8,24},{12,28},{16,0},{20,4},{0,8},{4,12},{24,16},{28,20},{9,25},{... | collective-permute-start | bytes 786440 | tf_op jit(solution)/shard_map/ppermute | solution.py:75
  28.1 5.0 %collective-permute-start.8 = (f32[128,256]{1,0:T(8,128)S(1)}, f32[128,256]{1,0:T(8,128)S(1)}, u32[]{:S(2)}, u32[]{:S(2)}) collective-permute-start(f32[128,256]{1,0:T(8,128)S(1)} %slice.35), channel_id=1, source_target_pairs={{0,2},{1,3},{2,0},{3,1},{4,5},{5,4},{6,7},{7,6},{8,10},{9,11},{10,... | collective-permute-start | bytes 393224 | tf_op jit(solution)/shard_map/ppermute | solution.py:160
  31.4 5.0 %collective-permute-start.10 = (f32[128,256]{1,0:T(8,128)S(1)}, f32[128,256]{1,0:T(8,128)S(1)}, u32[]{:S(2)}, u32[]{:S(2)}) collective-permute-start(f32[128,256]{1,0:T(8,128)S(1)} %slice.37), channel_id=1, source_target_pairs={{0,2},{1,3},{2,0},{3,1},{4,5},{5,4},{6,7},{7,6},{8,10},{9,11},{10,... | collective-permute-start | bytes 393224 | tf_op jit(solution)/shard_map/ppermute | solution.py:160

commit v8 on v6

--- a/solution.py
+++ b/solution.py
@@ -111,7 +111,7 @@
     total += rows_of(weighted(z_last[:, :share], held), held)
     total, pair_held = lax.optimization_barrier((total, pair_held))
     last = rows_of(weighted(z_last[:, share:], pair_held), pair_held)
-    total, last, back = lax.optimization_barrier((total, last, back))
+    total, last = lax.optimization_barrier((total, last))
     returned = along(
         back, [(c, c ^ half) for c in inner_chips] + [(c, c ^ near) for c in outer_chips]
     )
@@ -125,7 +125,7 @@
         return sum(((place >> (bits - 1 - t)) & 1) << bit_at(t, on_core) for t in range(bits))
 
     masks = [jnp.where(q % CORES == 0, share_mask(p, 0), share_mask(p, 1)) for p in range(nshares)]
-    cut = orbitals.shape[1] * 1 // 2
+    cut = orbitals.shape[1] // 2
     cuts = [(0, cut), (cut, orbitals.shape[1] - cut)]
 
     def block_of(value, place, start, size):

time: 37.5 us -> 37.5 us (level)
  no operation moved by 1% of the time
where the time goes in v8:
time: 37.5 us; the launch traced here: 37.3 us
  starting transfers between devices  15.3 us (41%)
  waiting for transfers between devices  11.3 us (30%)
  matrix products  5.39 us (14%)
  local copies, waits for them, and re-layouts  2.72 us (7%)
  other arithmetic  1.37 us (4%)
  Pallas kernels  1.06 us (3%)
    ppermute x4, starting transfers between devices, along(): return lax.ppermute(value, 'blk', full)  9.56 us
    ppermute x4, waiting for transfers between devices, exchange(): return lax.ppermute(send, ('blk', 'split'), pairs)  7.65 us
    dot_general x9, matrix products, product(): lax.dot_general(a, b, (dims, ((), ())), precision=lax.Precision.HIGH, pre...  5.39 us
    ppermute x4, starting transfers between devices, exchange(): return lax.ppermute(send, ('blk', 'split'), pairs)  5.31 us
    ppermute x4, waiting for transfers between devices, along(): return lax.ppermute(value, 'blk', full)  2.54 us
    unnamed x5, local copies, waits for them, and re-layouts  1.61 us
    ppermute x4, waiting for transfers between devices, other_core(): lax.ppermute(value, 'blk', [(i, i ^ 1) for i in range(nchips * CORES)])  1.08 us
    pallas_call x1, Pallas kernels, pick_columns(): pl.pallas_call(pick_body, in_specs=[pl.BlockSpec(memory_space=pltpu.SMEM)...  1.06 us
  transfers between devices with their start and end apart: 12, of which 9 were waited for; matrix products, arithmetic and copies ran while one was open for 13% of the time, Pallas kernels for 3%

profile of v8, /device:TPU:0, one launch (start us, length us, event | category | flops | bytes accessed | tf_op | source)
XLA Modules:
  0.0 37.3 jit_solution(7364526132543740161)
XLA Ops:
  0.0 1.0 %constant_dynamic-slice_fusion = f32[128,512]{1,0:T(8,128)S(1)} fusion(f32[512,512]{1,0:T(8,128)} %param.2, s32[]{:T(128)S(6)} %select_n.78), kind=kLoop, calls=%fused_computation.31 | loop fusion | bytes 524292 | tf_op jit(solution)/shard_map/dynamic_slice | solution.py:71
  1.0 4.1 %collective-permute-start.1 = (f32[128,512]{1,0:T(8,128)S(1)}, f32[128,512]{1,0:T(8,128)S(1)}, u32[]{:S(2)}, u32[]{:S(2)}) collective-permute-start(f32[128,512]{1,0:T(8,128)S(1)} %constant_dynamic-slice_fusion), channel_id=1, source_target_pairs={{0,16},{4,20},{24,8},{28,12},{8,0},{12,4},{16,24},{20,28},{1,17},{... | collective-permute-start | bytes 786440 | tf_op jit(solution)/shard_map/ppermute | solution.py:66
  5.1 1.6 %copy-done = f32[512,1,1024]{2,1,0:T(1,128)S(1)} copy-done((f32[512,1,1024]{2,1,0:T(1,128)S(1)}, f32[512,1,1024]{2,1,0:T(1,128)}, u32[]{:S(2)}) %copy-start) | copy-done | bytes 2097176
  6.7 1.1 %shard_map.28 = (f32[512,256]{1,0:T(8,128)S(1)}, f32[512,256]{1,0:T(8,128)S(1)}, f32[512,256]{1,0:T(8,128)S(1)}) custom-call(s32[6]{0:T(128)S(1)} %stack.27.at_ref, f32[512,1,1024]{2,1,0:T(1,128)S(1)} %copy-done), custom_call_target="tpu_custom_call" | custom-call | bytes 2097152 | tf_op jit(solution)/shard_map/pallas_call | solution.py:34
  7.8 1.4 %collective-permute-start.4 = (f32[128,512]{1,0:T(8,128)S(1)}, f32[128,512]{1,0:T(8,128)}, u32[]{:S(2)}, u32[]{:S(2)}) collective-permute-start(f32[128,512]{1,0:T(8,128)S(1)} %constant_dynamic-slice_fusion), channel_id=1, source_target_pairs={{8,16},{12,20},{16,8},{20,12},{9,17},{13,21},{17,9},{21,13},{10,18... | collective-permute-start | bytes 786440 | tf_op jit(solution)/shard_map/ppermute | solution.py:66
  9.2 1.4 %collective-permute-done.1 = f32[128,512]{1,0:T(8,128)S(1)} collective-permute-done((f32[128,512]{1,0:T(8,128)S(1)}, f32[128,512]{1,0:T(8,128)S(1)}, u32[]{:S(2)}, u32[]{:S(2)}) %collective-permute-start.1) | collective-permute-done | bytes 262176 | tf_op jit(solution)/shard_map/ppermute | solution.py:66
  10.6 2.4 %collective-permute-start.5 = (f32[128,512]{1,0:T(8,128)S(1)}, f32[128,512]{1,0:T(8,128)S(1)}, u32[]{:S(2)}, u32[]{:S(2)}) collective-permute-start(f32[128,512]{1,0:T(8,128)S(1)} %collective-permute-done.1), channel_id=1, source_target_pairs={{0,8},{4,12},{8,0},{12,4},{16,24},{20,28},{24,16},{28,20},{1,9},{5... | collective-permute-start | bytes 786440 | tf_op jit(solution)/shard_map/ppermute | solution.py:66
  13.0 0.6 %fusion.1 = f32[512,256]{1,0:T(8,128)S(1)} fusion(f32[512,256]{1,0:T(8,128)S(1)} %get-tuple-element.23, f32[512,512]{1,0:T(8,128)S(1)} %copy-done.1, f32[128,512]{1,0:T(8,128)S(1)} %collective-permute-done, f32[128,512]{1,0:T(8,128)S(1)} %constant_dynamic-slice_fusion), kind=kOutput, calls=%fused_computation.4 | convolution fusion | flops 402915328 | bytes 2621440 | tf_op jit(solution)/shard_map/dot_general | solution.py:15
  13.7 0.6 %fusion.4 = f32[512,512]{1,0:T(8,128)S(1)} fusion(f32[512,256]{1,0:T(8,128)S(1)} %fusion.1, f32[128,512]{1,0:T(8,128)S(1)} %collective-permute-done, f32[128,512]{1,0:T(8,128)S(1)} %constant_dynamic-slice_fusion), kind=kOutput, calls=%fused_computation.10 | convolution fusion | flops 402784256 | bytes 2097152 | tf_op jit(solution)/shard_map/dot_general | solution.py:15
  14.6 0.6 %fusion = f32[512,256]{1,0:T(8,128)S(1)} fusion(f32[512,256]{1,0:T(8,128)S(1)} %get-tuple-element.26, f32[256,512]{1,0:T(8,128)S(1)} %constant_dynamic-update-slice_fusion, f32[512,512]{1,0:T(8,128)S(1)} %copy-done.1), kind=kOutput, calls=%fused_computation.2 | convolution fusion | flops 402784256 | bytes 2621440 | tf_op jit(solution)/shard_map/dot_general | solution.py:15
  15.2 0.7 %fusion.7 = f32[256,512]{1,0:T(8,128)S(1)} fusion(f32[512,256]{1,0:T(8,128)S(1)} %fusion, f32[512,512]{1,0:T(8,128)S(1)} %copy-done.1), kind=kOutput, calls=%fused_computation.34 | convolution fusion | flops 402653184 | bytes 2097152 | tf_op jit(solution)/shard_map/dot_general | solution.py:15
  16.2 0.6 %convolution_add_fusion = f32[512,512]{1,0:T(8,128)S(1)} fusion(f32[512,512]{1,0:T(8,128)S(1)} %fusion.4, f32[512,256]{1,0:T(8,128)S(1)} %fusion, f32[256,512]{1,0:T(8,128)S(1)} %constant_dynamic-update-slice_fusion), kind=kOutput, calls=%fused_computation | convolution fusion | flops 402915328 | bytes 3145728 | tf_op jit(solution)/shard_map/dot_general | solution.py:15
  16.8 0.7 %collective-permute-done.3 = f32[128,512]{1,0:T(8,128)S(1)} collective-permute-done((f32[128,512]{1,0:T(8,128)S(1)}, f32[128,512]{1,0:T(8,128)S(1)}, u32[]{:S(2)}, u32[]{:S(2)}) %collective-permute-start.3) | collective-permute-done | bytes 262176 | tf_op jit(solution)/shard_map/ppermute | solution.py:69
  17.6 1.1 %collective-permute-done.5 = f32[128,512]{1,0:T(8,128)S(1)} collective-permute-done((f32[128,512]{1,0:T(8,128)S(1)}, f32[128,512]{1,0:T(8,128)S(1)}, u32[]{:S(2)}, u32[]{:S(2)}) %collective-permute-start.5) | collective-permute-done | bytes 262176 | tf_op jit(solution)/shard_map/ppermute | solution.py:66
  20.3 0.6 %fusion.3 = f32[512,128]{1,0:T(8,128)S(1)} fusion(f32[128,512]{1,0:T(8,128)S(1)} %collective-permute-done.6, f32[512,512]{1,0:T(8,128)S(1)} %copy-done.1, f32[512,256]{1,0:T(8,128)S(1)} %get-tuple-element.32), kind=kOutput, calls=%fused_computation.8 | convolution fusion | flops 201392128 | bytes 1835008 | tf_op jit(solution)/shard_map/dot_general | solution.py:15
  21.7 1.5 %collective-permute-start.7 = (f32[256,256]{1,0:T(8,128)S(1)}, f32[256,256]{1,0:T(8,128)S(1)}, u32[]{:S(2)}, u32[]{:S(2)}) collective-permute-start(f32[256,256]{1,0:T(8,128)S(1)} %pad_maximum_fusion.3), channel_id=1, source_target_pairs={{0,1},{1,0},{2,3},{3,2},{4,6},{5,7},{6,4},{7,5},{8,9},{9,8},{10,11... | collective-permute-start | bytes 786440 | tf_op jit(solution)/shard_map/ppermute | solution.py:145
  23.2 0.6 %collective-permute-start.9 = (f32[256,256]{1,0:T(8,128)S(1)}, f32[256,256]{1,0:T(8,128)S(1)}, u32[]{:S(2)}, u32[]{:S(2)}) collective-permute-start(f32[256,256]{1,0:T(8,128)S(1)} %pad_maximum_fusion.4), channel_id=1, source_target_pairs={{0,1},{1,0},{2,3},{3,2},{4,6},{5,7},{6,4},{7,5},{8,9},{9,8},{10,11... | collective-permute-start | bytes 786440 | tf_op jit(solution)/shard_map/ppermute | solution.py:145
  23.8 1.7 %collective-permute-start.11 = (f32[128,512]{1,0:T(8,128)S(1)}, f32[128,512]{1,0:T(8,128)S(1)}, u32[]{:S(2)}, u32[]{:S(2)}) collective-permute-start(f32[128,512]{1,0:T(8,128)S(1)} %slice_add_fusion), channel_id=1, source_target_pairs={{8,24},{12,28},{16,0},{20,4},{0,8},{4,12},{24,16},{28,20},{9,25},{... | collective-permute-start | bytes 786440 | tf_op jit(solution)/shard_map/ppermute | solution.py:66
  25.6 2.5 %collective-permute-done.7 = f32[256,256]{1,0:T(8,128)S(1)} collective-permute-done((f32[256,256]{1,0:T(8,128)S(1)}, f32[256,256]{1,0:T(8,128)S(1)}, u32[]{:S(2)}, u32[]{:S(2)}) %collective-permute-start.7) | collective-permute-done | bytes 262176 | tf_op jit(solution)/shard_map/ppermute | solution.py:145
  28.2 1.6 %collective-permute-start.8 = (f32[128,256]{1,0:T(8,128)S(1)}, f32[128,256]{1,0:T(8,128)S(1)}, u32[]{:S(2)}, u32[]{:S(2)}) collective-permute-start(f32[128,256]{1,0:T(8,128)S(1)} %slice.35), channel_id=1, source_target_pairs={{0,2},{1,3},{2,0},{3,1},{4,5},{5,4},{6,7},{7,6},{8,10},{9,11},{10,... | collective-permute-start | bytes 393224 | tf_op jit(solution)/shard_map/ppermute | solution.py:145
  29.7 1.7 %collective-permute-done.9 = f32[256,256]{1,0:T(8,128)S(1)} collective-permute-done((f32[256,256]{1,0:T(8,128)S(1)}, f32[256,256]{1,0:T(8,128)S(1)}, u32[]{:S(2)}, u32[]{:S(2)}) %collective-permute-start.9) | collective-permute-done | bytes 262176 | tf_op jit(solution)/shard_map/ppermute | solution.py:145
  31.5 1.6 %collective-permute-start.10 = (f32[128,256]{1,0:T(8,128)S(1)}, f32[128,256]{1,0:T(8,128)S(1)}, u32[]{:S(2)}, u32[]{:S(2)}) collective-permute-start(f32[128,256]{1,0:T(8,128)S(1)} %slice.37), channel_id=1, source_target_pairs={{0,2},{1,3},{2,0},{3,1},{4,5},{5,4},{6,7},{7,6},{8,10},{9,11},{10,... | collective-permute-start | bytes 393224 | tf_op jit(solution)/shard_map/ppermute | solution.py:145
  33.2 3.3 %collective-permute-done.10 = f32[128,256]{1,0:T(8,128)S(1)} collective-permute-done((f32[128,256]{1,0:T(8,128)S(1)}, f32[128,256]{1,0:T(8,128)S(1)}, u32[]{:S(2)}, u32[]{:S(2)}) %collective-permute-start.10) | collective-permute-done | bytes 131104 | tf_op jit(solution)/shard_map/ppermute | solution.py:145
  36.5 0.7 %maximum_add_fusion.2 = f32[128,512]{1,0:T(8,128)} fusion(f32[128,512]{1,0:T(8,128)S(1)} %collective-permute-done.11, f32[128,256]{1,0:T(8,128)S(1)} %slice_add_fusion.1, f32[128,256]{1,0:T(8,128)S(1)} %slice_add_fusion.2), kind=kLoop, calls=%fused_computation.16 | loop fusion | flops 131072 | bytes 786432 | tf_op jit(solution)/shard_map/add | solution.py:155
  (33 shorter events, 3.5 us)
Async XLA Ops:
  1.0 9.7 %collective-permute-start.1 = (f32[128,512]{1,0:T(8,128)S(1)}, f32[128,512]{1,0:T(8,128)S(1)}, u32[]{:S(2)}, u32[]{:S(2)}) collective-permute-start(f32[128,512]{1,0:T(8,128)S(1)} %constant_dynamic-slice_fusion), channel_id=1, source_target_pairs={{0,16},{4,20},{24,8},{28,12},{8,0},{12,4},{16,24},{20,28},{1,17},{... | collective-permute-start | bytes 786440 | tf_op jit(solution)/shard_map/ppermute | solution.py:66
  5.1 8.0 %collective-permute-start = (f32[128,512]{1,0:T(8,128)S(1)}, f32[128,512]{1,0:T(8,128)S(1)}, u32[]{:S(2)}, u32[]{:S(2)}) collective-permute-start(f32[128,512]{1,0:T(8,128)S(1)} %constant_dynamic-slice_fusion), channel_id=1, source_target_pairs={{0,4},{4,0},{8,12},{12,8},{16,20},{20,16},{24,28},{28,24},{1,5},{5... | collective-permute-start | bytes 786440 | tf_op jit(solution)/shard_map/ppermute | solution.py:69
  5.1 1.6 %copy-start = (f32[512,1,1024]{2,1,0:T(1,128)S(1)}, f32[512,1,1024]{2,1,0:T(1,128)}, u32[]{:S(2)}) copy-start(f32[512,1,1024]{2,1,0:T(1,128)} %kernel_ref.1) | copy-start | bytes 6291460
  6.7 6.3 %copy-start.1 = (f32[512,512]{1,0:T(8,128)S(1)}, f32[512,512]{1,0:T(8,128)}, u32[]{:S(2)}) copy-start(f32[512,512]{1,0:T(8,128)} %param.2) | copy-start | bytes 3145732
  7.8 9.7 %collective-permute-start.4 = (f32[128,512]{1,0:T(8,128)S(1)}, f32[128,512]{1,0:T(8,128)}, u32[]{:S(2)}, u32[]{:S(2)}) collective-permute-start(f32[128,512]{1,0:T(8,128)S(1)} %constant_dynamic-slice_fusion), channel_id=1, source_target_pairs={{8,16},{12,20},{16,8},{20,12},{9,17},{13,21},{17,9},{21,13},{10,18... | collective-permute-start | bytes 786440 | tf_op jit(solution)/shard_map/ppermute | solution.py:66
  10.6 8.0 %collective-permute-start.5 = (f32[128,512]{1,0:T(8,128)S(1)}, f32[128,512]{1,0:T(8,128)S(1)}, u32[]{:S(2)}, u32[]{:S(2)}) collective-permute-start(f32[128,512]{1,0:T(8,128)S(1)} %collective-permute-done.1), channel_id=1, source_target_pairs={{0,8},{4,12},{8,0},{12,4},{16,24},{20,28},{24,16},{28,20},{1,9},{5... | collective-permute-start | bytes 786440 | tf_op jit(solution)/shard_map/ppermute | solution.py:66
  13.0 1.5 %collective-permute-start.2 = (f32[128,512]{1,0:T(8,128)S(1)}, f32[128,512]{1,0:T(8,128)S(1)}, u32[]{:S(2)}, u32[]{:S(2)}) collective-permute-start(f32[128,512]{1,0:T(8,128)S(1)} %collective-permute-done.1), channel_id=1, source_target_pairs={{0,4},{4,0},{8,12},{12,8},{16,20},{20,16},{24,28},{28,24},{1,5},{5... | collective-permute-start | bytes 786440 | tf_op jit(solution)/shard_map/ppermute | solution.py:69
  15.9 1.6 %collective-permute-start.3 = (f32[128,512]{1,0:T(8,128)S(1)}, f32[128,512]{1,0:T(8,128)S(1)}, u32[]{:S(2)}, u32[]{:S(2)}) collective-permute-start(f32[128,512]{1,0:T(8,128)S(1)} %slice.33), channel_id=1, source_target_pairs={{0,4},{4,0},{8,12},{12,8},{16,20},{20,16},{24,28},{28,24},{1,5},{5... | collective-permute-start | bytes 786440 | tf_op jit(solution)/shard_map/ppermute | solution.py:69
  18.7 1.6 %collective-permute-start.6 = (f32[128,512]{1,0:T(8,128)S(1)}, f32[128,512]{1,0:T(8,128)S(1)}, u32[]{:S(2)}, u32[]{:S(2)}) collective-permute-start(f32[128,512]{1,0:T(8,128)S(1)} %broadcast_select_fusion), channel_id=1, source_target_pairs={{0,4},{4,0},{8,12},{12,8},{16,20},{20,16},{24,28},{28,24},{1,5},{5... | collective-permute-start | bytes 786440 | tf_op jit(solution)/shard_map/ppermute | solution.py:69
  21.7 6.4 %collective-permute-start.7 = (f32[256,256]{1,0:T(8,128)S(1)}, f32[256,256]{1,0:T(8,128)S(1)}, u32[]{:S(2)}, u32[]{:S(2)}) collective-permute-start(f32[256,256]{1,0:T(8,128)S(1)} %pad_maximum_fusion.3), channel_id=1, source_target_pairs={{0,1},{1,0},{2,3},{3,2},{4,6},{5,7},{6,4},{7,5},{8,9},{9,8},{10,11... | collective-permute-start | bytes 786440 | tf_op jit(solution)/shard_map/ppermute | solution.py:145
  23.2 8.2 %collective-permute-start.9 = (f32[256,256]{1,0:T(8,128)S(1)}, f32[256,256]{1,0:T(8,128)S(1)}, u32[]{:S(2)}, u32[]{:S(2)}) collective-permute-start(f32[256,256]{1,0:T(8,128)S(1)} %pad_maximum_fusion.4), channel_id=1, source_target_pairs={{0,1},{1,0},{2,3},{3,2},{4,6},{5,7},{6,4},{7,5},{8,9},{9,8},{10,11... | collective-permute-start | bytes 786440 | tf_op jit(solution)/shard_map/ppermute | solution.py:145
  23.8 12.7 %collective-permute-start.11 = (f32[128,512]{1,0:T(8,128)S(1)}, f32[128,512]{1,0:T(8,128)S(1)}, u32[]{:S(2)}, u32[]{:S(2)}) collective-permute-start(f32[128,512]{1,0:T(8,128)S(1)} %slice_add_fusion), channel_id=1, source_target_pairs={{8,24},{12,28},{16,0},{20,4},{0,8},{4,12},{24,16},{28,20},{9,25},{... | collective-permute-start | bytes 786440 | tf_op jit(solution)/shard_map/ppermute | solution.py:66
  28.2 5.0 %collective-permute-start.8 = (f32[128,256]{1,0:T(8,128)S(1)}, f32[128,256]{1,0:T(8,128)S(1)}, u32[]{:S(2)}, u32[]{:S(2)}) collective-permute-start(f32[128,256]{1,0:T(8,128)S(1)} %slice.35), channel_id=1, source_target_pairs={{0,2},{1,3},{2,0},{3,1},{4,5},{5,4},{6,7},{7,6},{8,10},{9,11},{10,... | collective-permute-start | bytes 393224 | tf_op jit(solution)/shard_map/ppermute | solution.py:145
  31.5 5.0 %collective-permute-start.10 = (f32[128,256]{1,0:T(8,128)S(1)}, f32[128,256]{1,0:T(8,128)S(1)}, u32[]{:S(2)}, u32[]{:S(2)}) collective-permute-start(f32[128,256]{1,0:T(8,128)S(1)} %slice.37), channel_id=1, source_target_pairs={{0,2},{1,3},{2,0},{3,1},{4,5},{5,4},{6,7},{7,6},{8,10},{9,11},{10,... | collective-permute-start | bytes 393224 | tf_op jit(solution)/shard_map/ppermute | solution.py:145

commit v9 on v7

--- a/solution.py
+++ b/solution.py
@@ -126,7 +126,7 @@
         jnp.concatenate([high, high, low], axis=0),
         ((1,), (0,)),
     )
-    total, last, back = lax.optimization_barrier((total, last, back))
+    total, last = lax.optimization_barrier((total, last))
     returned = along(
         back, [(c, c ^ half) for c in inner_chips] + [(c, c ^ near) for c in outer_chips]
     )

time: 37.4 us -> 37.4 us (level)
  no operation moved by 1% of the time
where the time goes in v9:
time: 37.4 us; the launch traced here: 37.2 us
  starting transfers between devices  15.3 us (41%)
  waiting for transfers between devices  11.3 us (30%)
  matrix products  5.25 us (14%)
  local copies, waits for them, and re-layouts  2.72 us (7%)
  other arithmetic  1.41 us (4%)
  Pallas kernels  1.06 us (3%)
    ppermute x4, starting transfers between devices, along(): return lax.ppermute(value, 'blk', full)  9.55 us
    ppermute x4, waiting for transfers between devices, exchange(): return lax.ppermute(send, ('blk', 'split'), pairs)  7.62 us
    ppermute x4, starting transfers between devices, exchange(): return lax.ppermute(send, ('blk', 'split'), pairs)  5.32 us
    dot_general x8, matrix products, product(): lax.dot_general(a, b, (dims, ((), ())), precision=lax.Precision.HIGH, pre...  4.83 us
    ppermute x4, waiting for transfers between devices, along(): return lax.ppermute(value, 'blk', full)  2.55 us
    unnamed x5, local copies, waits for them, and re-layouts  1.61 us
    ppermute x4, waiting for transfers between devices, other_core(): lax.ppermute(value, 'blk', [(i, i ^ 1) for i in range(nchips * CORES)])  1.08 us
    pallas_call x1, Pallas kernels, pick_columns(): pl.pallas_call(pick_body, in_specs=[pl.BlockSpec(memory_space=pltpu.SMEM)...  1.06 us
  transfers between devices with their start and end apart: 12, of which 9 were waited for; matrix products, arithmetic and copies ran while one was open for 13% of the time, Pallas kernels for 3%

profile of v9, /device:TPU:0, one launch (start us, length us, event | category | flops | bytes accessed | tf_op | source)
XLA Modules:
  0.0 37.2 jit_solution(6222908991945824596)
XLA Ops:
  0.0 1.0 %constant_dynamic-slice_fusion = f32[128,512]{1,0:T(8,128)S(1)} fusion(f32[512,512]{1,0:T(8,128)} %param.2, s32[]{:T(128)S(6)} %select_n.78), kind=kLoop, calls=%fused_computation.48 | loop fusion | bytes 524292 | tf_op jit(solution)/shard_map/dynamic_slice | solution.py:80
  1.0 4.1 %collective-permute-start.1 = (f32[128,512]{1,0:T(8,128)S(1)}, f32[128,512]{1,0:T(8,128)S(1)}, u32[]{:S(2)}, u32[]{:S(2)}) collective-permute-start(f32[128,512]{1,0:T(8,128)S(1)} %constant_dynamic-slice_fusion), channel_id=1, source_target_pairs={{0,16},{4,20},{24,8},{28,12},{8,0},{12,4},{16,24},{20,28},{1,17},{... | collective-permute-start | bytes 786440 | tf_op jit(solution)/shard_map/ppermute | solution.py:75
  5.1 1.6 %copy-done = f32[512,1,1024]{2,1,0:T(1,128)S(1)} copy-done((f32[512,1,1024]{2,1,0:T(1,128)S(1)}, f32[512,1,1024]{2,1,0:T(1,128)}, u32[]{:S(2)}) %copy-start) | copy-done | bytes 2097176
  6.7 1.1 %shard_map.28 = (f32[512,256]{1,0:T(8,128)S(1)}, f32[512,256]{1,0:T(8,128)S(1)}, f32[512,256]{1,0:T(8,128)S(1)}) custom-call(s32[6]{0:T(128)S(1)} %stack.27.at_ref, f32[512,1,1024]{2,1,0:T(1,128)S(1)} %copy-done), custom_call_target="tpu_custom_call" | custom-call | bytes 2097152 | tf_op jit(solution)/shard_map/pallas_call | solution.py:43
  7.8 1.4 %collective-permute-start.4 = (f32[128,512]{1,0:T(8,128)S(1)}, f32[128,512]{1,0:T(8,128)}, u32[]{:S(2)}, u32[]{:S(2)}) collective-permute-start(f32[128,512]{1,0:T(8,128)S(1)} %constant_dynamic-slice_fusion), channel_id=1, source_target_pairs={{8,16},{12,20},{16,8},{20,12},{9,17},{13,21},{17,9},{21,13},{10,18... | collective-permute-start | bytes 786440 | tf_op jit(solution)/shard_map/ppermute | solution.py:75
  9.2 1.5 %collective-permute-done.1 = f32[128,512]{1,0:T(8,128)S(1)} collective-permute-done((f32[128,512]{1,0:T(8,128)S(1)}, f32[128,512]{1,0:T(8,128)S(1)}, u32[]{:S(2)}, u32[]{:S(2)}) %collective-permute-start.1) | collective-permute-done | bytes 262176 | tf_op jit(solution)/shard_map/ppermute | solution.py:75
  10.6 2.4 %collective-permute-start.5 = (f32[128,512]{1,0:T(8,128)S(1)}, f32[128,512]{1,0:T(8,128)S(1)}, u32[]{:S(2)}, u32[]{:S(2)}) collective-permute-start(f32[128,512]{1,0:T(8,128)S(1)} %collective-permute-done.1), channel_id=1, source_target_pairs={{0,8},{4,12},{8,0},{12,4},{16,24},{20,28},{24,16},{28,20},{1,9},{5... | collective-permute-start | bytes 786440 | tf_op jit(solution)/shard_map/ppermute | solution.py:75
  13.0 0.6 %fusion.1 = f32[512,256]{1,0:T(8,128)S(1)} fusion(f32[512,256]{1,0:T(8,128)S(1)} %get-tuple-element.23, f32[512,512]{1,0:T(8,128)S(1)} %copy-done.1, f32[128,512]{1,0:T(8,128)S(1)} %collective-permute-done, f32[128,512]{1,0:T(8,128)S(1)} %constant_dynamic-slice_fusion), kind=kOutput, calls=%fused_computation.4 | convolution fusion | flops 402915328 | bytes 2621440 | tf_op jit(solution)/shard_map/dot_general | solution.py:15
  13.7 0.6 %fusion.4 = f32[512,512]{1,0:T(8,128)S(1)} fusion(f32[512,256]{1,0:T(8,128)S(1)} %fusion.1, f32[128,512]{1,0:T(8,128)S(1)} %collective-permute-done, f32[128,512]{1,0:T(8,128)S(1)} %constant_dynamic-slice_fusion), kind=kOutput, calls=%fused_computation.10 | convolution fusion | flops 402784256 | bytes 2097152 | tf_op jit(solution)/shard_map/dot_general | solution.py:15
  14.6 0.6 %fusion = f32[512,256]{1,0:T(8,128)S(1)} fusion(f32[512,256]{1,0:T(8,128)S(1)} %get-tuple-element.26, f32[256,512]{1,0:T(8,128)S(1)} %constant_dynamic-update-slice_fusion, f32[512,512]{1,0:T(8,128)S(1)} %copy-done.1), kind=kOutput, calls=%fused_computation.2 | convolution fusion | flops 402784256 | bytes 2621440 | tf_op jit(solution)/shard_map/dot_general | solution.py:15
  15.2 0.7 %fusion.21 = f32[256,512]{1,0:T(8,128)S(1)} fusion(f32[512,256]{1,0:T(8,128)S(1)} %fusion, f32[512,512]{1,0:T(8,128)S(1)} %copy-done.1), kind=kOutput, calls=%fused_computation.52 | convolution fusion | flops 402653184 | bytes 2097152 | tf_op jit(solution)/shard_map/dot_general | solution.py:15
  16.2 0.6 %convolution_add_fusion = f32[512,512]{1,0:T(8,128)S(1)} fusion(f32[512,512]{1,0:T(8,128)S(1)} %fusion.4, f32[512,256]{1,0:T(8,128)S(1)} %fusion, f32[256,512]{1,0:T(8,128)S(1)} %constant_dynamic-update-slice_fusion), kind=kOutput, calls=%fused_computation | convolution fusion | flops 402915328 | bytes 3145728 | tf_op jit(solution)/shard_map/dot_general | solution.py:15
  16.8 0.7 %collective-permute-done.3 = f32[128,512]{1,0:T(8,128)S(1)} collective-permute-done((f32[128,512]{1,0:T(8,128)S(1)}, f32[128,512]{1,0:T(8,128)S(1)}, u32[]{:S(2)}, u32[]{:S(2)}) %collective-permute-start.3) | collective-permute-done | bytes 262176 | tf_op jit(solution)/shard_map/ppermute | solution.py:78
  17.6 1.1 %collective-permute-done.5 = f32[128,512]{1,0:T(8,128)S(1)} collective-permute-done((f32[128,512]{1,0:T(8,128)S(1)}, f32[128,512]{1,0:T(8,128)S(1)}, u32[]{:S(2)}, u32[]{:S(2)}) %collective-permute-start.5) | collective-permute-done | bytes 262176 | tf_op jit(solution)/shard_map/ppermute | solution.py:75
  20.3 0.6 %fusion.16 = (bf16[512,128]{1,0:T(8,128)(2,1)S(1)}, bf16[512,128]{1,0:T(8,128)(2,1)S(1)}) fusion(f32[128,512]{1,0:T(8,128)S(1)} %collective-permute-done.6, f32[512,512]{1,0:T(8,128)S(1)} %copy-done.1, f32[512,256]{1,0:T(8,128)S(1)} %get-tuple-element.32), kind=kOutput, calls=%fused_computation.26 | convolution fusion | flops 201654272 | bytes 1835008 | tf_op jit(solution)/shard_map/dot_general | solution.py:15
  21.6 1.6 %collective-permute-start.7 = (f32[256,256]{1,0:T(8,128)S(1)}, f32[256,256]{1,0:T(8,128)S(1)}, u32[]{:S(2)}, u32[]{:S(2)}) collective-permute-start(f32[256,256]{1,0:T(8,128)S(1)} %pad_maximum_fusion.3), channel_id=1, source_target_pairs={{0,1},{1,0},{2,3},{3,2},{4,6},{5,7},{6,4},{7,5},{8,9},{9,8},{10,11... | collective-permute-start | bytes 786440 | tf_op jit(solution)/shard_map/ppermute | solution.py:160
  23.1 0.6 %collective-permute-start.9 = (f32[256,256]{1,0:T(8,128)S(1)}, f32[256,256]{1,0:T(8,128)S(1)}, u32[]{:S(2)}, u32[]{:S(2)}) collective-permute-start(f32[256,256]{1,0:T(8,128)S(1)} %pad_maximum_fusion.4), channel_id=1, source_target_pairs={{0,1},{1,0},{2,3},{3,2},{4,6},{5,7},{6,4},{7,5},{8,9},{9,8},{10,11... | collective-permute-start | bytes 786440 | tf_op jit(solution)/shard_map/ppermute | solution.py:160
  23.7 1.7 %collective-permute-start.11 = (f32[128,512]{1,0:T(8,128)S(1)}, f32[128,512]{1,0:T(8,128)S(1)}, u32[]{:S(2)}, u32[]{:S(2)}) collective-permute-start(f32[128,512]{1,0:T(8,128)S(1)} %slice_add_fusion), channel_id=1, source_target_pairs={{8,24},{12,28},{16,0},{20,4},{0,8},{4,12},{24,16},{28,20},{9,25},{... | collective-permute-start | bytes 786440 | tf_op jit(solution)/shard_map/ppermute | solution.py:75
  25.5 2.5 %collective-permute-done.7 = f32[256,256]{1,0:T(8,128)S(1)} collective-permute-done((f32[256,256]{1,0:T(8,128)S(1)}, f32[256,256]{1,0:T(8,128)S(1)}, u32[]{:S(2)}, u32[]{:S(2)}) %collective-permute-start.7) | collective-permute-done | bytes 262176 | tf_op jit(solution)/shard_map/ppermute | solution.py:160
  28.1 1.6 %collective-permute-start.8 = (f32[128,256]{1,0:T(8,128)S(1)}, f32[128,256]{1,0:T(8,128)S(1)}, u32[]{:S(2)}, u32[]{:S(2)}) collective-permute-start(f32[128,256]{1,0:T(8,128)S(1)} %slice.35), channel_id=1, source_target_pairs={{0,2},{1,3},{2,0},{3,1},{4,5},{5,4},{6,7},{7,6},{8,10},{9,11},{10,... | collective-permute-start | bytes 393224 | tf_op jit(solution)/shard_map/ppermute | solution.py:160
  29.6 1.7 %collective-permute-done.9 = f32[256,256]{1,0:T(8,128)S(1)} collective-permute-done((f32[256,256]{1,0:T(8,128)S(1)}, f32[256,256]{1,0:T(8,128)S(1)}, u32[]{:S(2)}, u32[]{:S(2)}) %collective-permute-start.9) | collective-permute-done | bytes 262176 | tf_op jit(solution)/shard_map/ppermute | solution.py:160
  31.4 1.6 %collective-permute-start.10 = (f32[128,256]{1,0:T(8,128)S(1)}, f32[128,256]{1,0:T(8,128)S(1)}, u32[]{:S(2)}, u32[]{:S(2)}) collective-permute-start(f32[128,256]{1,0:T(8,128)S(1)} %slice.37), channel_id=1, source_target_pairs={{0,2},{1,3},{2,0},{3,1},{4,5},{5,4},{6,7},{7,6},{8,10},{9,11},{10,... | collective-permute-start | bytes 393224 | tf_op jit(solution)/shard_map/ppermute | solution.py:160
  33.1 3.3 %collective-permute-done.10 = f32[128,256]{1,0:T(8,128)S(1)} collective-permute-done((f32[128,256]{1,0:T(8,128)S(1)}, f32[128,256]{1,0:T(8,128)S(1)}, u32[]{:S(2)}, u32[]{:S(2)}) %collective-permute-start.10) | collective-permute-done | bytes 131104 | tf_op jit(solution)/shard_map/ppermute | solution.py:160
  36.4 0.7 %maximum_add_fusion.2 = f32[128,512]{1,0:T(8,128)} fusion(f32[128,512]{1,0:T(8,128)S(1)} %collective-permute-done.11, f32[128,256]{1,0:T(8,128)S(1)} %slice_add_fusion.1, f32[128,256]{1,0:T(8,128)S(1)} %slice_add_fusion.2), kind=kLoop, calls=%fused_computation.33 | loop fusion | flops 131072 | bytes 786432 | tf_op jit(solution)/shard_map/add | solution.py:170
  (34 shorter events, 3.4 us)
Async XLA Ops:
  1.0 9.7 %collective-permute-start.1 = (f32[128,512]{1,0:T(8,128)S(1)}, f32[128,512]{1,0:T(8,128)S(1)}, u32[]{:S(2)}, u32[]{:S(2)}) collective-permute-start(f32[128,512]{1,0:T(8,128)S(1)} %constant_dynamic-slice_fusion), channel_id=1, source_target_pairs={{0,16},{4,20},{24,8},{28,12},{8,0},{12,4},{16,24},{20,28},{1,17},{... | collective-permute-start | bytes 786440 | tf_op jit(solution)/shard_map/ppermute | solution.py:75
  5.1 8.0 %collective-permute-start = (f32[128,512]{1,0:T(8,128)S(1)}, f32[128,512]{1,0:T(8,128)S(1)}, u32[]{:S(2)}, u32[]{:S(2)}) collective-permute-start(f32[128,512]{1,0:T(8,128)S(1)} %constant_dynamic-slice_fusion), channel_id=1, source_target_pairs={{0,4},{4,0},{8,12},{12,8},{16,20},{20,16},{24,28},{28,24},{1,5},{5... | collective-permute-start | bytes 786440 | tf_op jit(solution)/shard_map/ppermute | solution.py:78
  5.1 1.6 %copy-start = (f32[512,1,1024]{2,1,0:T(1,128)S(1)}, f32[512,1,1024]{2,1,0:T(1,128)}, u32[]{:S(2)}) copy-start(f32[512,1,1024]{2,1,0:T(1,128)} %kernel_ref.1) | copy-start | bytes 6291460
  6.7 6.3 %copy-start.1 = (f32[512,512]{1,0:T(8,128)S(1)}, f32[512,512]{1,0:T(8,128)}, u32[]{:S(2)}) copy-start(f32[512,512]{1,0:T(8,128)} %param.2) | copy-start | bytes 3145732
  7.8 9.7 %collective-permute-start.4 = (f32[128,512]{1,0:T(8,128)S(1)}, f32[128,512]{1,0:T(8,128)}, u32[]{:S(2)}, u32[]{:S(2)}) collective-permute-start(f32[128,512]{1,0:T(8,128)S(1)} %constant_dynamic-slice_fusion), channel_id=1, source_target_pairs={{8,16},{12,20},{16,8},{20,12},{9,17},{13,21},{17,9},{21,13},{10,18... | collective-permute-start | bytes 786440 | tf_op jit(solution)/shard_map/ppermute | solution.py:75
  10.6 8.0 %collective-permute-start.5 = (f32[128,512]{1,0:T(8,128)S(1)}, f32[128,512]{1,0:T(8,128)S(1)}, u32[]{:S(2)}, u32[]{:S(2)}) collective-permute-start(f32[128,512]{1,0:T(8,128)S(1)} %collective-permute-done.1), channel_id=1, source_target_pairs={{0,8},{4,12},{8,0},{12,4},{16,24},{20,28},{24,16},{28,20},{1,9},{5... | collective-permute-start | bytes 786440 | tf_op jit(solution)/shard_map/ppermute | solution.py:75
  13.0 1.5 %collective-permute-start.2 = (f32[128,512]{1,0:T(8,128)S(1)}, f32[128,512]{1,0:T(8,128)S(1)}, u32[]{:S(2)}, u32[]{:S(2)}) collective-permute-start(f32[128,512]{1,0:T(8,128)S(1)} %collective-permute-done.1), channel_id=1, source_target_pairs={{0,4},{4,0},{8,12},{12,8},{16,20},{20,16},{24,28},{28,24},{1,5},{5... | collective-permute-start | bytes 786440 | tf_op jit(solution)/shard_map/ppermute | solution.py:78
  15.9 1.6 %collective-permute-start.3 = (f32[128,512]{1,0:T(8,128)S(1)}, f32[128,512]{1,0:T(8,128)S(1)}, u32[]{:S(2)}, u32[]{:S(2)}) collective-permute-start(f32[128,512]{1,0:T(8,128)S(1)} %slice.33), channel_id=1, source_target_pairs={{0,4},{4,0},{8,12},{12,8},{16,20},{20,16},{24,28},{28,24},{1,5},{5... | collective-permute-start | bytes 786440 | tf_op jit(solution)/shard_map/ppermute | solution.py:78
  18.7 1.6 %collective-permute-start.6 = (f32[128,512]{1,0:T(8,128)S(1)}, f32[128,512]{1,0:T(8,128)S(1)}, u32[]{:S(2)}, u32[]{:S(2)}) collective-permute-start(f32[128,512]{1,0:T(8,128)S(1)} %broadcast_select_fusion), channel_id=1, source_target_pairs={{0,4},{4,0},{8,12},{12,8},{16,20},{20,16},{24,28},{28,24},{1,5},{5... | collective-permute-start | bytes 786440 | tf_op jit(solution)/shard_map/ppermute | solution.py:78
  21.6 6.4 %collective-permute-start.7 = (f32[256,256]{1,0:T(8,128)S(1)}, f32[256,256]{1,0:T(8,128)S(1)}, u32[]{:S(2)}, u32[]{:S(2)}) collective-permute-start(f32[256,256]{1,0:T(8,128)S(1)} %pad_maximum_fusion.3), channel_id=1, source_target_pairs={{0,1},{1,0},{2,3},{3,2},{4,6},{5,7},{6,4},{7,5},{8,9},{9,8},{10,11... | collective-permute-start | bytes 786440 | tf_op jit(solution)/shard_map/ppermute | solution.py:160
  23.1 8.2 %collective-permute-start.9 = (f32[256,256]{1,0:T(8,128)S(1)}, f32[256,256]{1,0:T(8,128)S(1)}, u32[]{:S(2)}, u32[]{:S(2)}) collective-permute-start(f32[256,256]{1,0:T(8,128)S(1)} %pad_maximum_fusion.4), channel_id=1, source_target_pairs={{0,1},{1,0},{2,3},{3,2},{4,6},{5,7},{6,4},{7,5},{8,9},{9,8},{10,11... | collective-permute-start | bytes 786440 | tf_op jit(solution)/shard_map/ppermute | solution.py:160
  23.7 12.7 %collective-permute-start.11 = (f32[128,512]{1,0:T(8,128)S(1)}, f32[128,512]{1,0:T(8,128)S(1)}, u32[]{:S(2)}, u32[]{:S(2)}) collective-permute-start(f32[128,512]{1,0:T(8,128)S(1)} %slice_add_fusion), channel_id=1, source_target_pairs={{8,24},{12,28},{16,0},{20,4},{0,8},{4,12},{24,16},{28,20},{9,25},{... | collective-permute-start | bytes 786440 | tf_op jit(solution)/shard_map/ppermute | solution.py:75
  28.1 5.0 %collective-permute-start.8 = (f32[128,256]{1,0:T(8,128)S(1)}, f32[128,256]{1,0:T(8,128)S(1)}, u32[]{:S(2)}, u32[]{:S(2)}) collective-permute-start(f32[128,256]{1,0:T(8,128)S(1)} %slice.35), channel_id=1, source_target_pairs={{0,2},{1,3},{2,0},{3,1},{4,5},{5,4},{6,7},{7,6},{8,10},{9,11},{10,... | collective-permute-start | bytes 393224 | tf_op jit(solution)/shard_map/ppermute | solution.py:160
  31.4 5.0 %collective-permute-start.10 = (f32[128,256]{1,0:T(8,128)S(1)}, f32[128,256]{1,0:T(8,128)S(1)}, u32[]{:S(2)}, u32[]{:S(2)}) collective-permute-start(f32[128,256]{1,0:T(8,128)S(1)} %slice.37), channel_id=1, source_target_pairs={{0,2},{1,3},{2,0},{3,1},{4,5},{5,4},{6,7},{7,6},{8,10},{9,11},{10,... | collective-permute-start | bytes 393224 | tf_op jit(solution)/shard_map/ppermute | solution.py:160

commit v10 on v8

--- a/solution.py
+++ b/solution.py
@@ -111,7 +111,7 @@
     total += rows_of(weighted(z_last[:, :share], held), held)
     total, pair_held = lax.optimization_barrier((total, pair_held))
     last = rows_of(weighted(z_last[:, share:], pair_held), pair_held)
-    total, last = lax.optimization_barrier((total, last))
+    total, last, back = lax.optimization_barrier((total, last, back))
     returned = along(
         back, [(c, c ^ half) for c in inner_chips] + [(c, c ^ near) for c in outer_chips]
     )
@@ -119,7 +119,7 @@
     bits = nshares.bit_length() - 1
 
     def bit_at(step, on_core):
-        return (step + on_core * (bits // 2)) % bits
+        return (step + (1 - on_core) * (bits // 2)) % bits
 
     def share_mask(place, on_core):
         return sum(((place >> (bits - 1 - t)) & 1) << bit_at(t, on_core) for t in range(bits))

time: 37.5 us -> 37.5 us (level)
  no operation moved by 1% of the time
where the time goes in v10:
time: 37.5 us; the launch traced here: 37.3 us
  starting transfers between devices  15.2 us (41%)
  waiting for transfers between devices  11.3 us (30%)
  matrix products  5.39 us (14%)
  local copies, waits for them, and re-layouts  2.72 us (7%)
  other arithmetic  1.37 us (4%)
  Pallas kernels  1.06 us (3%)
    ppermute x4, starting transfers between devices, along(): return lax.ppermute(value, 'blk', full)  9.56 us
    ppermute x4, waiting for transfers between devices, exchange(): return lax.ppermute(send, ('blk', 'split'), pairs)  7.7 us
    dot_general x9, matrix products, product(): lax.dot_general(a, b, (dims, ((), ())), precision=lax.Precision.HIGH, pre...  5.39 us
    ppermute x4, starting transfers between devices, exchange(): return lax.ppermute(send, ('blk', 'split'), pairs)  5.25 us
    ppermute x4, waiting for transfers between devices, along(): return lax.ppermute(value, 'blk', full)  2.54 us
    unnamed x5, local copies, waits for them, and re-layouts  1.61 us
    ppermute x4, waiting for transfers between devices, other_core(): lax.ppermute(value, 'blk', [(i, i ^ 1) for i in range(nchips * CORES)])  1.08 us
    pallas_call x1, Pallas kernels, pick_columns(): pl.pallas_call(pick_body, in_specs=[pl.BlockSpec(memory_space=pltpu.SMEM)...  1.06 us
  transfers between devices with their start and end apart: 12, of which 9 were waited for; matrix products, arithmetic and copies ran while one was open for 13% of the time, Pallas kernels for 3%

profile of v10, /device:TPU:0, one launch (start us, length us, event | category | flops | bytes accessed | tf_op | source)
XLA Modules:
  0.0 37.3 jit_solution(10580211360040240624)
XLA Ops:
  0.0 1.0 %constant_dynamic-slice_fusion = f32[128,512]{1,0:T(8,128)S(1)} fusion(f32[512,512]{1,0:T(8,128)} %param.2, s32[]{:T(128)S(6)} %select_n.78), kind=kLoop, calls=%fused_computation.31 | loop fusion | bytes 524292 | tf_op jit(solution)/shard_map/dynamic_slice | solution.py:71
  1.0 4.1 %collective-permute-start.1 = (f32[128,512]{1,0:T(8,128)S(1)}, f32[128,512]{1,0:T(8,128)S(1)}, u32[]{:S(2)}, u32[]{:S(2)}) collective-permute-start(f32[128,512]{1,0:T(8,128)S(1)} %constant_dynamic-slice_fusion), channel_id=1, source_target_pairs={{0,16},{4,20},{24,8},{28,12},{8,0},{12,4},{16,24},{20,28},{1,17},{... | collective-permute-start | bytes 786440 | tf_op jit(solution)/shard_map/ppermute | solution.py:66
  5.1 1.6 %copy-done = f32[512,1,1024]{2,1,0:T(1,128)S(1)} copy-done((f32[512,1,1024]{2,1,0:T(1,128)S(1)}, f32[512,1,1024]{2,1,0:T(1,128)}, u32[]{:S(2)}) %copy-start) | copy-done | bytes 2097176
  6.7 1.1 %shard_map.28 = (f32[512,256]{1,0:T(8,128)S(1)}, f32[512,256]{1,0:T(8,128)S(1)}, f32[512,256]{1,0:T(8,128)S(1)}) custom-call(s32[6]{0:T(128)S(1)} %stack.27.at_ref, f32[512,1,1024]{2,1,0:T(1,128)S(1)} %copy-done), custom_call_target="tpu_custom_call" | custom-call | bytes 2097152 | tf_op jit(solution)/shard_map/pallas_call | solution.py:34
  7.8 1.4 %collective-permute-start.4 = (f32[128,512]{1,0:T(8,128)S(1)}, f32[128,512]{1,0:T(8,128)}, u32[]{:S(2)}, u32[]{:S(2)}) collective-permute-start(f32[128,512]{1,0:T(8,128)S(1)} %constant_dynamic-slice_fusion), channel_id=1, source_target_pairs={{8,16},{12,20},{16,8},{20,12},{9,17},{13,21},{17,9},{21,13},{10,18... | collective-permute-start | bytes 786440 | tf_op jit(solution)/shard_map/ppermute | solution.py:66
  9.2 1.4 %collective-permute-done.1 = f32[128,512]{1,0:T(8,128)S(1)} collective-permute-done((f32[128,512]{1,0:T(8,128)S(1)}, f32[128,512]{1,0:T(8,128)S(1)}, u32[]{:S(2)}, u32[]{:S(2)}) %collective-permute-start.1) | collective-permute-done | bytes 262176 | tf_op jit(solution)/shard_map/ppermute | solution.py:66
  10.6 2.4 %collective-permute-start.5 = (f32[128,512]{1,0:T(8,128)S(1)}, f32[128,512]{1,0:T(8,128)S(1)}, u32[]{:S(2)}, u32[]{:S(2)}) collective-permute-start(f32[128,512]{1,0:T(8,128)S(1)} %collective-permute-done.1), channel_id=1, source_target_pairs={{0,8},{4,12},{8,0},{12,4},{16,24},{20,28},{24,16},{28,20},{1,9},{5... | collective-permute-start | bytes 786440 | tf_op jit(solution)/shard_map/ppermute | solution.py:66
  13.0 0.6 %fusion.1 = f32[512,256]{1,0:T(8,128)S(1)} fusion(f32[512,256]{1,0:T(8,128)S(1)} %get-tuple-element.24, f32[512,512]{1,0:T(8,128)S(1)} %copy-done.1, f32[128,512]{1,0:T(8,128)S(1)} %collective-permute-done, f32[128,512]{1,0:T(8,128)S(1)} %constant_dynamic-slice_fusion), kind=kOutput, calls=%fused_computation.4 | convolution fusion | flops 402915328 | bytes 2621440 | tf_op jit(solution)/shard_map/dot_general | solution.py:15
  13.7 0.6 %fusion.4 = f32[512,512]{1,0:T(8,128)S(1)} fusion(f32[512,256]{1,0:T(8,128)S(1)} %fusion.1, f32[128,512]{1,0:T(8,128)S(1)} %collective-permute-done, f32[128,512]{1,0:T(8,128)S(1)} %constant_dynamic-slice_fusion), kind=kOutput, calls=%fused_computation.10 | convolution fusion | flops 402784256 | bytes 2097152 | tf_op jit(solution)/shard_map/dot_general | solution.py:15
  14.6 0.6 %fusion = f32[512,256]{1,0:T(8,128)S(1)} fusion(f32[512,256]{1,0:T(8,128)S(1)} %get-tuple-element.27, f32[256,512]{1,0:T(8,128)S(1)} %constant_dynamic-update-slice_fusion, f32[512,512]{1,0:T(8,128)S(1)} %copy-done.1), kind=kOutput, calls=%fused_computation.2 | convolution fusion | flops 402784256 | bytes 2621440 | tf_op jit(solution)/shard_map/dot_general | solution.py:15
  15.2 0.7 %fusion.7 = f32[256,512]{1,0:T(8,128)S(1)} fusion(f32[512,256]{1,0:T(8,128)S(1)} %fusion, f32[512,512]{1,0:T(8,128)S(1)} %copy-done.1), kind=kOutput, calls=%fused_computation.34 | convolution fusion | flops 402653184 | bytes 2097152 | tf_op jit(solution)/shard_map/dot_general | solution.py:15
  16.2 0.6 %convolution_add_fusion = f32[512,512]{1,0:T(8,128)S(1)} fusion(f32[512,512]{1,0:T(8,128)S(1)} %fusion.4, f32[512,256]{1,0:T(8,128)S(1)} %fusion, f32[256,512]{1,0:T(8,128)S(1)} %constant_dynamic-update-slice_fusion), kind=kOutput, calls=%fused_computation | convolution fusion | flops 402915328 | bytes 3145728 | tf_op jit(solution)/shard_map/dot_general | solution.py:15
  16.8 0.7 %collective-permute-done.3 = f32[128,512]{1,0:T(8,128)S(1)} collective-permute-done((f32[128,512]{1,0:T(8,128)S(1)}, f32[128,512]{1,0:T(8,128)S(1)}, u32[]{:S(2)}, u32[]{:S(2)}) %collective-permute-start.3) | collective-permute-done | bytes 262176 | tf_op jit(solution)/shard_map/ppermute | solution.py:69
  17.6 1.1 %collective-permute-done.5 = f32[128,512]{1,0:T(8,128)S(1)} collective-permute-done((f32[128,512]{1,0:T(8,128)S(1)}, f32[128,512]{1,0:T(8,128)S(1)}, u32[]{:S(2)}, u32[]{:S(2)}) %collective-permute-start.5) | collective-permute-done | bytes 262176 | tf_op jit(solution)/shard_map/ppermute | solution.py:66
  18.8 0.6 %fusion.2 = f32[512,128]{1,0:T(8,128)S(1)} fusion(f32[128,512]{1,0:T(8,128)S(1)} %broadcast_select_fusion, f32[512,512]{1,0:T(8,128)S(1)} %copy-done.1, f32[512,256]{1,0:T(8,128)S(1)} %get-tuple-element.33), kind=kOutput, calls=%fused_computation.7 | convolution fusion | flops 201392128 | bytes 1835008 | tf_op jit(solution)/shard_map/dot_general | solution.py:15
  20.3 0.6 %fusion.3 = f32[512,128]{1,0:T(8,128)S(1)} fusion(f32[128,512]{1,0:T(8,128)S(1)} %collective-permute-done.6, f32[512,512]{1,0:T(8,128)S(1)} %copy-done.1, f32[512,256]{1,0:T(8,128)S(1)} %get-tuple-element.33), kind=kOutput, calls=%fused_computation.8 | convolution fusion | flops 201392128 | bytes 1835008 | tf_op jit(solution)/shard_map/dot_general | solution.py:15
  21.7 1.6 %collective-permute-start.7 = (f32[256,256]{1,0:T(8,128)S(1)}, f32[256,256]{1,0:T(8,128)S(1)}, u32[]{:S(2)}, u32[]{:S(2)}) collective-permute-start(f32[256,256]{1,0:T(8,128)S(1)} %pad_maximum_fusion.3), channel_id=1, source_target_pairs={{0,2},{1,3},{2,0},{3,1},{4,5},{5,4},{6,7},{7,6},{8,10},{9,11},{10,... | collective-permute-start | bytes 786440 | tf_op jit(solution)/shard_map/ppermute | solution.py:145
  23.8 1.7 %collective-permute-start.11 = (f32[128,512]{1,0:T(8,128)S(1)}, f32[128,512]{1,0:T(8,128)S(1)}, u32[]{:S(2)}, u32[]{:S(2)}) collective-permute-start(f32[128,512]{1,0:T(8,128)S(1)} %slice_add_fusion), channel_id=1, source_target_pairs={{8,24},{12,28},{16,0},{20,4},{0,8},{4,12},{24,16},{28,20},{9,25},{... | collective-permute-start | bytes 786440 | tf_op jit(solution)/shard_map/ppermute | solution.py:66
  25.6 2.5 %collective-permute-done.7 = f32[256,256]{1,0:T(8,128)S(1)} collective-permute-done((f32[256,256]{1,0:T(8,128)S(1)}, f32[256,256]{1,0:T(8,128)S(1)}, u32[]{:S(2)}, u32[]{:S(2)}) %collective-permute-start.7) | collective-permute-done | bytes 262176 | tf_op jit(solution)/shard_map/ppermute | solution.py:145
  28.2 1.5 %collective-permute-start.8 = (f32[128,256]{1,0:T(8,128)S(1)}, f32[128,256]{1,0:T(8,128)S(1)}, u32[]{:S(2)}, u32[]{:S(2)}) collective-permute-start(f32[128,256]{1,0:T(8,128)S(1)} %slice.35), channel_id=1, source_target_pairs={{0,1},{1,0},{2,3},{3,2},{4,6},{5,7},{6,4},{7,5},{8,9},{9,8},{10,11... | collective-permute-start | bytes 393224 | tf_op jit(solution)/shard_map/ppermute | solution.py:145
  29.7 1.7 %collective-permute-done.9 = f32[256,256]{1,0:T(8,128)S(1)} collective-permute-done((f32[256,256]{1,0:T(8,128)S(1)}, f32[256,256]{1,0:T(8,128)S(1)}, u32[]{:S(2)}, u32[]{:S(2)}) %collective-permute-start.9) | collective-permute-done | bytes 262176 | tf_op jit(solution)/shard_map/ppermute | solution.py:145
  31.5 1.5 %collective-permute-start.10 = (f32[128,256]{1,0:T(8,128)S(1)}, f32[128,256]{1,0:T(8,128)S(1)}, u32[]{:S(2)}, u32[]{:S(2)}) collective-permute-start(f32[128,256]{1,0:T(8,128)S(1)} %slice.37), channel_id=1, source_target_pairs={{0,1},{1,0},{2,3},{3,2},{4,6},{5,7},{6,4},{7,5},{8,9},{9,8},{10,11... | collective-permute-start | bytes 393224 | tf_op jit(solution)/shard_map/ppermute | solution.py:145
  33.2 3.3 %collective-permute-done.10 = f32[128,256]{1,0:T(8,128)S(1)} collective-permute-done((f32[128,256]{1,0:T(8,128)S(1)}, f32[128,256]{1,0:T(8,128)S(1)}, u32[]{:S(2)}, u32[]{:S(2)}) %collective-permute-start.10) | collective-permute-done | bytes 131104 | tf_op jit(solution)/shard_map/ppermute | solution.py:145
  36.5 0.7 %maximum_add_fusion.2 = f32[128,512]{1,0:T(8,128)} fusion(f32[128,512]{1,0:T(8,128)S(1)} %collective-permute-done.11, f32[128,256]{1,0:T(8,128)S(1)} %slice_add_fusion.1, f32[128,256]{1,0:T(8,128)S(1)} %slice_add_fusion.2), kind=kLoop, calls=%fused_computation.16 | loop fusion | flops 131072 | bytes 786432 | tf_op jit(solution)/shard_map/add | solution.py:155
  (33 shorter events, 3.5 us)
Async XLA Ops:
  1.0 9.7 %collective-permute-start.1 = (f32[128,512]{1,0:T(8,128)S(1)}, f32[128,512]{1,0:T(8,128)S(1)}, u32[]{:S(2)}, u32[]{:S(2)}) collective-permute-start(f32[128,512]{1,0:T(8,128)S(1)} %constant_dynamic-slice_fusion), channel_id=1, source_target_pairs={{0,16},{4,20},{24,8},{28,12},{8,0},{12,4},{16,24},{20,28},{1,17},{... | collective-permute-start | bytes 786440 | tf_op jit(solution)/shard_map/ppermute | solution.py:66
  5.1 8.0 %collective-permute-start = (f32[128,512]{1,0:T(8,128)S(1)}, f32[128,512]{1,0:T(8,128)S(1)}, u32[]{:S(2)}, u32[]{:S(2)}) collective-permute-start(f32[128,512]{1,0:T(8,128)S(1)} %constant_dynamic-slice_fusion), channel_id=1, source_target_pairs={{0,4},{4,0},{8,12},{12,8},{16,20},{20,16},{24,28},{28,24},{1,5},{5... | collective-permute-start | bytes 786440 | tf_op jit(solution)/shard_map/ppermute | solution.py:69
  5.1 1.6 %copy-start = (f32[512,1,1024]{2,1,0:T(1,128)S(1)}, f32[512,1,1024]{2,1,0:T(1,128)}, u32[]{:S(2)}) copy-start(f32[512,1,1024]{2,1,0:T(1,128)} %kernel_ref.1) | copy-start | bytes 6291460
  6.7 6.3 %copy-start.1 = (f32[512,512]{1,0:T(8,128)S(1)}, f32[512,512]{1,0:T(8,128)}, u32[]{:S(2)}) copy-start(f32[512,512]{1,0:T(8,128)} %param.2) | copy-start | bytes 3145732
  7.8 9.7 %collective-permute-start.4 = (f32[128,512]{1,0:T(8,128)S(1)}, f32[128,512]{1,0:T(8,128)}, u32[]{:S(2)}, u32[]{:S(2)}) collective-permute-start(f32[128,512]{1,0:T(8,128)S(1)} %constant_dynamic-slice_fusion), channel_id=1, source_target_pairs={{8,16},{12,20},{16,8},{20,12},{9,17},{13,21},{17,9},{21,13},{10,18... | collective-permute-start | bytes 786440 | tf_op jit(solution)/shard_map/ppermute | solution.py:66
  10.6 8.0 %collective-permute-start.5 = (f32[128,512]{1,0:T(8,128)S(1)}, f32[128,512]{1,0:T(8,128)S(1)}, u32[]{:S(2)}, u32[]{:S(2)}) collective-permute-start(f32[128,512]{1,0:T(8,128)S(1)} %collective-permute-done.1), channel_id=1, source_target_pairs={{0,8},{4,12},{8,0},{12,4},{16,24},{20,28},{24,16},{28,20},{1,9},{5... | collective-permute-start | bytes 786440 | tf_op jit(solution)/shard_map/ppermute | solution.py:66
  13.0 1.5 %collective-permute-start.2 = (f32[128,512]{1,0:T(8,128)S(1)}, f32[128,512]{1,0:T(8,128)S(1)}, u32[]{:S(2)}, u32[]{:S(2)}) collective-permute-start(f32[128,512]{1,0:T(8,128)S(1)} %collective-permute-done.1), channel_id=1, source_target_pairs={{0,4},{4,0},{8,12},{12,8},{16,20},{20,16},{24,28},{28,24},{1,5},{5... | collective-permute-start | bytes 786440 | tf_op jit(solution)/shard_map/ppermute | solution.py:69
  15.9 1.6 %collective-permute-start.3 = (f32[128,512]{1,0:T(8,128)S(1)}, f32[128,512]{1,0:T(8,128)S(1)}, u32[]{:S(2)}, u32[]{:S(2)}) collective-permute-start(f32[128,512]{1,0:T(8,128)S(1)} %slice.33), channel_id=1, source_target_pairs={{0,4},{4,0},{8,12},{12,8},{16,20},{20,16},{24,28},{28,24},{1,5},{5... | collective-permute-start | bytes 786440 | tf_op jit(solution)/shard_map/ppermute | solution.py:69
  18.7 1.6 %collective-permute-start.6 = (f32[128,512]{1,0:T(8,128)S(1)}, f32[128,512]{1,0:T(8,128)S(1)}, u32[]{:S(2)}, u32[]{:S(2)}) collective-permute-start(f32[128,512]{1,0:T(8,128)S(1)} %broadcast_select_fusion), channel_id=1, source_target_pairs={{0,4},{4,0},{8,12},{12,8},{16,20},{20,16},{24,28},{28,24},{1,5},{5... | collective-permute-start | bytes 786440 | tf_op jit(solution)/shard_map/ppermute | solution.py:69
  21.7 6.4 %collective-permute-start.7 = (f32[256,256]{1,0:T(8,128)S(1)}, f32[256,256]{1,0:T(8,128)S(1)}, u32[]{:S(2)}, u32[]{:S(2)}) collective-permute-start(f32[256,256]{1,0:T(8,128)S(1)} %pad_maximum_fusion.3), channel_id=1, source_target_pairs={{0,2},{1,3},{2,0},{3,1},{4,5},{5,4},{6,7},{7,6},{8,10},{9,11},{10,... | collective-permute-start | bytes 786440 | tf_op jit(solution)/shard_map/ppermute | solution.py:145
  23.3 8.2 %collective-permute-start.9 = (f32[256,256]{1,0:T(8,128)S(1)}, f32[256,256]{1,0:T(8,128)S(1)}, u32[]{:S(2)}, u32[]{:S(2)}) collective-permute-start(f32[256,256]{1,0:T(8,128)S(1)} %pad_maximum_fusion.4), channel_id=1, source_target_pairs={{0,2},{1,3},{2,0},{3,1},{4,5},{5,4},{6,7},{7,6},{8,10},{9,11},{10,... | collective-permute-start | bytes 786440 | tf_op jit(solution)/shard_map/ppermute | solution.py:145
  23.8 12.7 %collective-permute-start.11 = (f32[128,512]{1,0:T(8,128)S(1)}, f32[128,512]{1,0:T(8,128)S(1)}, u32[]{:S(2)}, u32[]{:S(2)}) collective-permute-start(f32[128,512]{1,0:T(8,128)S(1)} %slice_add_fusion), channel_id=1, source_target_pairs={{8,24},{12,28},{16,0},{20,4},{0,8},{4,12},{24,16},{28,20},{9,25},{... | collective-permute-start | bytes 786440 | tf_op jit(solution)/shard_map/ppermute | solution.py:66
  28.2 5.0 %collective-permute-start.8 = (f32[128,256]{1,0:T(8,128)S(1)}, f32[128,256]{1,0:T(8,128)S(1)}, u32[]{:S(2)}, u32[]{:S(2)}) collective-permute-start(f32[128,256]{1,0:T(8,128)S(1)} %slice.35), channel_id=1, source_target_pairs={{0,1},{1,0},{2,3},{3,2},{4,6},{5,7},{6,4},{7,5},{8,9},{9,8},{10,11... | collective-permute-start | bytes 393224 | tf_op jit(solution)/shard_map/ppermute | solution.py:145
  31.5 5.0 %collective-permute-start.10 = (f32[128,256]{1,0:T(8,128)S(1)}, f32[128,256]{1,0:T(8,128)S(1)}, u32[]{:S(2)}, u32[]{:S(2)}) collective-permute-start(f32[128,256]{1,0:T(8,128)S(1)} %slice.37), channel_id=1, source_target_pairs={{0,1},{1,0},{2,3},{3,2},{4,6},{5,7},{6,4},{7,5},{8,9},{9,8},{10,11... | collective-permute-start | bytes 393224 | tf_op jit(solution)/shard_map/ppermute | solution.py:145
